TPU v7x, 256 devices: a whole 4x4x8 slice. The times are simulated.
256 devices in a mesh: dp: 16 (over x, y_hi, core), fsdp: 16 (over z, y_lo).
Axes of the slice: x: 4, y: 4 (y_hi: 2, y_lo: 2; y = y_hi * 2 + y_lo), z: 8, core: 2. Of those that a mesh axis runs over, the one named last changes fastest.
Arguments:
- patches: bfloat16 [16, 224, 8, 8, 768], P('fsdp', 'dp'), may hold values from -6 to 6
- out_grad: bfloat16 [16, 224, 8, 8, 768], P('fsdp', 'dp'), may hold values from -6 to 6
- row_counts: int32 [16, 16], P('fsdp', 'dp'), may hold values from 2 to 14, as said below
- dw_kernel: bfloat16 [49, 768], P(None, 'fsdp'), may hold values from -0.875 to 0.875
- ln_gain: bfloat16 [768], P('fsdp'), may hold values from 0.099609375 to 1.8984375
- ln_bias: bfloat16 [768], P('fsdp'), may hold values from -3 to 3
- w_first: bfloat16 [768, 2304], P('fsdp'), may hold values from -0.21875 to 0.21875
- first_bias: bfloat16 [2304], P('fsdp'), may hold values from -3 to 3
- w_second: bfloat16 [2304, 768], P('fsdp'), may hold values from -0.125 to 0.125
- layer_scale: bfloat16 [768], P('fsdp'), may hold values from 0.25 to 1
Outputs:
- in_grad: float32 [16, 224, 8, 8, 768], P('fsdp', 'dp')
- grad_first: float32 [768, 2304], P('fsdp')
- grad_second: float32 [2304, 768], P('fsdp')
- grad_kernel: float32 [49, 768], P(None, 'fsdp')
- grad_bias: float32 [2304], P('fsdp')
- grad_channels: float32 [3, 768], P(None, 'fsdp')
Inputs may be any that keep to these rules, and one draw needn't show every extreme that they name: In every column f the 16 counts row_counts[f, :] sum to exactly 128, and some device of every column holds 14 live slots.
All inputs are finite; a program needn't handle non-finite values.
Results may differ from a plain program's by a relative error of at most 0.007.
Values may be sent and summed in bfloat16 or wider, within the bound.
No kernel may reach another device: no remote copies, remote signals or barrier semaphores. Data moves between devices by JAX's collectives and lax.ppermute only.
A program may use at most 192 MiB of HBM per device.

v0:
```python
import functools
import math

import jax
import jax.numpy as jnp
from jax import lax
from jax.experimental import pallas as pl
from jax.experimental.pallas import tpu as pltpu
from jax.sharding import PartitionSpec as P

ROWS = 8
LANES = 128
SUBLANES = 8
SIDE = 8
SPOTS = SIDE * SIDE
REACH = 3
TAPS = 7
BLOCK = 384
TOKEN_BLOCK = 448
NORM_BLOCK = 128
PART_TILES = 7
GROUP_STEPS = 2
CUT = 384
AXES = ("dp", "fsdp")
X, Y, Z = 4, 4, 8
BF16, F32 = jnp.bfloat16, jnp.float32
VMEM_LIMIT = 56 * 1024 * 1024
SMALL_VMEM = 24 * 1024 * 1024


def whole(shape):
    return pl.BlockSpec(shape, lambda *_: (0,) * len(shape))


def spread_taps(taps_ref, spread):
    for tap in range(TAPS * TAPS):
        spread[tap] = jnp.broadcast_to(taps_ref[tap : tap + 1, :], (SUBLANES, LANES))


def to_patch_minor(rows, out, groups):
    def one(spot, _):
        for group in range(groups):
            out[group * SPOTS + spot] = rows[
                pl.ds(group * SUBLANES * SPOTS + spot, SUBLANES, stride=SPOTS), :
            ]
        return 0

    lax.fori_loop(0, SPOTS, one, 0, unroll=8)


def conv_rows(src, spread, group, flip, emit):
    for p in range(SIDE):
        sums = [None] * SIDE
        for a in range(TAPS):
            row = p + a - REACH
            if not 0 <= row < SIDE:
                continue
            values = [src[group * SPOTS + row * SIDE + q] for q in range(SIDE)]
            for b in range(TAPS):
                tap = a * TAPS + b
                weight = spread[TAPS * TAPS - 1 - tap if flip else tap]
                for q in range(SIDE):
                    col = q + b - REACH
                    if 0 <= col < SIDE:
                        term = values[col] * weight
                        sums[q] = term if sums[q] is None else sums[q] + term
        for q in range(SIDE):
            emit(p * SIDE + q, sums[q])


def conv_kernel(
    slots, x_ref, taps_ref, _after, _buffer, out_ref, rows, minor, spread, conv
):
    groups = rows.shape[0] // (SUBLANES * SPOTS)
    spread_taps(taps_ref, spread)

    def load(slot, _):
        rows[pl.ds(pl.multiple_of(slot * SPOTS, SPOTS), SPOTS), :] = (
            x_ref[slot].astype(F32).reshape(SPOTS, LANES)
        )
        return 0

    lax.fori_loop(0, slots, load, 0)
    to_patch_minor(rows, minor, groups)

    def convolve(group, _):
        def emit(spot, value):
            conv[pl.ds(group * SUBLANES * SPOTS + spot, SUBLANES, stride=SPOTS), :] = value

        conv_rows(minor, spread, group, False, emit)
        return 0

    lax.fori_loop(0, groups, convolve, 0)
    out_ref[...] = conv[: slots * SPOTS, :]


def shapes_of(x):
    slots, channels = x.shape[0], x.shape[3]
    groups = -(-slots // SUBLANES)
    return slots, channels, slots * SPOTS, groups, groups * SUBLANES * SPOTS


def conv_part(part, x, taps, after, buffer):
    slots, channels, tokens, groups, padded = shapes_of(x)
    base = part * GROUP_STEPS
    anywhere = pl.BlockSpec(memory_space=pl.ANY)
    if buffer is None:
        buffer, aliases = after, {}
    else:
        aliases = {3: 0}
    return pl.pallas_call(
        functools.partial(conv_kernel, slots),
        grid=(GROUP_STEPS,),
        in_specs=[
            pl.BlockSpec((slots, SIDE, SIDE, LANES), lambda j: (0, 0, 0, j + base)),
            pl.BlockSpec((TAPS * TAPS, LANES), lambda j: (0, j + base)),
            anywhere,
            anywhere,
        ],
        out_specs=pl.BlockSpec((tokens, LANES), lambda j: (0, j + base)),
        out_shape=jax.ShapeDtypeStruct((tokens, channels), F32),
        input_output_aliases=aliases,
        scratch_shapes=[
            pltpu.VMEM((padded, LANES), F32),
            pltpu.VMEM((groups * SPOTS, SUBLANES, LANES), F32),
            pltpu.VMEM((TAPS * TAPS, SUBLANES, LANES), F32),
            pltpu.VMEM((padded, LANES), F32),
        ],
        compiler_params=pltpu.CompilerParams(vmem_limit_bytes=SMALL_VMEM),
        cost_estimate=pl.CostEstimate(
            flops=2 * 49 * tokens * LANES * GROUP_STEPS,
            bytes_accessed=6 * tokens * LANES * GROUP_STEPS,
            transcendentals=0,
        ),
        name="conv",
    )(x, taps, after, buffer)


def norm_kernel(
    conv_ref, g_ref, count_ref, gain_ref, shift_ref, scale_ref, _after,
    normed_ref, std_ref, inv_ref, gb_ref,
):
    step = pl.program_id(0)
    count = count_ref[0, 0]
    channels = conv_ref.shape[1]
    parts = [slice(c, c + LANES) for c in range(0, channels, LANES)]
    gain, shift, scale = ([ref[:, c] for c in parts] for ref in (gain_ref, shift_ref, scale_ref))
    tall = 32

    def norm(i, _):
        at = pl.ds(pl.multiple_of(i * tall, tall), tall)
        values = [conv_ref[at, c] for c in parts]
        mean = sum(jnp.sum(v, axis=1, keepdims=True) for v in values) / channels
        values = [v - mean for v in values]
        var = sum(jnp.sum(v * v, axis=1, keepdims=True) for v in values) / channels
        inv = lax.rsqrt(var + 1e-06)
        inv_ref[at, :] = inv
        for c, v in enumerate(values):
            std = v * inv
            std_ref[at, parts[c]] = std
            normed_ref[at, parts[c]] = (std * gain[c] + shift[c]).astype(BF16)
        return 0

    lax.fori_loop(0, NORM_BLOCK // tall, norm, 0, unroll=2)
    for slot in range(NORM_BLOCK // SPOTS):
        live = jnp.where(step * (NORM_BLOCK // SPOTS) + slot < count, 1.0, 0.0)
        for c, lanes in enumerate(parts):
            g = g_ref[slot, :, :, lanes].astype(F32).reshape(SPOTS, LANES)
            gb_ref[slot * SPOTS : (slot + 1) * SPOTS, lanes] = (g * (scale[c] * live)).astype(BF16)


def norm(conv, g, count, gain, shift, scale, after):
    tokens, channels = conv.shape
    block = pl.BlockSpec((NORM_BLOCK, channels), lambda j: (j, 0))
    vector = whole((1, channels))
    return pl.pallas_call(
        norm_kernel,
        grid=(tokens // NORM_BLOCK,),
        in_specs=[
            block,
            pl.BlockSpec((NORM_BLOCK // SPOTS, SIDE, SIDE, channels), lambda j: (j, 0, 0, 0)),
            pl.BlockSpec(memory_space=pltpu.SMEM),
            vector, vector, vector,
            pl.BlockSpec(memory_space=pl.ANY),
        ],
        out_specs=[block, block, pl.BlockSpec((NORM_BLOCK, 1), lambda j: (j, 0)), block],
        out_shape=[
            jax.ShapeDtypeStruct((tokens, channels), BF16),
            jax.ShapeDtypeStruct((tokens, channels), F32),
            jax.ShapeDtypeStruct((tokens, 1), F32),
            jax.ShapeDtypeStruct((tokens, channels), BF16),
        ],
        compiler_params=pltpu.CompilerParams(vmem_limit_bytes=SMALL_VMEM),
        cost_estimate=pl.CostEstimate(
            flops=20 * tokens * channels, bytes_accessed=14 * tokens * channels, transcendentals=0
        ),
        name="norm",
    )(conv, g, count, gain, shift, scale, after)


def tile_of(part, i, across):
    return divmod(part * PART_TILES + i, across)


def mlp_kernel(
    count, core_ref, order_ref, mine_ref, theirs_ref, gb_mine_ref, gb_theirs_ref, bias_ref,
    second_ref, *refs,
):
    pieces = refs[:count]
    (
        sums_ref, gn_mine_ref, gn_theirs_ref, grad_bias_ref, scale_ref,
        first, second, sum_first, sum_second, tokens, cots, flipped, grad_normed, sems,
    ) = refs[count:]
    step = pl.program_id(0)
    steps = pl.num_programs(0)
    channels, hidden = first.shape
    chips = second_ref.shape[0]
    cuts = hidden // CUT
    own = pieces[0].shape[0] // (2 * cuts)
    shards = channels // own
    units = hidden // (shards // 2)
    first_rows = shards * PART_TILES * SUBLANES
    part_rows = PART_TILES * 2 * SUBLANES
    tall = 2 * SUBLANES
    dot = functools.partial(lax.dot_general, preferred_element_type=F32)

    def aligned(value, to):
        return pl.multiple_of(value * to, to)

    @pl.when(step == 0)
    def _():
        made = []
        for i, piece in enumerate(pieces):
            for parity in range(2):
                f = order_ref[2 * i + parity]
                for k in range(cuts):
                    made.append(
                        pltpu.make_async_copy(
                            piece.at[pl.ds((parity * cuts + k) * own, own), :],
                            first.at[pl.ds(aligned(f, own), own), pl.ds(k * CUT, CUT)],
                            sems.at[i],
                        )
                    )
        for copy in made:
            copy.start()

        def unpack_shard(f, _):
            for e in range(chips):
                for i in range(PART_TILES):
                    r, c = tile_of(e, i, channels // LANES)
                    if r * tall < units:
                        second[
                            pl.ds(pl.multiple_of(f * units + r * tall, tall), tall),
                            c * LANES : (c + 1) * LANES,
                        ] = second_ref[
                            e, pl.ds(pl.multiple_of(f * part_rows + i * tall, tall), tall), :
                        ]
            return 0

        lax.fori_loop(0, shards // 2, unpack_shard, 0)
        scale_ref[...] = jnp.zeros_like(scale_ref)
        grad_bias_ref[...] = jnp.zeros_like(grad_bias_ref)

        def clear(i, _):
            sum_first[pl.ds(aligned(i, tall), tall), :] = jnp.zeros((tall, hidden), F32)
            return 0

        lax.fori_loop(0, channels // tall, clear, 0)

        def clear_more(i, _):
            sum_second[pl.ds(aligned(i, tall), tall), :] = jnp.zeros((tall, channels), F32)
            return 0

        lax.fori_loop(0, hidden // tall, clear_more, 0)
        for copy in made:
            copy.wait()

    @pl.when(step < steps // 2)
    def _():
        tokens[...] = mine_ref[...]
        cots[...] = gb_mine_ref[...]

    @pl.when(step >= steps // 2)
    def _():
        tokens[...] = theirs_ref[...]
        cots[...] = gb_theirs_ref[...]

    flipped[...] = tokens[...].T
    grad_normed[...] = jnp.zeros_like(grad_normed)

    def chunk(h, _):
        at = pl.ds(aligned(h, BLOCK), BLOCK)
        normed, gb = tokens[...], cots[...]
        preact = dot(normed, first[:, at], (((1,), (0,)), ((), ()))) + bias_ref[:, at]
        grad_hidden = dot(gb, second[at, :], (((1,), (1,)), ((), ())))
        prob = 0.5 * (1.0 + lax.erf(preact * 0.7071067811865476))
        active = (preact * prob).astype(BF16)
        slope = prob + preact * jnp.exp(-0.5 * preact * preact) * 0.3989422804014327
        grad_preact = (grad_hidden * slope).astype(BF16)
        sum_second[at, :] += dot(active, gb, (((0,), (0,)), ((), ())))
        sum_first[:, at] += dot(flipped[...], grad_preact, (((1,), (0,)), ((), ())))
        grad_bias_ref[:, at] += jnp.sum(grad_preact.astype(F32), axis=0, keepdims=True)
        grad_normed[...] += dot(grad_preact, first[:, at], (((1,), (1,)), ((), ())))
        return 0

    lax.fori_loop(0, hidden // BLOCK, chunk, 0)

    @pl.when(step < steps // 2)
    def _():
        gn_mine_ref[...] = grad_normed[...]

    @pl.when(step >= steps // 2)
    def _():
        gn_theirs_ref[...] = grad_normed[...].astype(BF16)

    @pl.when(step == steps - 1)
    def _():
        def scale_rows(i, total):
            at = pl.ds(aligned(i, tall), tall)
            return total + sum_second[at, :] * second[at, :].astype(F32)

        total = lax.fori_loop(
            0, hidden // tall, scale_rows, jnp.zeros((tall, channels), F32)
        )
        scale_ref[...] = jnp.sum(total, axis=0, keepdims=True)
        none = jnp.zeros((SUBLANES, LANES), F32)

        def pack_pair(pair, _):
            for e in range(chips):
                tiles = []
                for f in range(2):
                    for i in range(PART_TILES):
                        r, c = tile_of(e, i, hidden // LANES)
                        row = pl.multiple_of((2 * pair + f) * own + r * SUBLANES, SUBLANES)
                        tiles.append(
                            sum_first[pl.ds(row, SUBLANES), c * LANES : (c + 1) * LANES]
                            if r * SUBLANES < own
                            else none
                        )
                for i in range(0, len(tiles), 2):
                    at = pl.multiple_of(pair * part_rows + i * SUBLANES, tall)
                    sums_ref[e, pl.ds(at, tall), :] = jnp.concatenate(tiles[i : i + 2]).astype(BF16)
            return 0

        lax.fori_loop(0, shards // 2, pack_pair, 0)

        def pack_shard(f, _):
            for e in range(chips):
                for i in range(PART_TILES):
                    r, c = tile_of(e, i, channels // LANES)
                    at = pl.multiple_of(first_rows + f * part_rows + i * tall, tall)
                    if r * tall < units:
                        row = pl.multiple_of(f * units + r * tall, tall)
                        value = sum_second[pl.ds(row, tall), c * LANES : (c + 1) * LANES]
                    else:
                        value = jnp.zeros((tall, LANES), F32)
                    sums_ref[e, pl.ds(at, tall), :] = value.astype(BF16)
            return 0

        lax.fori_loop(0, shards // 2, pack_shard, 0)


def mlp(core, order, mine, theirs, gb_mine, gb_theirs, bias, second, pieces):
    tokens, channels = mine.shape
    count = len(pieces)
    shards = 2 * count
    hidden = bias.shape[1]
    sums = (second.shape[0], shards * PART_TILES * SUBLANES + second.shape[1], LANES)
    steps = tokens // TOKEN_BLOCK
    early = pl.BlockSpec((TOKEN_BLOCK, channels), lambda j: (jnp.minimum(j, steps - 1), 0))
    late = pl.BlockSpec((TOKEN_BLOCK, channels), lambda j: (jnp.maximum(j - steps, 0), 0))
    anywhere = pl.BlockSpec(memory_space=pl.ANY)
    return pl.pallas_call(
        functools.partial(mlp_kernel, count),
        grid=(2 * steps,),
        in_specs=[
            pl.BlockSpec(memory_space=pltpu.SMEM),
            pl.BlockSpec(memory_space=pltpu.SMEM),
            early, late, early, late,
            whole((1, hidden)),
            whole(second.shape),
        ]
        + [anywhere] * count,
        out_specs=[
            whole(sums),
            early, late,
            whole((1, hidden)),
            whole((1, channels)),
        ],
        out_shape=[
            jax.ShapeDtypeStruct(sums, BF16),
            jax.ShapeDtypeStruct((tokens, channels), F32),
            jax.ShapeDtypeStruct((tokens, channels), BF16),
            jax.ShapeDtypeStruct((1, hidden), F32),
            jax.ShapeDtypeStruct((1, channels), F32),
        ],
        scratch_shapes=[
            pltpu.VMEM((channels, hidden), BF16),
            pltpu.VMEM((hidden, channels), BF16),
            pltpu.VMEM((channels, hidden), F32),
            pltpu.VMEM((hidden, channels), F32),
            pltpu.VMEM((TOKEN_BLOCK, channels), BF16),
            pltpu.VMEM((TOKEN_BLOCK, channels), BF16),
            pltpu.VMEM((channels, TOKEN_BLOCK), BF16),
            pltpu.VMEM((TOKEN_BLOCK, channels), F32),
            pltpu.SemaphoreType.DMA((count,)),
        ],
        compiler_params=pltpu.CompilerParams(vmem_limit_bytes=VMEM_LIMIT),
        cost_estimate=pl.CostEstimate(
            flops=20 * tokens * channels * hidden,
            bytes_accessed=12 * hidden * channels,
            transcendentals=4 * tokens * hidden,
        ),
        name="mlp",
    )(core, order, mine, theirs, gb_mine, gb_theirs, bias, second, *pieces)


def unnorm_kernel(gn_ref, gn_other_ref, std_ref, inv_ref, gain_ref, grad_conv_ref, channel_ref):
    step = pl.program_id(0)
    channels = gn_ref.shape[1]
    parts = [slice(c, c + LANES) for c in range(0, channels, LANES)]
    gain = [gain_ref[:, c] for c in parts]
    tall = 32

    @pl.when(step == 0)
    def _():
        channel_ref[...] = jnp.zeros_like(channel_ref)

    def one(i, sums):
        at = pl.ds(pl.multiple_of(i * tall, tall), tall)
        inv = inv_ref[at, :]
        scaled, new = [], []
        for c, lanes in enumerate(parts):
            gn = gn_ref[at, lanes] + gn_other_ref[at, lanes].astype(F32)
            std = std_ref[at, lanes]
            product = gn * std
            gain_sum, shift_sum = sums[2 * c], sums[2 * c + 1]
            for r in range(0, tall, SUBLANES):
                gain_sum = gain_sum + product[r : r + SUBLANES]
                shift_sum = shift_sum + gn[r : r + SUBLANES]
            new += [gain_sum, shift_sum]
            scaled.append((gn * gain[c], product * gain[c], std))
        mean = sum(jnp.sum(v[0], axis=1, keepdims=True) for v in scaled) / channels
        mean_std = sum(jnp.sum(v[1], axis=1, keepdims=True) for v in scaled) / channels
        for c, (v, _, std) in enumerate(scaled):
            grad_conv_ref[at, parts[c]] = inv * (v - mean - std * mean_std)
        return tuple(new)

    zero = jnp.zeros((SUBLANES, LANES), F32)
    sums = lax.fori_loop(0, NORM_BLOCK // tall, one, (zero,) * (2 * len(parts)))
    for c, lanes in enumerate(parts):
        channel_ref[0:1, lanes] += jnp.sum(sums[2 * c], axis=0, keepdims=True)
        channel_ref[1:2, lanes] += jnp.sum(sums[2 * c + 1], axis=0, keepdims=True)


def unnorm(gn, gn_other, std, inv, gain):
    tokens, channels = gn.shape
    block = pl.BlockSpec((NORM_BLOCK, channels), lambda j: (j, 0))
    return pl.pallas_call(
        unnorm_kernel,
        grid=(tokens // NORM_BLOCK,),
        in_specs=[
            block, block, block,
            pl.BlockSpec((NORM_BLOCK, 1), lambda j: (j, 0)),
            whole((1, channels)),
        ],
        out_specs=[block, whole((2, channels))],
        out_shape=[
            jax.ShapeDtypeStruct((tokens, channels), F32),
            jax.ShapeDtypeStruct((2, channels), F32),
        ],
        compiler_params=pltpu.CompilerParams(vmem_limit_bytes=SMALL_VMEM),
        cost_estimate=pl.CostEstimate(
            flops=20 * tokens * channels, bytes_accessed=14 * tokens * channels, transcendentals=0
        ),
        name="unnorm",
    )(gn, gn_other, std, inv, gain)


def load_grads(grad_ref, rows, grad_minor, groups, tokens):
    rows[:tokens, :] = grad_ref[...]
    if rows.shape[0] > tokens:
        rows[tokens:, :] = jnp.zeros((rows.shape[0] - tokens, LANES), F32)
    to_patch_minor(rows, grad_minor, groups)


def taps_kernel(
    slots, x_ref, grad_ref, _after, _buffer, grad_taps_ref, rows, minor, grad_minor, tap_sums
):
    groups = rows.shape[0] // (SUBLANES * SPOTS)
    load_grads(grad_ref, rows, grad_minor, groups, slots * SPOTS)

    def load(slot, _):
        rows[pl.ds(pl.multiple_of(slot * SPOTS, SPOTS), SPOTS), :] = (
            x_ref[slot].astype(F32).reshape(SPOTS, LANES)
        )
        return 0

    lax.fori_loop(0, slots, load, 0)
    to_patch_minor(rows, minor, groups)

    def taps(group, _):
        for a in range(TAPS):
            sums = [jnp.where(group == 0, 0.0, tap_sums[a * TAPS + b]) for b in range(TAPS)]
            for p in range(SIDE):
                row = p + a - REACH
                if not 0 <= row < SIDE:
                    continue
                values = [minor[group * SPOTS + row * SIDE + q] for q in range(SIDE)]
                grads = [grad_minor[group * SPOTS + p * SIDE + q] for q in range(SIDE)]
                for b in range(TAPS):
                    for q in range(SIDE):
                        col = q + b - REACH
                        if 0 <= col < SIDE:
                            sums[b] = sums[b] + grads[q] * values[col]
            for b in range(TAPS):
                tap_sums[a * TAPS + b] = sums[b]
        return 0

    lax.fori_loop(0, groups, taps, 0)
    for tap in range(TAPS * TAPS):
        grad_taps_ref[tap : tap + 1, :] = jnp.sum(tap_sums[tap], axis=0, keepdims=True)


def taps_part(part, x, grad_conv, after, buffer):
    slots, channels, tokens, groups, padded = shapes_of(x)
    base = part * GROUP_STEPS
    anywhere = pl.BlockSpec(memory_space=pl.ANY)
    if buffer is None:
        buffer, aliases = after, {}
    else:
        aliases = {3: 0}
    return pl.pallas_call(
        functools.partial(taps_kernel, slots),
        grid=(GROUP_STEPS,),
        in_specs=[
            pl.BlockSpec((slots, SIDE, SIDE, LANES), lambda j: (0, 0, 0, j + base)),
            pl.BlockSpec((tokens, LANES), lambda j: (0, j + base)),
            anywhere,
            anywhere,
        ],
        out_specs=pl.BlockSpec((TAPS * TAPS, LANES), lambda j: (0, j + base)),
        out_shape=jax.ShapeDtypeStruct((TAPS * TAPS, channels), F32),
        input_output_aliases=aliases,
        scratch_shapes=[
            pltpu.VMEM((padded, LANES), F32),
            pltpu.VMEM((groups * SPOTS, SUBLANES, LANES), F32),
            pltpu.VMEM((groups * SPOTS, SUBLANES, LANES), F32),
            pltpu.VMEM((TAPS * TAPS, SUBLANES, LANES), F32),
        ],
        compiler_params=pltpu.CompilerParams(vmem_limit_bytes=SMALL_VMEM),
        cost_estimate=pl.CostEstimate(
            flops=2 * 49 * tokens * LANES * GROUP_STEPS,
            bytes_accessed=6 * tokens * LANES * GROUP_STEPS,
            transcendentals=0,
        ),
        name="taps",
    )(x, grad_conv, after, buffer)


def back_kernel(
    slots, g_ref, grad_ref, count_ref, taps_ref, _after, _buffer, in_grad_ref,
    rows, grad_minor, spread, result,
):
    groups = rows.shape[0] // (SUBLANES * SPOTS)
    spread_taps(taps_ref, spread)
    load_grads(grad_ref, rows, grad_minor, groups, slots * SPOTS)

    def convolve(group, _):
        def emit(spot, value):
            result[pl.ds(group * SUBLANES * SPOTS + spot, SUBLANES, stride=SPOTS), :] = value

        conv_rows(grad_minor, spread, group, True, emit)
        return 0

    lax.fori_loop(0, groups, convolve, 0)
    count = count_ref[0, 0]

    def finish(slot, _):
        live = jnp.where(slot < count, 1.0, 0.0)
        g = g_ref[slot].astype(F32) * live
        at = pl.ds(pl.multiple_of(slot * SPOTS, SPOTS), SPOTS)
        in_grad_ref[slot] = g + result[at, :].reshape(SIDE, SIDE, LANES)
        return 0

    lax.fori_loop(0, slots, finish, 0)


def back_part(part, g, grad_conv, count, taps, after, buffer):
    slots, channels, tokens, groups, padded = shapes_of(g)
    base = part * GROUP_STEPS
    anywhere = pl.BlockSpec(memory_space=pl.ANY)
    if buffer is None:
        buffer, aliases = after, {}
    else:
        aliases = {5: 0}
    return pl.pallas_call(
        functools.partial(back_kernel, slots),
        grid=(GROUP_STEPS,),
        in_specs=[
            pl.BlockSpec((slots, SIDE, SIDE, LANES), lambda j: (0, 0, 0, j + base)),
            pl.BlockSpec((tokens, LANES), lambda j: (0, j + base)),
            pl.BlockSpec(memory_space=pltpu.SMEM),
            pl.BlockSpec((TAPS * TAPS, LANES), lambda j: (0, j + base)),
            anywhere,
            anywhere,
        ],
        out_specs=pl.BlockSpec((slots, SIDE, SIDE, LANES), lambda j: (0, 0, 0, j + base)),
        out_shape=jax.ShapeDtypeStruct((slots, SIDE, SIDE, channels), F32),
        input_output_aliases=aliases,
        scratch_shapes=[
            pltpu.VMEM((padded, LANES), F32),
            pltpu.VMEM((groups * SPOTS, SUBLANES, LANES), F32),
            pltpu.VMEM((TAPS * TAPS, SUBLANES, LANES), F32),
            pltpu.VMEM((padded, LANES), F32),
        ],
        compiler_params=pltpu.CompilerParams(vmem_limit_bytes=SMALL_VMEM),
        cost_estimate=pl.CostEstimate(
            flops=2 * 49 * tokens * LANES * GROUP_STEPS,
            bytes_accessed=10 * tokens * LANES * GROUP_STEPS,
            transcendentals=0,
        ),
        name="back",
    )(g, grad_conv, count, taps, after, buffer)


def device_index(x, y, z, core):
    high, low = divmod(y % Y, 2)
    return ((x % X) * 4 + high * 2 + core) * (2 * Z) + (z % Z) * 2 + low


def move(value, dy=0, dz=0, flip=0):
    pairs = [
        (device_index(x, y, z, core), device_index(x, y + dy, z + dz, core ^ flip))
        for x in range(X)
        for y in range(Y)
        for z in range(Z)
        for core in range(2)
    ]
    return lax.ppermute(value, AXES, pairs)


def gather_pieces(piece, z, low):
    other = lax.ppermute(piece, "fsdp", [(i, i ^ 1) for i in range(2 * Z)])
    pair = jnp.concatenate([piece, other])
    right = left = pair
    pieces, away = [pair], [0]
    for step in range(1, Z // 2 + 1):
        right = move(right, dz=1)
        pieces.append(right)
        away.append(Z - step)
        if step < Z // 2:
            left = move(left, dz=-1)
            pieces.append(left)
            away.append(step)
    order = [(z + s) % Z * 2 + (low ^ parity) for s in away for parity in range(2)]
    return jnp.stack(order).astype(jnp.int32), pieces


def add_up_kernel(terms_ref, _after, out_ref):
    tall = 8 * SUBLANES

    def rows(i, _):
        at = pl.ds(pl.multiple_of(i * tall, tall), tall)
        total = terms_ref[0, at, :].astype(F32)
        for e in range(1, terms_ref.shape[0]):
            total = total + terms_ref[e, at, :].astype(F32)
        out_ref[at, :] = total.astype(BF16)
        return 0

    lax.fori_loop(0, terms_ref.shape[1] // tall, rows, 0, unroll=2)


def add_up(terms, after):
    return pl.pallas_call(
        add_up_kernel,
        in_specs=[
            pl.BlockSpec(memory_space=pltpu.VMEM),
            pl.BlockSpec(memory_space=pl.ANY),
        ],
        out_shape=jax.ShapeDtypeStruct(terms.shape[1:], BF16),
        compiler_params=pltpu.CompilerParams(vmem_limit_bytes=SMALL_VMEM),
        name="add_up",
    )(terms, after)


def finish_kernel(factor, side_ref, terms_ref, first_ref, second_ref, small_ref):
    side = side_ref[0]
    chips = terms_ref.shape[0] // 2
    small_rows = PART_TILES * 2 * SUBLANES
    half = small_rows // 2
    wide = first_ref.shape[1] // 2 // LANES
    small = None
    for e in range(chips):
        for core in range(2):
            part = terms_ref[2 * e + core, :small_rows, :].astype(F32) * factor
            for i in range(PART_TILES):
                r, c = tile_of(e, i, wide)
                if r * SUBLANES < first_ref.shape[0]:
                    lane = (core * wide + c) * LANES
                    first_ref[r * SUBLANES : (r + 1) * SUBLANES, lane : lane + LANES] = part[
                        i * SUBLANES : (i + 1) * SUBLANES
                    ]
            more = terms_ref[2 * e + core, small_rows:, :].astype(F32)
            small = more if small is None else small + more
        part = jnp.concatenate(
            [
                terms_ref[2 * e + core, :small_rows, :].astype(F32)[half:]
                for core in (side, 1 - side)
            ]
        )
        part = part * factor
        for i in range(PART_TILES):
            r, c = tile_of(e, i, second_ref.shape[1] // LANES)
            if r * 2 * SUBLANES < second_ref.shape[0]:
                second_ref[r * 2 * SUBLANES : (r + 1) * 2 * SUBLANES, c * LANES : (c + 1) * LANES] = (
                    part[i * 2 * SUBLANES : (i + 1) * 2 * SUBLANES]
                )
    small_ref[...] = small * factor


def finish(side, terms, first_shape, second_shape, factor):
    small = (terms.shape[1] - PART_TILES * 2 * SUBLANES, LANES)
    return pl.pallas_call(
        functools.partial(finish_kernel, factor),
        in_specs=[
            pl.BlockSpec(memory_space=pltpu.SMEM),
            pl.BlockSpec(memory_space=pltpu.VMEM),
        ],
        out_shape=[
            jax.ShapeDtypeStruct(first_shape, F32),
            jax.ShapeDtypeStruct(second_shape, F32),
            jax.ShapeDtypeStruct(small, F32),
        ],
        compiler_params=pltpu.CompilerParams(vmem_limit_bytes=SMALL_VMEM),
        name="finish",
    )(side, terms)


def pack(rows):
    count, width = rows.shape[-2:]
    half = -(-count // 2)
    lead = [(0, 0)] * (rows.ndim - 2)
    rows = jnp.pad(rows, lead + [(0, 2 * half - count), (0, 0)])
    rows = jnp.concatenate([rows[..., :half, :], rows[..., half:, :]], axis=-1)
    return jnp.pad(rows, lead + [(0, -half % (2 * SUBLANES)), (0, LANES - 2 * width)])


def unpack(packed, count, width):
    half = -(-count // 2)
    rows = [packed[..., :half, :width], packed[..., :half, width : 2 * width]]
    return jnp.concatenate(rows, axis=-2)[..., :count, :]


def local(
    patches,
    out_grad,
    row_counts,
    dw_kernel,
    ln_gain,
    ln_bias,
    w_first,
    first_bias,
    w_second,
    layer_scale,
):
    fsdp, dp = lax.axis_size("fsdp"), lax.axis_size("dp")
    own = ln_gain.shape[0]
    units = first_bias.shape[0]
    channels, hidden = own * fsdp, units * fsdp
    mine = hidden // 2
    tap_count = dw_kernel.shape[0]
    dp_index, fsdp_index = lax.axis_index("dp"), lax.axis_index("fsdp")
    core = dp_index % 2
    z, low = fsdp_index // 2, fsdp_index % 2

    chip, chips = dp_index // 2, dp // 2
    side = fsdp_index // (fsdp // 2)
    same_core = [[2 * i + c for i in range(chips)] for c in range(2)]
    flat = (PART_TILES * SUBLANES, LANES)

    tall, across = units // (2 * SUBLANES), channels // LANES
    tiles = w_second.reshape(tall, 2 * SUBLANES, across, LANES).transpose(0, 2, 1, 3)
    tiles = tiles.reshape(tall * across, 2 * SUBLANES, LANES)
    tiles = jnp.pad(tiles, ((0, chips * PART_TILES - tall * across), (0, 0), (0, 0)))
    tiles = tiles.reshape(chips * 2, *flat)
    tiles = lax.dynamic_index_in_dim(tiles, 2 * chip + (core ^ side), 0, keepdims=False)
    vectors = [ln_gain[None], ln_bias[None], layer_scale[None], first_bias.reshape(-1, own)]
    small = jnp.concatenate([dw_kernel] + vectors)
    lines = small.shape[0]
    small = jnp.concatenate([tiles, pack(small)])
    small = lax.all_to_all(
        jnp.broadcast_to(small, (fsdp,) + small.shape), "fsdp", 0, 0, tiled=True
    )
    tiles, small = small[:, : flat[0]], unpack(small[:, flat[0] :], lines, own)
    kept = lax.dynamic_slice_in_dim(tiles, core * (fsdp // 2), fsdp // 2)
    swapped = move(lax.dynamic_slice_in_dim(tiles, (1 - core) * (fsdp // 2), fsdp // 2), flip=1)
    second = jnp.concatenate([kept, swapped], axis=1).reshape(fsdp * flat[0], LANES)
    second = lax.all_to_all(
        jnp.broadcast_to(second, (chips,) + second.shape),
        "dp", 0, 0, tiled=True, axis_index_groups=same_core,
    )
    taps = small[:, :tap_count].transpose(1, 0, 2).reshape(tap_count, channels).astype(F32)
    gain, shift, scale = (
        small[:, tap_count + i].reshape(1, channels).astype(F32) for i in range(3)
    )
    bias = small[:, tap_count + 3 :].reshape(1, hidden).astype(F32)
    bias = lax.dynamic_slice_in_dim(bias, core * mine, mine, 1)

    part = lax.dynamic_slice_in_dim(w_first, core * mine, mine, 1)
    part = [part[:, k * CUT : (k + 1) * CUT] for k in range(mine // CUT)]
    order, pieces = gather_pieces(jnp.concatenate(part), z, low)

    x, g = patches[0], out_grad[0]
    conv = conv_part(0, x, taps, pieces[2], None)
    conv = conv_part(1, x, taps, pieces[4], conv)
    conv = conv_part(2, x, taps, pieces[5], conv)
    normed, std, inv, gb = norm(conv, g, row_counts, gain, shift, scale, pieces[6])
    normed_other, gb_other = move(normed, flip=1), move(gb, flip=1)
    terms, gn_mine, gn_theirs, grad_bias, scale_sum = mlp(
        core.reshape(1), order, normed, normed_other, gb, gb_other, bias, second, pieces
    )
    gn_other = move(gn_theirs, flip=1)
    scale_sum = scale_sum / scale
    grad_conv, channel_sums = unnorm(gn_mine, gn_other, std, inv, gain)
    grad_taps = taps_part(0, x, grad_conv, terms, None)
    grad_taps = taps_part(1, x, grad_conv, terms, grad_taps)
    grad_taps = taps_part(2, x, grad_conv, terms, grad_taps)
    in_grad = back_part(0, g, grad_conv, row_counts, taps, terms, None)
    in_grad = back_part(1, g, grad_conv, row_counts, taps, terms, in_grad)
    in_grad = back_part(2, g, grad_conv, row_counts, taps, terms, in_grad)

    terms = lax.all_to_all(terms, "dp", 0, 0, tiled=True, axis_index_groups=same_core)
    terms = add_up(terms, in_grad)
    first = terms[: fsdp * flat[0]].reshape((fsdp,) + flat)
    second = terms[fsdp * flat[0] :].reshape((fsdp // 2, 2) + flat)
    swapped = move(second[:, 1], flip=1)
    second = jnp.where(
        core == 0,
        jnp.concatenate([second[:, 0], swapped]),
        jnp.concatenate([swapped, second[:, 0]]),
    )
    sums = jnp.concatenate([grad_taps, channel_sums, scale_sum], axis=0)
    sums = sums.reshape(sums.shape[0], fsdp, own).transpose(1, 0, 2)
    grad_bias = jnp.concatenate([grad_bias, grad_bias], axis=1).reshape(fsdp, -1, own)
    computed = (jnp.arange(fsdp, dtype=jnp.int32) // (fsdp // 2) == core)[:, None, None]
    sums = jnp.concatenate([sums, jnp.where(computed, grad_bias, 0.0)], axis=1)
    terms = jnp.concatenate([first, second, pack(sums.astype(BF16))], axis=1)
    terms = lax.all_to_all(terms, "fsdp", 0, 0, tiled=True)
    terms = jnp.sum(terms.astype(F32), axis=0).astype(BF16)
    terms = lax.all_to_all(
        jnp.broadcast_to(terms[None], (dp,) + terms.shape), "dp", 0, 0, tiled=True
    )
    factor = 1.0 / math.sqrt(fsdp * dp * ROWS * SPOTS)
    first, second, sums = finish(
        side.reshape(1), terms, (own, hidden), (units, channels), factor
    )
    sums = unpack(sums, lines, own)
    return (
        in_grad[None],
        first,
        second,
        sums[:tap_count],
        sums[tap_count + 3 :].reshape(units),
        sums[tap_count : tap_count + 3],
    )


def solution(mesh):
    placed = (
        P("fsdp", "dp", None, None, None),
        P("fsdp", "dp", None, None, None),
        P("fsdp", "dp"),
        P(None, "fsdp"),
        P("fsdp"),
        P("fsdp"),
        P("fsdp", None),
        P("fsdp"),
        P("fsdp", None),
        P("fsdp"),
    )
    return jax.shard_map(
        local,
        mesh=mesh,
        in_specs=placed,
        out_specs=(
            P("fsdp", "dp", None, None, None),
            P("fsdp", None),
            P("fsdp", None),
            P(None, "fsdp"),
            P("fsdp"),
            P(None, "fsdp"),
        ),
        check_vma=False,
    )
```

profile of v0, /device:TPU:1, one launch (start us, length us, event | category | flops | bytes accessed | tf_op | source)
XLA Modules:
  0.0 226.0 jit_solution(13878192466281283154)
XLA Ops:
  0.7 1.2 reshape.125
  2.0 0.8 copy.43
  2.8 0.7 reshape.128
  4.4 0.8 broadcast_in_dim.40
  5.2 10.1 %all-to-all-start = ((bf16[16,88,128]{2,1,0:T(8,128)(2,1)}), bf16[16,88,128]{2,1,0:T(8,128)(2,1)S(1)}, u32[]{:S(2)}, u32[]{:S(2)}) async-start(bf16[16,88,128]{2,1,0:T(8,128)(2,1)} %broadcast_in_dim.40), calls=%async_computation | async-start | bytes 720896 | tf_op jit(solution)/shard_map/all_to_all | solution.py:792
  15.4 1.4 collective-permute-start
  16.8 2.4 %collective-permute-done = bf16[144,384]{1,0:T(8,128)(2,1)S(1)} collective-permute-done((bf16[144,384]{1,0:T(8,128)(2,1)S(1)}, bf16[144,384]{1,0:T(8,128)(2,1)S(1)}, u32[]{:S(2)}, u32[]{:S(2)}) %collective-permute-start) | collective-permute-done | bytes 110624 | tf_op jit(solution)/shard_map/ppermute | solution.py:644
  19.3 2.0 collective-permute-start.1
  21.3 1.4 collective-permute-start.4
  22.7 8.4 %collective-permute-done.1.refs_1_ = bf16[288,384]{1,0:T(8,128)(2,1)S(1)} collective-permute-done((bf16[288,384]{1,0:T(8,128)(2,1)S(1)}, bf16[288,384]{1,0:T(8,128)(2,1)S(1)}, u32[]{:S(2)}, u32[]{:S(2)}) %collective-permute-start.1) | collective-permute-done | bytes 221216 | tf_op jit(solution)/shard_map/ppermute | solution.py:640
  31.1 2.7 %collective-permute-start.5 = (bf16[288,384]{1,0:T(8,128)(2,1)S(1)}, bf16[288,384]{1,0:T(8,128)(2,1)S(1)}, u32[]{:S(2)}, u32[]{:S(2)}) collective-permute-start(bf16[288,384]{1,0:T(8,128)(2,1)S(1)} %collective-permute-done.4._after._buffer.refs_2_), channel_id=1, source_target_pairs={{0,14},{16,30},{2,0},{18,16},{4,2},{20,18},{6,4},{22,20},{8,6},{24... | collective-permute-start | bytes 663560 | tf_op jit(solution)/shard_map/ppermute | solution.py:640
  34.5 3.7 %collective-permute-done.2.refs_3_ = bf16[288,384]{1,0:T(8,128)(2,1)} collective-permute-done((bf16[288,384]{1,0:T(8,128)(2,1)S(1)}, bf16[288,384]{1,0:T(8,128)(2,1)}, u32[]{:S(2)}, u32[]{:S(2)}) %collective-permute-start.2) | collective-permute-done | bytes 221216 | tf_op jit(solution)/shard_map/ppermute | solution.py:640
  38.2 2.7 %collective-permute-start.6 = (bf16[288,384]{1,0:T(8,128)(2,1)S(1)}, bf16[288,384]{1,0:T(8,128)(2,1)S(1)}, u32[]{:S(2)}, u32[]{:S(2)}) collective-permute-start(bf16[288,384]{1,0:T(8,128)(2,1)S(1)} %collective-permute-done.5._after.refs_4_), channel_id=1, source_target_pairs={{0,14},{16,30},{2,0},{18,16},{4,2},{20,18},{6,4},{22,20},{8,6},{24... | collective-permute-start | bytes 663560 | tf_op jit(solution)/shard_map/ppermute | solution.py:640
  40.9 2.7 %collective-permute-start.9 = (bf16[8,56,128]{2,1,0:T(8,128)(2,1)S(1)}, bf16[8,56,128]{2,1,0:T(8,128)(2,1)S(1)}, u32[]{:S(2)}, u32[]{:S(2)}) collective-permute-start(bf16[8,56,128]{2,1,0:T(8,128)(2,1)S(1)} %get-tuple-element.62), channel_id=1, source_target_pairs={{0,16},{16,0},{2,18},{18,2},{4,20},{20,4},{6,22},{22,6},{8,24},{24... | collective-permute-start | bytes 344072 | tf_op jit(solution)/shard_map/ppermute | solution.py:640
  43.7 0.9 collective-permute-done.9
  44.6 1.5 broadcast_in_dim.41
  46.1 6.4 %all-to-all-start.1 = ((bf16[8,896,128]{2,1,0:T(8,128)(2,1)}), bf16[8,896,128]{2,1,0:T(8,128)(2,1)}, u32[]{:S(2)}, u32[]{:S(2)}) async-start(bf16[8,896,128]{2,1,0:T(8,128)(2,1)} %broadcast_in_dim.41), calls=%async_computation.1 | async-start | bytes 3670016 | tf_op jit(solution)/shard_map/all_to_all | solution.py:799
  53.8 3.6 %conv.3._buffer = f32[896,768]{1,0:T(8,128)S(1)} custom-call(bf16[14,8,8,768]{3,2,1,0:T(8,128)(2,1)S(1)} %bitcast.41, f32[49,768]{1,0:T(8,128)S(1)} %reshape.136.taps_ref, bf16[288,384]{1,0:T(8,128)(2,1)S(1)} %collective-permute-done.4._after._buffer.refs_2_, bf16[288,384]{1,0:T(8,128)(2,1)S(1)} %collective-permute-done.4._after._buffer.refs_2_), custom_call_target="tpu_custom_call" | custom-call | flops 22478848 | bytes 1376256 | tf_op jit(solution)/shard_map/conv/pallas_call | solution.py:111
  57.4 3.6 %conv.4._buffer = f32[896,768]{1,0:T(8,128)S(1)} custom-call(bf16[14,8,8,768]{3,2,1,0:T(8,128)(2,1)S(1)} %bitcast.42, f32[49,768]{1,0:T(8,128)S(1)} %reshape.136.taps_ref, bf16[288,384]{1,0:T(8,128)(2,1)S(1)} %collective-permute-done.5._after.refs_4_, f32[896,768]{1,0:T(8,128)S(1)} %conv.3._buffer), custom_call_target="tpu_custom_call", output_to_operand_aliasing={{}: (3, {})} | custom-call | flops 22478848 | bytes 1376256 | tf_op jit(solution)/shard_map/conv/pallas_call | solution.py:111
  61.0 3.6 %conv.5.conv_ref = f32[896,768]{1,0:T(8,128)S(1)} custom-call(bf16[14,8,8,768]{3,2,1,0:T(8,128)(2,1)S(1)} %bitcast.43, f32[49,768]{1,0:T(8,128)S(1)} %reshape.136.taps_ref, bf16[288,384]{1,0:T(8,128)(2,1)S(1)} %collective-permute-done.3._after.refs_5_, f32[896,768]{1,0:T(8,128)S(1)} %conv.4._buffer), custom_call_target="tpu_custom_call", output_to_operand_aliasing={{}: (3, {})} | custom-call | flops 22478848 | bytes 1376256 | tf_op jit(solution)/shard_map/conv/pallas_call | solution.py:111
  64.6 5.2 %norm.1 = (bf16[896,768]{1,0:T(8,128)(2,1)S(1)}, f32[896,768]{1,0:T(8,128)S(1)}, f32[896,1]{1,0:T(8,128)S(1)}, bf16[896,768]{1,0:T(8,128)(2,1)}) custom-call(f32[896,768]{1,0:T(8,128)S(1)} %conv.5.conv_ref, bf16[14,8,8,768]{3,2,1,0:T(8,128)(2,1)S(1)} %bitcast.48, s32[1,1]{1,0:T(1,128)S(6)} %copy.61.count_ref, f32[1,768]{1,0:T(1,128)S(1)} %reshape.137.gain_ref, ...), custom_call_target="tpu_custom_call" | custom-call | flops 13762560 | bytes 9633792 | tf_op jit(solution)/shard_map/norm/pallas_call | solution.py:176
  69.8 1.6 copy-done.7
  73.8 7.1 %collective-permute-done.10.refs_7_ = bf16[288,384]{1,0:T(8,128)(2,1)S(1)} collective-permute-done((bf16[288,384]{1,0:T(8,128)(2,1)S(1)}, bf16[288,384]{1,0:T(8,128)(2,1)S(1)}, u32[]{:S(2)}, u32[]{:S(2)}) %collective-permute-start.10) | collective-permute-done | bytes 221216 | tf_op jit(solution)/shard_map/ppermute | solution.py:640
  81.6 34.4 %mlp.1 = (bf16[8,1792,128]{2,1,0:T(8,128)(2,1)}, f32[896,768]{1,0:T(8,128)}, bf16[896,768]{1,0:T(8,128)(2,1)}, f32[1,1152]{1,0:T(1,128)}, f32[1,768]{1,0:T(1,128)}) custom-call(s32[1]{0:T(128)} %bitcast.1.core_ref, s32[16]{0:T(128)} %stack.67.order_ref, bf16[896,768]{1,0:T(8,128)(2,1)} %copy-done.16, bf16[896,768]{1,0:T(8,128)(2,1)} %collective-permute-done.7.theirs_ref, ...), custom_call_target="tpu_custom_call" | custom-call | flops 15854469120 | bytes 10616832 | tf_op jit(solution)/shard_map/mlp/pallas_call | solution.py:373
  116.1 6.9 %all-to-all-start.2 = ((bf16[8,1792,128]{2,1,0:T(8,128)(2,1)}), bf16[8,1792,128]{2,1,0:T(8,128)(2,1)}, u32[]{:S(2)}, u32[]{:S(2)}) async-start(bf16[8,1792,128]{2,1,0:T(8,128)(2,1)} %get-tuple-element.27._after._buffer), calls=%async_computation.2 | async-start | bytes 7340032 | tf_op jit(solution)/shard_map/all_to_all | solution.py:833
  123.0 1.6 collective-permute-start.11
  124.9 2.7 %collective-permute-done.11.gn_other_ref = bf16[896,768]{1,0:T(8,128)(2,1)S(1)} collective-permute-done((bf16[896,768]{1,0:T(8,128)(2,1)}, bf16[896,768]{1,0:T(8,128)(2,1)S(1)}, u32[]{:S(2)}, u32[]{:S(2)}) %collective-permute-start.11) | collective-permute-done | bytes 1376288 | tf_op jit(solution)/shard_map/ppermute | solution.py:640
  127.6 1.1 copy-done.10
  128.7 1.8 copy-done.8
  130.5 1.8 copy-done.9
  132.3 1.3 copy-done.11
  133.6 4.5 %unnorm.1 = (f32[896,768]{1,0:T(8,128)S(1)}, f32[2,768]{1,0:T(2,128)S(1)}) custom-call(f32[896,768]{1,0:T(8,128)S(1)} %copy-done.9, bf16[896,768]{1,0:T(8,128)(2,1)S(1)} %copy-done.11, f32[896,768]{1,0:T(8,128)S(1)} %copy-done.8, f32[896,1]{1,0:T(8,128)S(1)} %get-tuple-element.25.inv_ref, f32[1,768]{1,0:T(1,128)S(1)} %reshape.137.gain_ref), custom_call_target="tpu_custom_call" | custom-call | flops 13762560 | bytes 9633792 | tf_op jit(solution)/shard_map/unnorm/pallas_call | solution.py:459
  138.2 4.6 %taps.3._buffer = f32[49,768]{1,0:T(8,128)S(1)} custom-call(bf16[14,8,8,768]{3,2,1,0:T(8,128)(2,1)S(1)} %bitcast.44, f32[896,768]{1,0:T(8,128)S(1)} %get-tuple-element.26.grad_ref, bf16[8,1792,128]{2,1,0:T(8,128)(2,1)S(1)} %copy-done, bf16[8,1792,128]{2,1,0:T(8,128)(2,1)S(1)} %copy-done), custom_call_target="tpu_custom_call" | custom-call | flops 22478848 | bytes 1376256 | tf_op jit(solution)/shard_map/taps/pallas_call | solution.py:533
  142.8 4.6 %taps.4._buffer = f32[49,768]{1,0:T(8,128)S(1)} custom-call(bf16[14,8,8,768]{3,2,1,0:T(8,128)(2,1)S(1)} %bitcast.45, f32[896,768]{1,0:T(8,128)S(1)} %get-tuple-element.26.grad_ref, bf16[8,1792,128]{2,1,0:T(8,128)(2,1)S(1)} %copy-done, f32[49,768]{1,0:T(8,128)S(1)} %taps.3._buffer), custom_call_target="tpu_custom_call", output_to_operand_aliasing={{}: (3, {})} | custom-call | flops 22478848 | bytes 1376256 | tf_op jit(solution)/shard_map/taps/pallas_call | solution.py:533
  147.3 4.6 %taps.5 = f32[49,768]{1,0:T(8,128)S(1)} custom-call(bf16[14,8,8,768]{3,2,1,0:T(8,128)(2,1)S(1)} %bitcast.46, f32[896,768]{1,0:T(8,128)S(1)} %get-tuple-element.26.grad_ref, bf16[8,1792,128]{2,1,0:T(8,128)(2,1)S(1)} %copy-done, f32[49,768]{1,0:T(8,128)S(1)} %taps.4._buffer), custom_call_target="tpu_custom_call", output_to_operand_aliasing={{}: (3, {})} | custom-call | flops 22478848 | bytes 1376256 | tf_op jit(solution)/shard_map/taps/pallas_call | solution.py:533
  152.2 2.0 copy-done.1
  154.3 1.3 copy-done.6
  155.6 4.4 %back.3._buffer = f32[14,8,8,768]{3,2,1,0:T(8,128)} custom-call(bf16[14,8,8,768]{3,2,1,0:T(8,128)(2,1)S(1)} %bitcast.49, f32[896,768]{1,0:T(8,128)S(1)} %get-tuple-element.26.grad_ref, s32[1,1]{1,0:T(1,128)S(6)} %copy.61.count_ref, f32[49,768]{1,0:T(8,128)S(1)} %reshape.136.taps_ref, bf16[8,1792,128]{2,1,0:T(8,128)(2,1)S(1)} %copy-done.1, ...), custom_call_target="tpu_custom_call" | custom-call | flops 22478848 | bytes 2293760 | tf_op jit(solution)/shard_map/back/pallas_call | solution.py:597
  160.0 4.4 %back.4._buffer = f32[14,8,8,768]{3,2,1,0:T(8,128)} custom-call(bf16[14,8,8,768]{3,2,1,0:T(8,128)(2,1)S(1)} %bitcast.50, f32[896,768]{1,0:T(8,128)S(1)} %get-tuple-element.26.grad_ref, s32[1,1]{1,0:T(1,128)S(6)} %copy.61.count_ref, f32[49,768]{1,0:T(8,128)S(1)} %reshape.136.taps_ref, ...), custom_call_target="tpu_custom_call", output_to_operand_aliasing={{}: (5, {})} | custom-call | flops 22478848 | bytes 2293760 | tf_op jit(solution)/shard_map/back/pallas_call | solution.py:597
  164.3 4.4 %back.5._after = f32[14,8,8,768]{3,2,1,0:T(8,128)} custom-call(bf16[14,8,8,768]{3,2,1,0:T(8,128)(2,1)S(1)} %bitcast.51, f32[896,768]{1,0:T(8,128)S(1)} %get-tuple-element.26.grad_ref, s32[1,1]{1,0:T(1,128)S(6)} %copy.61.count_ref, f32[49,768]{1,0:T(8,128)S(1)} %reshape.136.taps_ref, ...), custom_call_target="tpu_custom_call", output_to_operand_aliasing={{}: (5, {})} | custom-call | flops 22478848 | bytes 2293760 | tf_op jit(solution)/shard_map/back/pallas_call | solution.py:597
  168.7 5.8 %all-to-all-done.2.terms_ref = bf16[8,1792,128]{2,1,0:T(8,128)(2,1)} async-done(((bf16[8,1792,128]{2,1,0:T(8,128)(2,1)}), bf16[8,1792,128]{2,1,0:T(8,128)(2,1)}, u32[]{:S(2)}, u32[]{:S(2)}) %all-to-all-start.2) | async-done | bytes 3670048 | tf_op jit(solution)/shard_map/all_to_all | solution.py:833
  174.6 1.8 copy-done.4
  176.4 2.6 %add_up.1 = bf16[1792,128]{1,0:T(8,128)(2,1)S(1)} custom-call(bf16[8,1792,128]{2,1,0:T(8,128)(2,1)} %all-to-all-done.2.terms_ref, f32[14,8,8,768]{3,2,1,0:T(8,128)S(1)} %copy-done.4), custom_call_target="tpu_custom_call" | custom-call | tf_op jit(solution)/shard_map/add_up/pallas_call | solution.py:675
  179.0 2.1 collective-permute-start.12
  181.2 0.8 collective-permute-done.12
  182.2 22.5 %all_to_all.25 = bf16[16,144,128]{2,1,0:T(8,128)(2,1)S(1)} all-to-all(bf16[16,144,128]{2,1,0:T(8,128)(2,1)S(1)} %fusion.1), channel_id=1, replica_groups=mesh['dp'=16,'fsdp'=16] {'fsdp'}, dimensions={0} | all-to-all | bytes 1179648 | tf_op jit(solution)/shard_map/all_to_all | solution.py:849
  204.9 18.1 %all_to_all.26.terms_ref = bf16[16,144,128]{2,1,0:T(8,128)(2,1)S(1)} all-to-all(bf16[16,144,128]{2,1,0:T(8,128)(2,1)S(1)} %broadcast_in_dim.45), channel_id=1, replica_groups=mesh['dp'=16,'fsdp'=16] {'dp'}, dimensions={0} | all-to-all | bytes 1179648 | tf_op jit(solution)/shard_map/all_to_all | solution.py:851
  223.0 1.0 finish.1
  (100 shorter events, 8.6 us)
Async XLA Ops:
  0.7 14.7 %copy-start.18 = (bf16[48,2304]{1,0:T(8,128)(2,1)S(1)}, bf16[48,2304]{1,0:T(8,128)(2,1)}, u32[]{:S(2)}) copy-start(bf16[48,2304]{1,0:T(8,128)(2,1)} %param.16) | copy-start | bytes 663556
  5.2 35.7 %all-to-all-start = ((bf16[16,88,128]{2,1,0:T(8,128)(2,1)}), bf16[16,88,128]{2,1,0:T(8,128)(2,1)S(1)}, u32[]{:S(2)}, u32[]{:S(2)}) async-start(bf16[16,88,128]{2,1,0:T(8,128)(2,1)} %broadcast_in_dim.40), calls=%async_computation | async-start | bytes 720896 | tf_op jit(solution)/shard_map/all_to_all | solution.py:792
  15.4 3.9 %collective-permute-start = (bf16[144,384]{1,0:T(8,128)(2,1)S(1)}, bf16[144,384]{1,0:T(8,128)(2,1)S(1)}, u32[]{:S(2)}, u32[]{:S(2)}) collective-permute-start(bf16[144,384]{1,0:T(8,128)(2,1)S(1)} %pad_maximum_fusion.4), channel_id=1, source_target_pairs={{0,1},{1,0},{2,3},{3,2},{4,5},{5,4},{6,7},{7,6},{8,9},{9,8},{10,11... | collective-permute-start | bytes 331784 | tf_op jit(solution)/shard_map/ppermute | solution.py:644
  19.3 11.8 %copy-start.17 = (bf16[288,384]{1,0:T(8,128)(2,1)}, bf16[288,384]{1,0:T(8,128)(2,1)S(1)}, u32[]{:S(2)}) copy-start(bf16[288,384]{1,0:T(8,128)(2,1)S(1)} %pad_maximum_fusion.2.refs_0_) | copy-start | bytes 663556
  19.3 11.8 %collective-permute-start.1 = (bf16[288,384]{1,0:T(8,128)(2,1)S(1)}, bf16[288,384]{1,0:T(8,128)(2,1)S(1)}, u32[]{:S(2)}, u32[]{:S(2)}) collective-permute-start(bf16[288,384]{1,0:T(8,128)(2,1)S(1)} %pad_maximum_fusion.2.refs_0_), channel_id=1, source_target_pairs={{0,2},{16,18},{2,4},{18,20},{4,6},{20,22},{6,8},{22,24},{8,10},{24... | collective-permute-start | bytes 663560 | tf_op jit(solution)/shard_map/ppermute | solution.py:640
  21.3 9.8 %collective-permute-start.4 = (bf16[288,384]{1,0:T(8,128)(2,1)S(1)}, bf16[288,384]{1,0:T(8,128)(2,1)S(1)}, u32[]{:S(2)}, u32[]{:S(2)}) collective-permute-start(bf16[288,384]{1,0:T(8,128)(2,1)S(1)} %pad_maximum_fusion.2.refs_0_), channel_id=1, source_target_pairs={{0,14},{16,30},{2,0},{18,16},{4,2},{20,18},{6,4},{22,20},{8,6},{24... | collective-permute-start | bytes 663560 | tf_op jit(solution)/shard_map/ppermute | solution.py:640
  31.1 3.4 %copy-start.21 = (bf16[288,384]{1,0:T(8,128)(2,1)}, bf16[288,384]{1,0:T(8,128)(2,1)S(1)}, u32[]{:S(2)}) copy-start(bf16[288,384]{1,0:T(8,128)(2,1)S(1)} %collective-permute-done.1.refs_1_) | copy-start | bytes 663556
  31.1 7.1 %collective-permute-start.2 = (bf16[288,384]{1,0:T(8,128)(2,1)S(1)}, bf16[288,384]{1,0:T(8,128)(2,1)}, u32[]{:S(2)}, u32[]{:S(2)}) collective-permute-start(bf16[288,384]{1,0:T(8,128)(2,1)S(1)} %collective-permute-done.1.refs_1_), channel_id=1, source_target_pairs={{0,2},{16,18},{2,4},{18,20},{4,6},{20,22},{6,8},{22,24},{8,10},{24... | collective-permute-start | bytes 663560 | tf_op jit(solution)/shard_map/ppermute | solution.py:640
  31.1 22.1 %copy-start.12 = (bf16[288,384]{1,0:T(8,128)(2,1)}, bf16[288,384]{1,0:T(8,128)(2,1)S(1)}, u32[]{:S(2)}) copy-start(bf16[288,384]{1,0:T(8,128)(2,1)S(1)} %collective-permute-done.4._after._buffer.refs_2_) | copy-start | bytes 663556
  31.1 7.1 %collective-permute-start.5 = (bf16[288,384]{1,0:T(8,128)(2,1)S(1)}, bf16[288,384]{1,0:T(8,128)(2,1)S(1)}, u32[]{:S(2)}, u32[]{:S(2)}) collective-permute-start(bf16[288,384]{1,0:T(8,128)(2,1)S(1)} %collective-permute-done.4._after._buffer.refs_2_), channel_id=1, source_target_pairs={{0,14},{16,30},{2,0},{18,16},{4,2},{20,18},{6,4},{22,20},{8,6},{24... | collective-permute-start | bytes 663560 | tf_op jit(solution)/shard_map/ppermute | solution.py:640
  38.2 22.8 %collective-permute-start.3 = (bf16[288,384]{1,0:T(8,128)(2,1)}, bf16[288,384]{1,0:T(8,128)(2,1)S(1)}, u32[]{:S(2)}, u32[]{:S(2)}) collective-permute-start(bf16[288,384]{1,0:T(8,128)(2,1)} %collective-permute-done.2.refs_3_), channel_id=1, source_target_pairs={{0,2},{16,18},{2,4},{18,20},{4,6},{20,22},{6,8},{22,24},{8,10},{24... | collective-permute-start | bytes 663560 | tf_op jit(solution)/shard_map/ppermute | solution.py:640
  38.2 19.2 %copy-start.13 = (bf16[288,384]{1,0:T(8,128)(2,1)}, bf16[288,384]{1,0:T(8,128)(2,1)S(1)}, u32[]{:S(2)}) copy-start(bf16[288,384]{1,0:T(8,128)(2,1)S(1)} %collective-permute-done.5._after.refs_4_) | copy-start | bytes 663556
  38.2 26.4 %collective-permute-start.6 = (bf16[288,384]{1,0:T(8,128)(2,1)S(1)}, bf16[288,384]{1,0:T(8,128)(2,1)S(1)}, u32[]{:S(2)}, u32[]{:S(2)}) collective-permute-start(bf16[288,384]{1,0:T(8,128)(2,1)S(1)} %collective-permute-done.5._after.refs_4_), channel_id=1, source_target_pairs={{0,14},{16,30},{2,0},{18,16},{4,2},{20,18},{6,4},{22,20},{8,6},{24... | collective-permute-start | bytes 663560 | tf_op jit(solution)/shard_map/ppermute | solution.py:640
  40.9 3.7 %collective-permute-start.9 = (bf16[8,56,128]{2,1,0:T(8,128)(2,1)S(1)}, bf16[8,56,128]{2,1,0:T(8,128)(2,1)S(1)}, u32[]{:S(2)}, u32[]{:S(2)}) collective-permute-start(bf16[8,56,128]{2,1,0:T(8,128)(2,1)S(1)} %get-tuple-element.62), channel_id=1, source_target_pairs={{0,16},{16,0},{2,18},{18,2},{4,20},{20,4},{6,22},{22,6},{8,24},{24... | collective-permute-start | bytes 344072 | tf_op jit(solution)/shard_map/ppermute | solution.py:640
  46.1 34.9 %all-to-all-start.1 = ((bf16[8,896,128]{2,1,0:T(8,128)(2,1)}), bf16[8,896,128]{2,1,0:T(8,128)(2,1)}, u32[]{:S(2)}, u32[]{:S(2)}) async-start(bf16[8,896,128]{2,1,0:T(8,128)(2,1)} %broadcast_in_dim.41), calls=%async_computation.1 | async-start | bytes 3670016 | tf_op jit(solution)/shard_map/all_to_all | solution.py:799
  52.4 1.3 copy-start.2
  61.0 3.7 %copy-start.5 = (bf16[1,14,8,8,768]{4,3,2,1,0:T(8,128)(2,1)S(1)}, bf16[1,14,8,8,768]{4,3,2,1,0:T(8,128)(2,1)}, u32[]{:S(2)}) copy-start(bf16[1,14,8,8,768]{4,3,2,1,0:T(8,128)(2,1)} %param.11) | copy-start | bytes 4128772
  61.0 12.0 %copy-start.14 = (bf16[288,384]{1,0:T(8,128)(2,1)}, bf16[288,384]{1,0:T(8,128)(2,1)S(1)}, u32[]{:S(2)}) copy-start(bf16[288,384]{1,0:T(8,128)(2,1)S(1)} %collective-permute-done.3._after.refs_5_) | copy-start | bytes 663556
  64.6 5.2 %copy-start.15 = (bf16[288,384]{1,0:T(8,128)(2,1)}, bf16[288,384]{1,0:T(8,128)(2,1)S(1)}, u32[]{:S(2)}) copy-start(bf16[288,384]{1,0:T(8,128)(2,1)S(1)} %collective-permute-done.6._after.refs_6_) | copy-start | bytes 663556
  69.8 1.6 copy-start.7
  71.4 9.5 %copy-start.16 = (bf16[896,768]{1,0:T(8,128)(2,1)}, bf16[896,768]{1,0:T(8,128)(2,1)S(1)}, u32[]{:S(2)}) copy-start(bf16[896,768]{1,0:T(8,128)(2,1)S(1)} %get-tuple-element.20.mine_ref) | copy-start | bytes 4128772
  71.4 9.5 %collective-permute-start.7 = (bf16[896,768]{1,0:T(8,128)(2,1)S(1)}, bf16[896,768]{1,0:T(8,128)(2,1)}, u32[]{:S(2)}, u32[]{:S(2)}) collective-permute-start(bf16[896,768]{1,0:T(8,128)(2,1)S(1)} %get-tuple-element.20.mine_ref), channel_id=1, source_target_pairs={{0,16},{16,0},{2,18},{18,2},{4,20},{20,4},{6,22},{22,6},{8,24},{24... | collective-permute-start | bytes 4128776 | tf_op jit(solution)/shard_map/ppermute | solution.py:640
  72.1 8.9 %collective-permute-start.8 = (bf16[896,768]{1,0:T(8,128)(2,1)}, bf16[896,768]{1,0:T(8,128)(2,1)}, u32[]{:S(2)}, u32[]{:S(2)}) collective-permute-start(bf16[896,768]{1,0:T(8,128)(2,1)} %get-tuple-element.21.gb_mine_ref), channel_id=1, source_target_pairs={{0,16},{16,0},{2,18},{18,2},{4,20},{20,4},{6,22},{22,6},{8,24},{24... | collective-permute-start | bytes 4128776 | tf_op jit(solution)/shard_map/ppermute | solution.py:640
  73.0 8.0 %collective-permute-start.10 = (bf16[288,384]{1,0:T(8,128)(2,1)S(1)}, bf16[288,384]{1,0:T(8,128)(2,1)S(1)}, u32[]{:S(2)}, u32[]{:S(2)}) collective-permute-start(bf16[288,384]{1,0:T(8,128)(2,1)S(1)} %collective-permute-done.3._after.refs_5_), channel_id=1, source_target_pairs={{0,2},{16,18},{2,4},{18,20},{4,6},{20,22},{6,8},{22,24},{8,10},{24... | collective-permute-start | bytes 663560 | tf_op jit(solution)/shard_map/ppermute | solution.py:640
  80.9 0.7 copy-start.22
  116.1 8.6 %copy-start.19 = (f32[1,1152]{1,0:T(1,128)S(1)}, f32[1,1152]{1,0:T(1,128)}, u32[]{:S(2)}) copy-start(f32[1,1152]{1,0:T(1,128)} %get-tuple-element.30) | copy-start | bytes 13828
  116.1 8.7 %copy-start.20 = (f32[1,768]{1,0:T(1,128)S(1)}, f32[1,768]{1,0:T(1,128)}, u32[]{:S(2)}) copy-start(f32[1,768]{1,0:T(1,128)} %get-tuple-element.29) | copy-start | bytes 9220
  116.1 58.5 %all-to-all-start.2 = ((bf16[8,1792,128]{2,1,0:T(8,128)(2,1)}), bf16[8,1792,128]{2,1,0:T(8,128)(2,1)}, u32[]{:S(2)}, u32[]{:S(2)}) async-start(bf16[8,1792,128]{2,1,0:T(8,128)(2,1)} %get-tuple-element.27._after._buffer), calls=%async_computation.2 | async-start | bytes 7340032 | tf_op jit(solution)/shard_map/all_to_all | solution.py:833
  123.0 4.6 %collective-permute-start.11 = (bf16[896,768]{1,0:T(8,128)(2,1)}, bf16[896,768]{1,0:T(8,128)(2,1)S(1)}, u32[]{:S(2)}, u32[]{:S(2)}) collective-permute-start(bf16[896,768]{1,0:T(8,128)(2,1)} %get-tuple-element.23), channel_id=1, source_target_pairs={{0,16},{16,0},{2,18},{18,2},{4,20},{20,4},{6,22},{22,6},{8,24},{24... | collective-permute-start | bytes 4128776 | tf_op jit(solution)/shard_map/ppermute | solution.py:640
  127.6 1.1 copy-start.10
  128.7 1.8 copy-start.8
  130.5 1.8 copy-start.9
  132.3 1.3 copy-start.11
  133.6 4.5 %copy-start = (bf16[8,1792,128]{2,1,0:T(8,128)(2,1)S(1)}, bf16[8,1792,128]{2,1,0:T(8,128)(2,1)}, u32[]{:S(2)}) copy-start(bf16[8,1792,128]{2,1,0:T(8,128)(2,1)} %get-tuple-element.27._after._buffer) | copy-start | bytes 11010052
  133.6 4.6 %copy-start.3 = (bf16[1,14,8,8,768]{4,3,2,1,0:T(8,128)(2,1)S(1)}, bf16[1,14,8,8,768]{4,3,2,1,0:T(8,128)(2,1)}, u32[]{:S(2)}) copy-start(bf16[1,14,8,8,768]{4,3,2,1,0:T(8,128)(2,1)} %param.10) | copy-start | bytes 4128772
  152.2 2.0 copy-start.1
  154.3 1.3 copy-start.6
  174.6 1.8 copy-start.4
  179.0 3.0 %collective-permute-start.12 = (bf16[8,56,128]{2,1,0:T(8,128)(2,1)S(1)}, bf16[8,56,128]{2,1,0:T(8,128)(2,1)S(1)}, u32[]{:S(2)}, u32[]{:S(2)}) collective-permute-start(bf16[8,56,128]{2,1,0:T(8,128)(2,1)S(1)} %get-tuple-element.60), channel_id=1, source_target_pairs={{0,16},{16,0},{2,18},{18,2},{4,20},{20,4},{6,22},{22,6},{8,24},{24... | collective-permute-start | bytes 344072 | tf_op jit(solution)/shard_map/ppermute | solution.py:640
where the time goes:
time: 227 us; the launch traced here: 226 us
  Pallas kernels  85.3 us (38%)
  starting transfers between devices  41 us (18%)
  blocking collectives  40.7 us (18%)
  waiting for transfers between devices  31.8 us (14%)
  local copies, waits for them, and re-layouts  24.5 us (11%)
    pallas_call x1, Pallas kernels, mlp(): pl.pallas_call(functools.partial(mlp_kernel, count), grid=(2 * steps,), i...  34.4 us
    ppermute x12, waiting for transfers between devices, move(): return lax.ppermute(value, AXES, pairs)  23.5 us
    all_to_all x1, blocking collectives, local(): terms = lax.all_to_all(terms, 'fsdp', 0, 0, tiled=True)  22.5 us
    all_to_all x1, blocking collectives, local(): lax.all_to_all(jnp.broadcast_to(terms[None], (dp,) + terms.shape), 'dp',...  18.1 us
    ppermute x12, starting transfers between devices, move(): return lax.ppermute(value, AXES, pairs)  16.1 us
    unnamed x49, local copies, waits for them, and re-layouts  15.5 us
    pallas_call x3, Pallas kernels, taps_part(): pl.pallas_call(functools.partial(taps_kernel, slots), grid=(GROUP_STEPS,)...  13.7 us
    pallas_call x3, Pallas kernels, back_part(): pl.pallas_call(functools.partial(back_kernel, slots), grid=(GROUP_STEPS,)...  13.1 us
  transfers between devices with their start and end apart: 16, of which 8 were waited for; matrix products, arithmetic and copies ran while one was open for 2% of the time, Pallas kernels for 21%

commit v1 on v0

--- a/solution.py
+++ b/solution.py
@@ -15,8 +15,7 @@
 SPOTS = SIDE * SIDE
 REACH = 3
 TAPS = 7
-BLOCK = 384
-TOKEN_BLOCK = 448
+BLOCK = 256
 NORM_BLOCK = 128
 PART_TILES = 7
 GROUP_STEPS = 2
@@ -202,6 +201,20 @@
     return divmod(part * PART_TILES + i, across)
 
 
+def aligned(value, to):
+    return pl.multiple_of(value * to, to)
+
+
+def clear(ref):
+    tall = 2 * SUBLANES
+
+    def rows(i, _):
+        ref[pl.ds(aligned(i, tall), tall), :] = jnp.zeros((tall, ref.shape[1]), F32)
+        return 0
+
+    lax.fori_loop(0, ref.shape[0] // tall, rows, 0)
+
+
 def mlp_kernel(
     count, core_ref, order_ref, mine_ref, theirs_ref, gb_mine_ref, gb_theirs_ref, bias_ref,
     second_ref, *refs,
@@ -209,11 +222,11 @@
     pieces = refs[:count]
     (
         sums_ref, gn_mine_ref, gn_theirs_ref, grad_bias_ref, scale_ref,
-        first, second, sum_first, sum_second, tokens, cots, flipped, grad_normed, sems,
+        first, second, sum_first, sum_second, tokens, cots, flipped, grad_normed,
+        actives, grads, sems, more_sems,
     ) = refs[count:]
-    step = pl.program_id(0)
-    steps = pl.num_programs(0)
     channels, hidden = first.shape
+    half = mine_ref.shape[0]
     chips = second_ref.shape[0]
     cuts = hidden // CUT
     own = pieces[0].shape[0] // (2 * cuts)
@@ -224,169 +237,148 @@
     tall = 2 * SUBLANES
     dot = functools.partial(lax.dot_general, preferred_element_type=F32)
 
-    def aligned(value, to):
-        return pl.multiple_of(value * to, to)
-
-    @pl.when(step == 0)
-    def _():
-        made = []
-        for i, piece in enumerate(pieces):
-            for parity in range(2):
-                f = order_ref[2 * i + parity]
-                for k in range(cuts):
-                    made.append(
-                        pltpu.make_async_copy(
-                            piece.at[pl.ds((parity * cuts + k) * own, own), :],
-                            first.at[pl.ds(aligned(f, own), own), pl.ds(k * CUT, CUT)],
-                            sems.at[i],
-                        )
+    loads = [
+        pltpu.make_async_copy(src, dst.at[pl.ds(row, half), :], more_sems.at[i])
+        for i, (src, dst, row) in enumerate(
+            (
+                (mine_ref, tokens, 0),
+                (theirs_ref, tokens, half),
+                (gb_mine_ref, cots, 0),
+                (gb_theirs_ref, cots, half),
+            )
+        )
+    ]
+    for i, piece in enumerate(pieces):
+        for parity in range(2):
+            f = order_ref[2 * i + parity]
+            for k in range(cuts):
+                loads.append(
+                    pltpu.make_async_copy(
+                        piece.at[pl.ds((parity * cuts + k) * own, own), :],
+                        first.at[pl.ds(aligned(f, own), own), pl.ds(k * CUT, CUT)],
+                        sems.at[i],
                     )
-        for copy in made:
-            copy.start()
-
-        def unpack_shard(f, _):
-            for e in range(chips):
+                )
+    for load in loads:
+        load.start()
+
+    def unpack_shard(f, _):
+        for e in range(chips):
+            for i in range(PART_TILES):
+                r, c = tile_of(e, i, channels // LANES)
+                if r * tall < units:
+                    second[
+                        pl.ds(pl.multiple_of(f * units + r * tall, tall), tall),
+                        c * LANES : (c + 1) * LANES,
+                    ] = second_ref[
+                        e, pl.ds(pl.multiple_of(f * part_rows + i * tall, tall), tall), :
+                    ]
+        return 0
+
+    lax.fori_loop(0, shards // 2, unpack_shard, 0)
+    clear(grad_normed)
+    for load in loads:
+        load.wait()
+
+    def flip(j, _):
+        at = pl.ds(aligned(j, BLOCK), BLOCK)
+        flipped[:, at] = tokens[at, :].T
+        return 0
+
+    lax.fori_loop(0, 2 * half // BLOCK, flip, 0)
+
+    def chunk(start, wide):
+        units_at = pl.ds(start, wide)
+
+        def block(j, bias_sum):
+            at = pl.ds(aligned(j, half), half)
+            preact = dot(tokens[at, :], first[:, units_at], (((1,), (0,)), ((), ())))
+            preact = preact + bias_ref[:, units_at]
+            grad_hidden = dot(cots[at, :], second[units_at, :], (((1,), (1,)), ((), ())))
+            prob = 0.5 * (1.0 + lax.erf(preact * 0.7071067811865476))
+            actives[at, :wide] = (preact * prob).astype(BF16)
+            slope = prob + preact * jnp.exp(-0.5 * preact * preact) * 0.3989422804014327
+            grad_preact = (grad_hidden * slope).astype(BF16)
+            grads[at, :wide] = grad_preact
+            grad_normed[at, :] += dot(grad_preact, first[:, units_at], (((1,), (1,)), ((), ())))
+            return bias_sum + jnp.sum(grad_preact.astype(F32), axis=0, keepdims=True)
+
+        grad_bias_ref[:, units_at] = lax.fori_loop(
+            0, 2, block, jnp.zeros((1, wide), F32)
+        )
+        sum_second[units_at, :] = dot(actives[:, :wide], cots[...], (((0,), (0,)), ((), ())))
+        sum_first[:, units_at] = dot(flipped[...], grads[:, :wide], (((1,), (0,)), ((), ())))
+
+    def whole_chunk(h, _):
+        chunk(aligned(h, BLOCK), BLOCK)
+        return 0
+
+    lax.fori_loop(0, hidden // BLOCK, whole_chunk, 0)
+    if hidden % BLOCK:
+        chunk(hidden // BLOCK * BLOCK, hidden % BLOCK)
+
+    def unload(i, _):
+        at = pl.ds(aligned(i, tall), tall)
+        gn_mine_ref[at, :] = grad_normed[at, :]
+        gn_theirs_ref[at, :] = grad_normed[pl.ds(half + aligned(i, tall), tall), :].astype(BF16)
+        return 0
+
+    lax.fori_loop(0, half // tall, unload, 0)
+
+    def scale_rows(i, total):
+        at = pl.ds(aligned(i, tall), tall)
+        return total + sum_second[at, :] * second[at, :].astype(F32)
+
+    total = lax.fori_loop(0, hidden // tall, scale_rows, jnp.zeros((tall, channels), F32))
+    scale_ref[...] = jnp.sum(total, axis=0, keepdims=True)
+    none = jnp.zeros((SUBLANES, LANES), F32)
+
+    def pack_pair(pair, _):
+        for e in range(chips):
+            tiles = []
+            for f in range(2):
                 for i in range(PART_TILES):
-                    r, c = tile_of(e, i, channels // LANES)
-                    if r * tall < units:
-                        second[
-                            pl.ds(pl.multiple_of(f * units + r * tall, tall), tall),
-                            c * LANES : (c + 1) * LANES,
-                        ] = second_ref[
-                            e, pl.ds(pl.multiple_of(f * part_rows + i * tall, tall), tall), :
-                        ]
-            return 0
-
-        lax.fori_loop(0, shards // 2, unpack_shard, 0)
-        scale_ref[...] = jnp.zeros_like(scale_ref)
-        grad_bias_ref[...] = jnp.zeros_like(grad_bias_ref)
-
-        def clear(i, _):
-            sum_first[pl.ds(aligned(i, tall), tall), :] = jnp.zeros((tall, hidden), F32)
-            return 0
-
-        lax.fori_loop(0, channels // tall, clear, 0)
-
-        def clear_more(i, _):
-            sum_second[pl.ds(aligned(i, tall), tall), :] = jnp.zeros((tall, channels), F32)
-            return 0
-
-        lax.fori_loop(0, hidden // tall, clear_more, 0)
-        for copy in made:
-            copy.wait()
-
-    @pl.when(step < steps // 2)
-    def _():
-        tokens[...] = mine_ref[...]
-        cots[...] = gb_mine_ref[...]
-
-    @pl.when(step >= steps // 2)
-    def _():
-        tokens[...] = theirs_ref[...]
-        cots[...] = gb_theirs_ref[...]
-
-    flipped[...] = tokens[...].T
-    grad_normed[...] = jnp.zeros_like(grad_normed)
-
-    def chunk(h, _):
-        at = pl.ds(aligned(h, BLOCK), BLOCK)
-        normed, gb = tokens[...], cots[...]
-        preact = dot(normed, first[:, at], (((1,), (0,)), ((), ()))) + bias_ref[:, at]
-        grad_hidden = dot(gb, second[at, :], (((1,), (1,)), ((), ())))
-        prob = 0.5 * (1.0 + lax.erf(preact * 0.7071067811865476))
-        active = (preact * prob).astype(BF16)
-        slope = prob + preact * jnp.exp(-0.5 * preact * preact) * 0.3989422804014327
-        grad_preact = (grad_hidden * slope).astype(BF16)
-        sum_second[at, :] += dot(active, gb, (((0,), (0,)), ((), ())))
-        sum_first[:, at] += dot(flipped[...], grad_preact, (((1,), (0,)), ((), ())))
-        grad_bias_ref[:, at] += jnp.sum(grad_preact.astype(F32), axis=0, keepdims=True)
-        grad_normed[...] += dot(grad_preact, first[:, at], (((1,), (1,)), ((), ())))
-        return 0
-
-    lax.fori_loop(0, hidden // BLOCK, chunk, 0)
-
-    @pl.when(step < steps // 2)
-    def _():
-        gn_mine_ref[...] = grad_normed[...]
-
-    @pl.when(step >= steps // 2)
-    def _():
-        gn_theirs_ref[...] = grad_normed[...].astype(BF16)
-
-    @pl.when(step == steps - 1)
-    def _():
-        def scale_rows(i, total):
-            at = pl.ds(aligned(i, tall), tall)
-            return total + sum_second[at, :] * second[at, :].astype(F32)
-
-        total = lax.fori_loop(
-            0, hidden // tall, scale_rows, jnp.zeros((tall, channels), F32)
-        )
-        scale_ref[...] = jnp.sum(total, axis=0, keepdims=True)
-        none = jnp.zeros((SUBLANES, LANES), F32)
-
-        def pack_pair(pair, _):
-            for e in range(chips):
-                tiles = []
-                for f in range(2):
-                    for i in range(PART_TILES):
-                        r, c = tile_of(e, i, hidden // LANES)
-                        row = pl.multiple_of((2 * pair + f) * own + r * SUBLANES, SUBLANES)
-                        tiles.append(
-                            sum_first[pl.ds(row, SUBLANES), c * LANES : (c + 1) * LANES]
-                            if r * SUBLANES < own
-                            else none
-                        )
-                for i in range(0, len(tiles), 2):
-                    at = pl.multiple_of(pair * part_rows + i * SUBLANES, tall)
-                    sums_ref[e, pl.ds(at, tall), :] = jnp.concatenate(tiles[i : i + 2]).astype(BF16)
-            return 0
-
-        lax.fori_loop(0, shards // 2, pack_pair, 0)
-
-        def pack_shard(f, _):
-            for e in range(chips):
-                for i in range(PART_TILES):
-                    r, c = tile_of(e, i, channels // LANES)
-                    at = pl.multiple_of(first_rows + f * part_rows + i * tall, tall)
-                    if r * tall < units:
-                        row = pl.multiple_of(f * units + r * tall, tall)
-                        value = sum_second[pl.ds(row, tall), c * LANES : (c + 1) * LANES]
-                    else:
-                        value = jnp.zeros((tall, LANES), F32)
-                    sums_ref[e, pl.ds(at, tall), :] = value.astype(BF16)
-            return 0
-
-        lax.fori_loop(0, shards // 2, pack_shard, 0)
+                    r, c = tile_of(e, i, hidden // LANES)
+                    row = pl.multiple_of((2 * pair + f) * own + r * SUBLANES, SUBLANES)
+                    tiles.append(
+                        sum_first[pl.ds(row, SUBLANES), c * LANES : (c + 1) * LANES]
+                        if r * SUBLANES < own
+                        else none
+                    )
+            for i in range(0, len(tiles), 2):
+                at = pl.multiple_of(pair * part_rows + i * SUBLANES, tall)
+                sums_ref[e, pl.ds(at, tall), :] = jnp.concatenate(tiles[i : i + 2]).astype(BF16)
+        return 0
+
+    lax.fori_loop(0, shards // 2, pack_pair, 0)
+
+    def pack_shard(f, _):
+        for e in range(chips):
+            for i in range(PART_TILES):
+                r, c = tile_of(e, i, channels // LANES)
+                at = pl.multiple_of(first_rows + f * part_rows + i * tall, tall)
+                if r * tall < units:
+                    row = pl.multiple_of(f * units + r * tall, tall)
+                    value = sum_second[pl.ds(row, tall), c * LANES : (c + 1) * LANES]
+                else:
+                    value = jnp.zeros((tall, LANES), F32)
+                sums_ref[e, pl.ds(at, tall), :] = value.astype(BF16)
+        return 0
+
+    lax.fori_loop(0, shards // 2, pack_shard, 0)
 
 
 def mlp(core, order, mine, theirs, gb_mine, gb_theirs, bias, second, pieces):
     tokens, channels = mine.shape
-    count = len(pieces)
-    shards = 2 * count
-    hidden = bias.shape[1]
-    sums = (second.shape[0], shards * PART_TILES * SUBLANES + second.shape[1], LANES)
-    steps = tokens // TOKEN_BLOCK
-    early = pl.BlockSpec((TOKEN_BLOCK, channels), lambda j: (jnp.minimum(j, steps - 1), 0))
-    late = pl.BlockSpec((TOKEN_BLOCK, channels), lambda j: (jnp.maximum(j - steps, 0), 0))
+    count, hidden = len(pieces), bias.shape[1]
+    sums = (second.shape[0], 2 * count * PART_TILES * SUBLANES + second.shape[1], LANES)
+    smem = pl.BlockSpec(memory_space=pltpu.SMEM)
+    vmem = pl.BlockSpec(memory_space=pltpu.VMEM)
     anywhere = pl.BlockSpec(memory_space=pl.ANY)
     return pl.pallas_call(
         functools.partial(mlp_kernel, count),
-        grid=(2 * steps,),
-        in_specs=[
-            pl.BlockSpec(memory_space=pltpu.SMEM),
-            pl.BlockSpec(memory_space=pltpu.SMEM),
-            early, late, early, late,
-            whole((1, hidden)),
-            whole(second.shape),
-        ]
-        + [anywhere] * count,
-        out_specs=[
-            whole(sums),
-            early, late,
-            whole((1, hidden)),
-            whole((1, channels)),
-        ],
+        in_specs=[smem, smem] + [anywhere] * 4 + [vmem, vmem] + [anywhere] * count,
+        out_specs=[vmem] * 5,
         out_shape=[
             jax.ShapeDtypeStruct(sums, BF16),
             jax.ShapeDtypeStruct((tokens, channels), F32),
@@ -399,11 +391,14 @@
             pltpu.VMEM((hidden, channels), BF16),
             pltpu.VMEM((channels, hidden), F32),
             pltpu.VMEM((hidden, channels), F32),
-            pltpu.VMEM((TOKEN_BLOCK, channels), BF16),
-            pltpu.VMEM((TOKEN_BLOCK, channels), BF16),
-            pltpu.VMEM((channels, TOKEN_BLOCK), BF16),
-            pltpu.VMEM((TOKEN_BLOCK, channels), F32),
+            pltpu.VMEM((2 * tokens, channels), BF16),
+            pltpu.VMEM((2 * tokens, channels), BF16),
+            pltpu.VMEM((channels, 2 * tokens), BF16),
+            pltpu.VMEM((2 * tokens, channels), F32),
+            pltpu.VMEM((2 * tokens, BLOCK), BF16),
+            pltpu.VMEM((2 * tokens, BLOCK), BF16),
             pltpu.SemaphoreType.DMA((count,)),
+            pltpu.SemaphoreType.DMA((4,)),
         ],
         compiler_params=pltpu.CompilerParams(vmem_limit_bytes=VMEM_LIMIT),
         cost_estimate=pl.CostEstimate(
@@ -640,12 +635,13 @@
     return lax.ppermute(value, AXES, pairs)
 
 
-def gather_pieces(piece, z, low):
+def gather_pieces(piece, z, low, between):
     other = lax.ppermute(piece, "fsdp", [(i, i ^ 1) for i in range(2 * Z)])
     pair = jnp.concatenate([piece, other])
-    right = left = pair
-    pieces, away = [pair], [0]
-    for step in range(1, Z // 2 + 1):
+    right, left = move(pair, dz=1), move(pair, dz=-1)
+    right, left, made = between(right, left)
+    pieces, away = [pair, right, left], [0, Z - 1, 1]
+    for step in range(2, Z // 2 + 1):
         right = move(right, dz=1)
         pieces.append(right)
         away.append(Z - step)
@@ -654,7 +650,38 @@
             pieces.append(left)
             away.append(step)
     order = [(z + s) % Z * 2 + (low ^ parity) for s in away for parity in range(2)]
-    return jnp.stack(order).astype(jnp.int32), pieces
+    return jnp.stack(order).astype(jnp.int32), pieces, made
+
+
+def copies_kernel(kept_ref, swapped_ref, _right, _left, out_ref, _right_out, _left_out):
+    def shard(f, _):
+        both = [kept_ref[f].astype(F32), swapped_ref[f].astype(F32)]
+        both = jnp.concatenate(both).astype(BF16)
+        rows = both.shape[0]
+        for e in range(out_ref.shape[0]):
+            out_ref[e, pl.ds(pl.multiple_of(f * rows, rows), rows), :] = both
+        return 0
+
+    lax.fori_loop(0, kept_ref.shape[0], shard, 0)
+
+
+def copies(chips, kept, swapped, right, left):
+    shards, rows, lanes = kept.shape
+    vmem = pl.BlockSpec(memory_space=pltpu.VMEM)
+    anywhere = pl.BlockSpec(memory_space=pl.ANY)
+    return pl.pallas_call(
+        copies_kernel,
+        in_specs=[vmem, vmem, anywhere, anywhere],
+        out_specs=[vmem, anywhere, anywhere],
+        out_shape=[
+            jax.ShapeDtypeStruct((chips, shards * 2 * rows, lanes), BF16),
+            jax.ShapeDtypeStruct(right.shape, BF16),
+            jax.ShapeDtypeStruct(left.shape, BF16),
+        ],
+        input_output_aliases={2: 1, 3: 2},
+        compiler_params=pltpu.CompilerParams(vmem_limit_bytes=SMALL_VMEM),
+        name="copies",
+    )(kept, swapped, right, left)
 
 
 def add_up_kernel(terms_ref, _after, out_ref):
@@ -795,11 +822,16 @@
     tiles, small = small[:, : flat[0]], unpack(small[:, flat[0] :], lines, own)
     kept = lax.dynamic_slice_in_dim(tiles, core * (fsdp // 2), fsdp // 2)
     swapped = move(lax.dynamic_slice_in_dim(tiles, (1 - core) * (fsdp // 2), fsdp // 2), flip=1)
-    second = jnp.concatenate([kept, swapped], axis=1).reshape(fsdp * flat[0], LANES)
-    second = lax.all_to_all(
-        jnp.broadcast_to(second, (chips,) + second.shape),
-        "dp", 0, 0, tiled=True, axis_index_groups=same_core,
-    )
+
+    def between(right, left):
+        made, right, left = copies(chips, kept, swapped, right, left)
+        made = lax.all_to_all(made, "dp", 0, 0, tiled=True, axis_index_groups=same_core)
+        return right, left, made
+
+    part = lax.dynamic_slice_in_dim(w_first, core * mine, mine, 1)
+    part = [part[:, k * CUT : (k + 1) * CUT] for k in range(mine // CUT)]
+    order, pieces, second = gather_pieces(jnp.concatenate(part), z, low, between)
+
     taps = small[:, :tap_count].transpose(1, 0, 2).reshape(tap_count, channels).astype(F32)
     gain, shift, scale = (
         small[:, tap_count + i].reshape(1, channels).astype(F32) for i in range(3)
@@ -807,15 +839,11 @@
     bias = small[:, tap_count + 3 :].reshape(1, hidden).astype(F32)
     bias = lax.dynamic_slice_in_dim(bias, core * mine, mine, 1)
 
-    part = lax.dynamic_slice_in_dim(w_first, core * mine, mine, 1)
-    part = [part[:, k * CUT : (k + 1) * CUT] for k in range(mine // CUT)]
-    order, pieces = gather_pieces(jnp.concatenate(part), z, low)
-
     x, g = patches[0], out_grad[0]
-    conv = conv_part(0, x, taps, pieces[2], None)
+    conv = conv_part(0, x, taps, pieces[1], None)
     conv = conv_part(1, x, taps, pieces[4], conv)
-    conv = conv_part(2, x, taps, pieces[5], conv)
-    normed, std, inv, gb = norm(conv, g, row_counts, gain, shift, scale, pieces[6])
+    conv = conv_part(2, x, taps, pieces[6], conv)
+    normed, std, inv, gb = norm(conv, g, row_counts, gain, shift, scale, pieces[7])
     normed_other, gb_other = move(normed, flip=1), move(gb, flip=1)
     terms, gn_mine, gn_theirs, grad_bias, scale_sum = mlp(
         core.reshape(1), order, normed, normed_other, gb, gb_other, bias, second, pieces

time: 227 us -> 223 us (0.982)
  waiting for transfers between devices: 31.8 us -> 27.6 us
    ppermute x12, waiting for transfers between devices: 23.5 us -> 10.5 us  [move(): return lax.ppermute(value, AXES, pairs)]
    all_to_all x1, waiting for transfers between devices: 0.01 us -> 5.19 us  [local(): lax.all_to_all(jnp.broadcast_to(small, (fsdp,) + small.shape), 'fsdp', 0,...]
    pallas_call x1 -> x2, Pallas kernels: 34.4 us -> 35.1 us  [the longest x1 33.6 us: mlp(): pl.pallas_call(functools.partial(mlp_kernel, count), in_specs=[smem, smem...]
  transfers between devices with their start and end apart: 16 -> 16, of which waited for: 8 -> 9; matrix products, arithmetic and copies ran while one was open for 2% -> 1% of each run, Pallas kernels for 21% -> 21%
where the time goes in v1:
time: 223 us; the launch traced here: 222 us
  Pallas kernels  86 us (39%)
  blocking collectives  42.3 us (19%)
  starting transfers between devices  40.9 us (18%)
  waiting for transfers between devices  27.6 us (12%)
  local copies, waits for them, and re-layouts  22.3 us (10%)
    pallas_call x1, Pallas kernels, mlp(): pl.pallas_call(functools.partial(mlp_kernel, count), in_specs=[smem, smem...  33.6 us
    all_to_all x1, blocking collectives, local(): terms = lax.all_to_all(terms, 'fsdp', 0, 0, tiled=True)  23 us
    all_to_all x1, blocking collectives, local(): lax.all_to_all(jnp.broadcast_to(terms[None], (dp,) + terms.shape), 'dp',...  19.3 us
    ppermute x12, starting transfers between devices, move(): return lax.ppermute(value, AXES, pairs)  16.1 us
    unnamed x49, local copies, waits for them, and re-layouts  14.9 us
    pallas_call x3, Pallas kernels, taps_part(): pl.pallas_call(functools.partial(taps_kernel, slots), grid=(GROUP_STEPS,)...  13.7 us
    pallas_call x3, Pallas kernels, back_part(): pl.pallas_call(functools.partial(back_kernel, slots), grid=(GROUP_STEPS,)...  13.1 us
    pallas_call x3, Pallas kernels, conv_part(): pl.pallas_call(functools.partial(conv_kernel, slots), grid=(GROUP_STEPS,)...  10.8 us
  transfers between devices with their start and end apart: 16, of which 9 were waited for; matrix products, arithmetic and copies ran while one was open for 1% of the time, Pallas kernels for 21%

profile of v1, /device:TPU:1, one launch (start us, length us, event | category | flops | bytes accessed | tf_op | source)
XLA Modules:
  0.0 221.8 jit_solution(3197626860832923795)
XLA Ops:
  0.7 1.2 reshape.122
  2.0 0.8 copy.45
  4.4 0.8 broadcast_in_dim.37
  5.2 10.1 %all-to-all-start = ((bf16[16,88,128]{2,1,0:T(8,128)(2,1)}), bf16[16,88,128]{2,1,0:T(8,128)(2,1)S(1)}, u32[]{:S(2)}, u32[]{:S(2)}) async-start(bf16[16,88,128]{2,1,0:T(8,128)(2,1)} %broadcast_in_dim.37), calls=%async_computation | async-start | bytes 720896 | tf_op jit(solution)/shard_map/all_to_all | solution.py:819
  15.4 1.4 collective-permute-start.1
  16.8 2.4 %collective-permute-done.1 = bf16[144,384]{1,0:T(8,128)(2,1)S(1)} collective-permute-done((bf16[144,384]{1,0:T(8,128)(2,1)S(1)}, bf16[144,384]{1,0:T(8,128)(2,1)S(1)}, u32[]{:S(2)}, u32[]{:S(2)}) %collective-permute-start.1) | collective-permute-done | bytes 110624 | tf_op jit(solution)/shard_map/ppermute | solution.py:639
  19.3 2.0 collective-permute-start.2
  21.3 1.4 collective-permute-start.3
  22.7 5.2 %all-to-all-done = bf16[16,88,128]{2,1,0:T(8,128)(2,1)S(1)} async-done(((bf16[16,88,128]{2,1,0:T(8,128)(2,1)}), bf16[16,88,128]{2,1,0:T(8,128)(2,1)S(1)}, u32[]{:S(2)}, u32[]{:S(2)}) %all-to-all-start) | async-done | bytes 360480 | tf_op jit(solution)/shard_map/all_to_all | solution.py:819
  27.9 3.5 %collective-permute-start = (bf16[8,56,128]{2,1,0:T(8,128)(2,1)S(1)}, bf16[8,56,128]{2,1,0:T(8,128)(2,1)S(1)}, u32[]{:S(2)}, u32[]{:S(2)}) collective-permute-start(bf16[8,56,128]{2,1,0:T(8,128)(2,1)S(1)} %get-tuple-element.67), channel_id=1, source_target_pairs={{0,16},{16,0},{2,18},{18,2},{4,20},{20,4},{6,22},{22,6},{8,24},{24... | collective-permute-start | bytes 344072 | tf_op jit(solution)/shard_map/ppermute | solution.py:635
  31.5 1.0 collective-permute-done.swapped_ref
  32.4 1.5 copies.1
  34.6 2.7 %collective-permute-start.4 = (bf16[288,384]{1,0:T(8,128)(2,1)S(1)}, bf16[288,384]{1,0:T(8,128)(2,1)S(1)}, u32[]{:S(2)}, u32[]{:S(2)}) collective-permute-start(bf16[288,384]{1,0:T(8,128)(2,1)S(1)} %get-tuple-element.23.refs_2_), channel_id=1, source_target_pairs={{0,14},{16,30},{2,0},{18,16},{4,2},{20,18},{6,4},{22,20},{8,6},{24... | collective-permute-start | bytes 663560 | tf_op jit(solution)/shard_map/ppermute | solution.py:635
  37.3 4.5 %collective-permute-done.6.refs_3_ = bf16[288,384]{1,0:T(8,128)(2,1)S(1)} collective-permute-done((bf16[288,384]{1,0:T(8,128)(2,1)S(1)}, bf16[288,384]{1,0:T(8,128)(2,1)S(1)}, u32[]{:S(2)}, u32[]{:S(2)}) %collective-permute-start.6) | collective-permute-done | bytes 221216 | tf_op jit(solution)/shard_map/ppermute | solution.py:635
  42.5 6.4 %all-to-all-start.1 = ((bf16[8,896,128]{2,1,0:T(8,128)(2,1)}), bf16[8,896,128]{2,1,0:T(8,128)(2,1)}, u32[]{:S(2)}, u32[]{:S(2)}) async-start(bf16[8,896,128]{2,1,0:T(8,128)(2,1)} %get-tuple-element.27), calls=%async_computation.1 | async-start | bytes 3670016 | tf_op jit(solution)/shard_map/all_to_all | solution.py:828
  48.9 2.2 %collective-permute-start.5 = (bf16[288,384]{1,0:T(8,128)(2,1)S(1)}, bf16[288,384]{1,0:T(8,128)(2,1)S(1)}, u32[]{:S(2)}, u32[]{:S(2)}) collective-permute-start(bf16[288,384]{1,0:T(8,128)(2,1)S(1)} %collective-permute-done.4._after.refs_4_), channel_id=1, source_target_pairs={{0,14},{16,30},{2,0},{18,16},{4,2},{20,18},{6,4},{22,20},{8,6},{24... | collective-permute-start | bytes 663560 | tf_op jit(solution)/shard_map/ppermute | solution.py:635
  51.9 3.6 %conv.3._buffer = f32[896,768]{1,0:T(8,128)S(1)} custom-call(bf16[14,8,8,768]{3,2,1,0:T(8,128)(2,1)S(1)} %bitcast.40, f32[49,768]{1,0:T(8,128)S(1)} %reshape.132.taps_ref, bf16[288,384]{1,0:T(8,128)(2,1)S(1)} %get-tuple-element.24._after._buffer.refs_1_, bf16[288,384]{1,0:T(8,128)(2,1)S(1)} %get-tuple-element.24._after._buffer.refs_1_), custom_call_target="tpu_custom_call" | custom-call | flops 22478848 | bytes 1376256 | tf_op jit(solution)/shard_map/conv/pallas_call | solution.py:110
  55.5 3.6 %conv.4._buffer = f32[896,768]{1,0:T(8,128)S(1)} custom-call(bf16[14,8,8,768]{3,2,1,0:T(8,128)(2,1)S(1)} %bitcast.41, f32[49,768]{1,0:T(8,128)S(1)} %reshape.132.taps_ref, bf16[288,384]{1,0:T(8,128)(2,1)S(1)} %collective-permute-done.4._after.refs_4_, f32[896,768]{1,0:T(8,128)S(1)} %conv.3._buffer), custom_call_target="tpu_custom_call", output_to_operand_aliasing={{}: (3, {})} | custom-call | flops 22478848 | bytes 1376256 | tf_op jit(solution)/shard_map/conv/pallas_call | solution.py:110
  59.1 3.6 %conv.5.conv_ref = f32[896,768]{1,0:T(8,128)S(1)} custom-call(bf16[14,8,8,768]{3,2,1,0:T(8,128)(2,1)S(1)} %bitcast.42, f32[49,768]{1,0:T(8,128)S(1)} %reshape.132.taps_ref, bf16[288,384]{1,0:T(8,128)(2,1)S(1)} %collective-permute-done.5._after.refs_6_, f32[896,768]{1,0:T(8,128)S(1)} %conv.4._buffer), custom_call_target="tpu_custom_call", output_to_operand_aliasing={{}: (3, {})} | custom-call | flops 22478848 | bytes 1376256 | tf_op jit(solution)/shard_map/conv/pallas_call | solution.py:110
  62.8 5.2 %norm.1 = (bf16[896,768]{1,0:T(8,128)(2,1)S(1)}, f32[896,768]{1,0:T(8,128)S(1)}, f32[896,1]{1,0:T(8,128)S(1)}, bf16[896,768]{1,0:T(8,128)(2,1)}) custom-call(f32[896,768]{1,0:T(8,128)S(1)} %conv.5.conv_ref, bf16[14,8,8,768]{3,2,1,0:T(8,128)(2,1)S(1)} %bitcast.47, s32[1,1]{1,0:T(1,128)S(6)} %copy.65.count_ref, f32[1,768]{1,0:T(1,128)S(1)} %reshape.133.gain_ref, ...), custom_call_target="tpu_custom_call" | custom-call | flops 13762560 | bytes 9633792 | tf_op jit(solution)/shard_map/norm/pallas_call | solution.py:175
  67.9 1.6 copy-done.7
  69.5 2.0 collective-permute-start.10
  73.0 2.1 all-to-all-done.1.second_ref
  75.1 1.5 collective-permute-done.10.gb_theirs_ref
  76.6 33.6 %mlp.1 = (bf16[8,1792,128]{2,1,0:T(8,128)(2,1)}, f32[896,768]{1,0:T(8,128)}, bf16[896,768]{1,0:T(8,128)(2,1)}, f32[1,1152]{1,0:T(1,128)}, f32[1,768]{1,0:T(1,128)}) custom-call(s32[1]{0:T(128)} %bitcast.1.core_ref, s32[16]{0:T(128)} %stack.67.order_ref, bf16[896,768]{1,0:T(8,128)(2,1)} %copy-done.17, bf16[896,768]{1,0:T(8,128)(2,1)} %collective-permute-done.9.theirs_ref, ...), custom_call_target="tpu_custom_call" | custom-call | flops 15854469120 | bytes 10616832 | tf_op jit(solution)/shard_map/mlp/pallas_call | solution.py:378
  110.2 6.9 %all-to-all-start.2 = ((bf16[8,1792,128]{2,1,0:T(8,128)(2,1)}), bf16[8,1792,128]{2,1,0:T(8,128)(2,1)}, u32[]{:S(2)}, u32[]{:S(2)}) async-start(bf16[8,1792,128]{2,1,0:T(8,128)(2,1)} %get-tuple-element.33._after._buffer), calls=%async_computation.2 | async-start | bytes 7340032 | tf_op jit(solution)/shard_map/all_to_all | solution.py:861
  118.0 2.7 %collective-permute-done.11.gn_other_ref = bf16[896,768]{1,0:T(8,128)(2,1)S(1)} collective-permute-done((bf16[896,768]{1,0:T(8,128)(2,1)}, bf16[896,768]{1,0:T(8,128)(2,1)S(1)}, u32[]{:S(2)}, u32[]{:S(2)}) %collective-permute-start.11) | collective-permute-done | bytes 1376288 | tf_op jit(solution)/shard_map/ppermute | solution.py:635
  120.8 1.1 copy-done.11
  121.9 1.8 copy-done.8
  123.6 1.8 copy-done.9
  125.4 1.3 copy-done.12
  126.8 4.5 %unnorm.1 = (f32[896,768]{1,0:T(8,128)S(1)}, f32[2,768]{1,0:T(2,128)S(1)}) custom-call(f32[896,768]{1,0:T(8,128)S(1)} %copy-done.9, bf16[896,768]{1,0:T(8,128)(2,1)S(1)} %copy-done.12, f32[896,768]{1,0:T(8,128)S(1)} %copy-done.8, f32[896,1]{1,0:T(8,128)S(1)} %get-tuple-element.31.inv_ref, f32[1,768]{1,0:T(1,128)S(1)} %reshape.133.gain_ref), custom_call_target="tpu_custom_call" | custom-call | flops 13762560 | bytes 9633792 | tf_op jit(solution)/shard_map/unnorm/pallas_call | solution.py:454
  131.3 4.6 %taps.3._buffer = f32[49,768]{1,0:T(8,128)S(1)} custom-call(bf16[14,8,8,768]{3,2,1,0:T(8,128)(2,1)S(1)} %bitcast.43, f32[896,768]{1,0:T(8,128)S(1)} %get-tuple-element.32.grad_ref, bf16[8,1792,128]{2,1,0:T(8,128)(2,1)S(1)} %copy-done, bf16[8,1792,128]{2,1,0:T(8,128)(2,1)S(1)} %copy-done), custom_call_target="tpu_custom_call" | custom-call | flops 22478848 | bytes 1376256 | tf_op jit(solution)/shard_map/taps/pallas_call | solution.py:528
  135.9 4.6 %taps.4._buffer = f32[49,768]{1,0:T(8,128)S(1)} custom-call(bf16[14,8,8,768]{3,2,1,0:T(8,128)(2,1)S(1)} %bitcast.44, f32[896,768]{1,0:T(8,128)S(1)} %get-tuple-element.32.grad_ref, bf16[8,1792,128]{2,1,0:T(8,128)(2,1)S(1)} %copy-done, f32[49,768]{1,0:T(8,128)S(1)} %taps.3._buffer), custom_call_target="tpu_custom_call", output_to_operand_aliasing={{}: (3, {})} | custom-call | flops 22478848 | bytes 1376256 | tf_op jit(solution)/shard_map/taps/pallas_call | solution.py:528
  140.5 4.6 %taps.5 = f32[49,768]{1,0:T(8,128)S(1)} custom-call(bf16[14,8,8,768]{3,2,1,0:T(8,128)(2,1)S(1)} %bitcast.45, f32[896,768]{1,0:T(8,128)S(1)} %get-tuple-element.32.grad_ref, bf16[8,1792,128]{2,1,0:T(8,128)(2,1)S(1)} %copy-done, f32[49,768]{1,0:T(8,128)S(1)} %taps.4._buffer), custom_call_target="tpu_custom_call", output_to_operand_aliasing={{}: (3, {})} | custom-call | flops 22478848 | bytes 1376256 | tf_op jit(solution)/shard_map/taps/pallas_call | solution.py:528
  145.4 2.0 copy-done.1
  147.4 1.3 copy-done.6
  148.8 4.4 %back.3._buffer = f32[14,8,8,768]{3,2,1,0:T(8,128)} custom-call(bf16[14,8,8,768]{3,2,1,0:T(8,128)(2,1)S(1)} %bitcast.48, f32[896,768]{1,0:T(8,128)S(1)} %get-tuple-element.32.grad_ref, s32[1,1]{1,0:T(1,128)S(6)} %copy.65.count_ref, f32[49,768]{1,0:T(8,128)S(1)} %reshape.132.taps_ref, bf16[8,1792,128]{2,1,0:T(8,128)(2,1)S(1)} %copy-done.1, ...), custom_call_target="tpu_custom_call" | custom-call | flops 22478848 | bytes 2293760 | tf_op jit(solution)/shard_map/back/pallas_call | solution.py:592
  153.1 4.4 %back.4._buffer = f32[14,8,8,768]{3,2,1,0:T(8,128)} custom-call(bf16[14,8,8,768]{3,2,1,0:T(8,128)(2,1)S(1)} %bitcast.49, f32[896,768]{1,0:T(8,128)S(1)} %get-tuple-element.32.grad_ref, s32[1,1]{1,0:T(1,128)S(6)} %copy.65.count_ref, f32[49,768]{1,0:T(8,128)S(1)} %reshape.132.taps_ref, ...), custom_call_target="tpu_custom_call", output_to_operand_aliasing={{}: (5, {})} | custom-call | flops 22478848 | bytes 2293760 | tf_op jit(solution)/shard_map/back/pallas_call | solution.py:592
  157.5 4.4 %back.5._after = f32[14,8,8,768]{3,2,1,0:T(8,128)} custom-call(bf16[14,8,8,768]{3,2,1,0:T(8,128)(2,1)S(1)} %bitcast.50, f32[896,768]{1,0:T(8,128)S(1)} %get-tuple-element.32.grad_ref, s32[1,1]{1,0:T(1,128)S(6)} %copy.65.count_ref, f32[49,768]{1,0:T(8,128)S(1)} %reshape.132.taps_ref, ...), custom_call_target="tpu_custom_call", output_to_operand_aliasing={{}: (5, {})} | custom-call | flops 22478848 | bytes 2293760 | tf_op jit(solution)/shard_map/back/pallas_call | solution.py:592
  161.9 7.4 %all-to-all-done.2.terms_ref = bf16[8,1792,128]{2,1,0:T(8,128)(2,1)} async-done(((bf16[8,1792,128]{2,1,0:T(8,128)(2,1)}), bf16[8,1792,128]{2,1,0:T(8,128)(2,1)}, u32[]{:S(2)}, u32[]{:S(2)}) %all-to-all-start.2) | async-done | bytes 3670048 | tf_op jit(solution)/shard_map/all_to_all | solution.py:861
  169.3 1.8 copy-done.4
  171.0 2.6 %add_up.1 = bf16[1792,128]{1,0:T(8,128)(2,1)S(1)} custom-call(bf16[8,1792,128]{2,1,0:T(8,128)(2,1)} %all-to-all-done.2.terms_ref, f32[14,8,8,768]{3,2,1,0:T(8,128)S(1)} %copy-done.4), custom_call_target="tpu_custom_call" | custom-call | tf_op jit(solution)/shard_map/add_up/pallas_call | solution.py:702
  173.7 1.5 collective-permute-start.12
  175.4 0.8 collective-permute-done.12
  176.3 23.0 %all_to_all.25 = bf16[16,144,128]{2,1,0:T(8,128)(2,1)S(1)} all-to-all(bf16[16,144,128]{2,1,0:T(8,128)(2,1)S(1)} %fusion.1), channel_id=1, replica_groups=mesh['dp'=16,'fsdp'=16] {'fsdp'}, dimensions={0} | all-to-all | bytes 1179648 | tf_op jit(solution)/shard_map/all_to_all | solution.py:877
  199.5 19.3 %all_to_all.26.terms_ref = bf16[16,144,128]{2,1,0:T(8,128)(2,1)S(1)} all-to-all(bf16[16,144,128]{2,1,0:T(8,128)(2,1)S(1)} %broadcast_in_dim.41), channel_id=1, replica_groups=mesh['dp'=16,'fsdp'=16] {'dp'}, dimensions={0} | all-to-all | bytes 1179648 | tf_op jit(solution)/shard_map/all_to_all | solution.py:879
  218.8 1.0 finish.1
  (99 shorter events, 8.3 us)
Async XLA Ops:
  0.7 14.7 %copy-start.19 = (bf16[48,2304]{1,0:T(8,128)(2,1)S(1)}, bf16[48,2304]{1,0:T(8,128)(2,1)}, u32[]{:S(2)}) copy-start(bf16[48,2304]{1,0:T(8,128)(2,1)} %param.16) | copy-start | bytes 663556
  5.2 22.7 %all-to-all-start = ((bf16[16,88,128]{2,1,0:T(8,128)(2,1)}), bf16[16,88,128]{2,1,0:T(8,128)(2,1)S(1)}, u32[]{:S(2)}, u32[]{:S(2)}) async-start(bf16[16,88,128]{2,1,0:T(8,128)(2,1)} %broadcast_in_dim.37), calls=%async_computation | async-start | bytes 720896 | tf_op jit(solution)/shard_map/all_to_all | solution.py:819
  15.4 3.9 %collective-permute-start.1 = (bf16[144,384]{1,0:T(8,128)(2,1)S(1)}, bf16[144,384]{1,0:T(8,128)(2,1)S(1)}, u32[]{:S(2)}, u32[]{:S(2)}) collective-permute-start(bf16[144,384]{1,0:T(8,128)(2,1)S(1)} %pad_maximum_fusion.3), channel_id=1, source_target_pairs={{0,1},{1,0},{2,3},{3,2},{4,5},{5,4},{6,7},{7,6},{8,9},{9,8},{10,11... | collective-permute-start | bytes 331784 | tf_op jit(solution)/shard_map/ppermute | solution.py:639
  19.3 22.6 %copy-start.18 = (bf16[288,384]{1,0:T(8,128)(2,1)}, bf16[288,384]{1,0:T(8,128)(2,1)S(1)}, u32[]{:S(2)}) copy-start(bf16[288,384]{1,0:T(8,128)(2,1)S(1)} %pad_maximum_fusion.1.refs_0_) | copy-start | bytes 663556
  19.3 12.2 %collective-permute-start.2 = (bf16[288,384]{1,0:T(8,128)(2,1)S(1)}, bf16[288,384]{1,0:T(8,128)(2,1)S(1)}, u32[]{:S(2)}, u32[]{:S(2)}) collective-permute-start(bf16[288,384]{1,0:T(8,128)(2,1)S(1)} %pad_maximum_fusion.1.refs_0_), channel_id=1, source_target_pairs={{0,2},{16,18},{2,4},{18,20},{4,6},{20,22},{6,8},{22,24},{8,10},{24... | collective-permute-start | bytes 663560 | tf_op jit(solution)/shard_map/ppermute | solution.py:635
  21.3 10.2 %collective-permute-start.3 = (bf16[288,384]{1,0:T(8,128)(2,1)S(1)}, bf16[288,384]{1,0:T(8,128)(2,1)S(1)}, u32[]{:S(2)}, u32[]{:S(2)}) collective-permute-start(bf16[288,384]{1,0:T(8,128)(2,1)S(1)} %pad_maximum_fusion.1.refs_0_), channel_id=1, source_target_pairs={{0,14},{16,30},{2,0},{18,16},{4,2},{20,18},{6,4},{22,20},{8,6},{24... | collective-permute-start | bytes 663560 | tf_op jit(solution)/shard_map/ppermute | solution.py:635
  27.9 4.5 %collective-permute-start = (bf16[8,56,128]{2,1,0:T(8,128)(2,1)S(1)}, bf16[8,56,128]{2,1,0:T(8,128)(2,1)S(1)}, u32[]{:S(2)}, u32[]{:S(2)}) collective-permute-start(bf16[8,56,128]{2,1,0:T(8,128)(2,1)S(1)} %get-tuple-element.67), channel_id=1, source_target_pairs={{0,16},{16,0},{2,18},{18,2},{4,20},{20,4},{6,22},{22,6},{8,24},{24... | collective-permute-start | bytes 344072 | tf_op jit(solution)/shard_map/ppermute | solution.py:635
  33.9 8.0 %copy-start.15 = (bf16[288,384]{1,0:T(8,128)(2,1)}, bf16[288,384]{1,0:T(8,128)(2,1)S(1)}, u32[]{:S(2)}) copy-start(bf16[288,384]{1,0:T(8,128)(2,1)S(1)} %get-tuple-element.23.refs_2_) | copy-start | bytes 663556
  33.9 17.9 %copy-start.10 = (bf16[288,384]{1,0:T(8,128)(2,1)}, bf16[288,384]{1,0:T(8,128)(2,1)S(1)}, u32[]{:S(2)}) copy-start(bf16[288,384]{1,0:T(8,128)(2,1)S(1)} %get-tuple-element.24._after._buffer.refs_1_) | copy-start | bytes 663556
  33.9 7.9 %collective-permute-start.6 = (bf16[288,384]{1,0:T(8,128)(2,1)S(1)}, bf16[288,384]{1,0:T(8,128)(2,1)S(1)}, u32[]{:S(2)}, u32[]{:S(2)}) collective-permute-start(bf16[288,384]{1,0:T(8,128)(2,1)S(1)} %get-tuple-element.24._after._buffer.refs_1_), channel_id=1, source_target_pairs={{0,2},{16,18},{2,4},{18,20},{4,6},{20,22},{6,8},{22,24},{8,10},{24... | collective-permute-start | bytes 663560 | tf_op jit(solution)/shard_map/ppermute | solution.py:635
  34.6 14.2 %collective-permute-start.4 = (bf16[288,384]{1,0:T(8,128)(2,1)S(1)}, bf16[288,384]{1,0:T(8,128)(2,1)S(1)}, u32[]{:S(2)}, u32[]{:S(2)}) collective-permute-start(bf16[288,384]{1,0:T(8,128)(2,1)S(1)} %get-tuple-element.23.refs_2_), channel_id=1, source_target_pairs={{0,14},{16,30},{2,0},{18,16},{4,2},{20,18},{6,4},{22,20},{8,6},{24... | collective-permute-start | bytes 663560 | tf_op jit(solution)/shard_map/ppermute | solution.py:635
  41.8 0.7 copy-start.22
  41.8 9.3 %collective-permute-start.7 = (bf16[288,384]{1,0:T(8,128)(2,1)S(1)}, bf16[288,384]{1,0:T(8,128)(2,1)}, u32[]{:S(2)}, u32[]{:S(2)}) collective-permute-start(bf16[288,384]{1,0:T(8,128)(2,1)S(1)} %collective-permute-done.6.refs_3_), channel_id=1, source_target_pairs={{0,2},{16,18},{2,4},{18,20},{4,6},{20,22},{6,8},{22,24},{8,10},{24... | collective-permute-start | bytes 663560 | tf_op jit(solution)/shard_map/ppermute | solution.py:635
  42.5 32.6 %all-to-all-start.1 = ((bf16[8,896,128]{2,1,0:T(8,128)(2,1)}), bf16[8,896,128]{2,1,0:T(8,128)(2,1)}, u32[]{:S(2)}, u32[]{:S(2)}) async-start(bf16[8,896,128]{2,1,0:T(8,128)(2,1)} %get-tuple-element.27), calls=%async_computation.1 | async-start | bytes 3670016 | tf_op jit(solution)/shard_map/all_to_all | solution.py:828
  48.8 3.0 %copy-start.2 = (bf16[1,14,8,8,768]{4,3,2,1,0:T(8,128)(2,1)S(1)}, bf16[1,14,8,8,768]{4,3,2,1,0:T(8,128)(2,1)}, u32[]{:S(2)}) copy-start(bf16[1,14,8,8,768]{4,3,2,1,0:T(8,128)(2,1)} %param.10) | copy-start | bytes 4128772
  48.8 6.6 %copy-start.13 = (bf16[288,384]{1,0:T(8,128)(2,1)}, bf16[288,384]{1,0:T(8,128)(2,1)S(1)}, u32[]{:S(2)}) copy-start(bf16[288,384]{1,0:T(8,128)(2,1)S(1)} %collective-permute-done.4._after.refs_4_) | copy-start | bytes 663556
  48.9 10.2 %collective-permute-start.5 = (bf16[288,384]{1,0:T(8,128)(2,1)S(1)}, bf16[288,384]{1,0:T(8,128)(2,1)S(1)}, u32[]{:S(2)}, u32[]{:S(2)}) collective-permute-start(bf16[288,384]{1,0:T(8,128)(2,1)S(1)} %collective-permute-done.4._after.refs_4_), channel_id=1, source_target_pairs={{0,14},{16,30},{2,0},{18,16},{4,2},{20,18},{6,4},{22,20},{8,6},{24... | collective-permute-start | bytes 663560 | tf_op jit(solution)/shard_map/ppermute | solution.py:635
  51.1 11.7 %collective-permute-start.8 = (bf16[288,384]{1,0:T(8,128)(2,1)}, bf16[288,384]{1,0:T(8,128)(2,1)S(1)}, u32[]{:S(2)}, u32[]{:S(2)}) collective-permute-start(bf16[288,384]{1,0:T(8,128)(2,1)} %collective-permute-done.7.refs_5_), channel_id=1, source_target_pairs={{0,2},{16,18},{2,4},{18,20},{4,6},{20,22},{6,8},{22,24},{8,10},{24... | collective-permute-start | bytes 663560 | tf_op jit(solution)/shard_map/ppermute | solution.py:635
  59.1 3.7 %copy-start.5 = (bf16[1,14,8,8,768]{4,3,2,1,0:T(8,128)(2,1)S(1)}, bf16[1,14,8,8,768]{4,3,2,1,0:T(8,128)(2,1)}, u32[]{:S(2)}) copy-start(bf16[1,14,8,8,768]{4,3,2,1,0:T(8,128)(2,1)} %param.11) | copy-start | bytes 4128772
  59.1 3.6 %copy-start.14 = (bf16[288,384]{1,0:T(8,128)(2,1)}, bf16[288,384]{1,0:T(8,128)(2,1)S(1)}, u32[]{:S(2)}) copy-start(bf16[288,384]{1,0:T(8,128)(2,1)S(1)} %collective-permute-done.5._after.refs_6_) | copy-start | bytes 663556
  62.7 5.2 %copy-start.16 = (bf16[288,384]{1,0:T(8,128)(2,1)}, bf16[288,384]{1,0:T(8,128)(2,1)S(1)}, u32[]{:S(2)}) copy-start(bf16[288,384]{1,0:T(8,128)(2,1)S(1)} %collective-permute-done.8._after.refs_7_) | copy-start | bytes 663556
  67.9 1.6 copy-start.7
  69.5 7.1 %copy-start.17 = (bf16[896,768]{1,0:T(8,128)(2,1)}, bf16[896,768]{1,0:T(8,128)(2,1)S(1)}, u32[]{:S(2)}) copy-start(bf16[896,768]{1,0:T(8,128)(2,1)S(1)} %get-tuple-element.25.mine_ref) | copy-start | bytes 4128772
  69.5 7.1 %collective-permute-start.10 = (bf16[896,768]{1,0:T(8,128)(2,1)}, bf16[896,768]{1,0:T(8,128)(2,1)}, u32[]{:S(2)}, u32[]{:S(2)}) collective-permute-start(bf16[896,768]{1,0:T(8,128)(2,1)} %get-tuple-element.26.gb_mine_ref), channel_id=1, source_target_pairs={{0,16},{16,0},{2,18},{18,2},{4,20},{20,4},{6,22},{22,6},{8,24},{24... | collective-permute-start | bytes 4128776 | tf_op jit(solution)/shard_map/ppermute | solution.py:635
  71.6 5.0 %collective-permute-start.9 = (bf16[896,768]{1,0:T(8,128)(2,1)S(1)}, bf16[896,768]{1,0:T(8,128)(2,1)}, u32[]{:S(2)}, u32[]{:S(2)}) collective-permute-start(bf16[896,768]{1,0:T(8,128)(2,1)S(1)} %get-tuple-element.25.mine_ref), channel_id=1, source_target_pairs={{0,16},{16,0},{2,18},{18,2},{4,20},{20,4},{6,22},{22,6},{8,24},{24... | collective-permute-start | bytes 4128776 | tf_op jit(solution)/shard_map/ppermute | solution.py:635
  110.2 7.6 %copy-start.20 = (f32[1,1152]{1,0:T(1,128)S(1)}, f32[1,1152]{1,0:T(1,128)}, u32[]{:S(2)}) copy-start(f32[1,1152]{1,0:T(1,128)} %get-tuple-element.36) | copy-start | bytes 13828
  110.2 7.7 %copy-start.21 = (f32[1,768]{1,0:T(1,128)S(1)}, f32[1,768]{1,0:T(1,128)}, u32[]{:S(2)}) copy-start(f32[1,768]{1,0:T(1,128)} %get-tuple-element.35) | copy-start | bytes 9220
  110.2 59.0 %all-to-all-start.2 = ((bf16[8,1792,128]{2,1,0:T(8,128)(2,1)}), bf16[8,1792,128]{2,1,0:T(8,128)(2,1)}, u32[]{:S(2)}, u32[]{:S(2)}) async-start(bf16[8,1792,128]{2,1,0:T(8,128)(2,1)} %get-tuple-element.33._after._buffer), calls=%async_computation.2 | async-start | bytes 7340032 | tf_op jit(solution)/shard_map/all_to_all | solution.py:861
  117.2 3.6 %collective-permute-start.11 = (bf16[896,768]{1,0:T(8,128)(2,1)}, bf16[896,768]{1,0:T(8,128)(2,1)S(1)}, u32[]{:S(2)}, u32[]{:S(2)}) collective-permute-start(bf16[896,768]{1,0:T(8,128)(2,1)} %get-tuple-element.29), channel_id=1, source_target_pairs={{0,16},{16,0},{2,18},{18,2},{4,20},{20,4},{6,22},{22,6},{8,24},{24... | collective-permute-start | bytes 4128776 | tf_op jit(solution)/shard_map/ppermute | solution.py:635
  120.8 1.1 copy-start.11
  121.9 1.8 copy-start.8
  123.6 1.8 copy-start.9
  125.4 1.3 copy-start.12
  126.8 4.5 %copy-start = (bf16[8,1792,128]{2,1,0:T(8,128)(2,1)S(1)}, bf16[8,1792,128]{2,1,0:T(8,128)(2,1)}, u32[]{:S(2)}) copy-start(bf16[8,1792,128]{2,1,0:T(8,128)(2,1)} %get-tuple-element.33._after._buffer) | copy-start | bytes 11010052
  126.8 4.6 %copy-start.3 = (bf16[1,14,8,8,768]{4,3,2,1,0:T(8,128)(2,1)S(1)}, bf16[1,14,8,8,768]{4,3,2,1,0:T(8,128)(2,1)}, u32[]{:S(2)}) copy-start(bf16[1,14,8,8,768]{4,3,2,1,0:T(8,128)(2,1)} %param.10) | copy-start | bytes 4128772
  145.4 2.0 copy-start.1
  147.4 1.3 copy-start.6
  169.3 1.8 copy-start.4
  173.7 2.5 %collective-permute-start.12 = (bf16[8,56,128]{2,1,0:T(8,128)(2,1)S(1)}, bf16[8,56,128]{2,1,0:T(8,128)(2,1)S(1)}, u32[]{:S(2)}, u32[]{:S(2)}) collective-permute-start(bf16[8,56,128]{2,1,0:T(8,128)(2,1)S(1)} %get-tuple-element.66), channel_id=1, source_target_pairs={{0,16},{16,0},{2,18},{18,2},{4,20},{20,4},{6,22},{22,6},{8,24},{24... | collective-permute-start | bytes 344072 | tf_op jit(solution)/shard_map/ppermute | solution.py:635

commit v2 on v1

--- a/solution.py
+++ b/solution.py
@@ -221,9 +221,9 @@
 ):
     pieces = refs[:count]
     (
-        sums_ref, gn_mine_ref, gn_theirs_ref, grad_bias_ref, scale_ref,
+        sums_out, gn_mine_out, gn_theirs_out, grad_bias_ref, scale_ref,
         first, second, sum_first, sum_second, tokens, cots, flipped, grad_normed,
-        actives, grads, sems, more_sems,
+        actives, grads, sums_ref, gn_theirs_ref, sems, more_sems, out_sems,
     ) = refs[count:]
     channels, hidden = first.shape
     half = mine_ref.shape[0]
@@ -287,8 +287,9 @@
 
     lax.fori_loop(0, 2 * half // BLOCK, flip, 0)
 
-    def chunk(start, wide):
+    def chunk(start, wide, slot):
         units_at = pl.ds(start, wide)
+        lanes = pl.ds(slot * BLOCK, wide)
 
         def block(j, bias_sum):
             at = pl.ds(aligned(j, half), half)
@@ -296,34 +297,46 @@
             preact = preact + bias_ref[:, units_at]
             grad_hidden = dot(cots[at, :], second[units_at, :], (((1,), (1,)), ((), ())))
             prob = 0.5 * (1.0 + lax.erf(preact * 0.7071067811865476))
-            actives[at, :wide] = (preact * prob).astype(BF16)
+            actives[at, lanes] = (preact * prob).astype(BF16)
             slope = prob + preact * jnp.exp(-0.5 * preact * preact) * 0.3989422804014327
             grad_preact = (grad_hidden * slope).astype(BF16)
-            grads[at, :wide] = grad_preact
+            grads[at, lanes] = grad_preact
             grad_normed[at, :] += dot(grad_preact, first[:, units_at], (((1,), (1,)), ((), ())))
             return bias_sum + jnp.sum(grad_preact.astype(F32), axis=0, keepdims=True)
 
         grad_bias_ref[:, units_at] = lax.fori_loop(
-            0, 2, block, jnp.zeros((1, wide), F32)
+            0, 2, block, jnp.zeros((1, wide), F32), unroll=True
         )
-        sum_second[units_at, :] = dot(actives[:, :wide], cots[...], (((0,), (0,)), ((), ())))
-        sum_first[:, units_at] = dot(flipped[...], grads[:, :wide], (((1,), (0,)), ((), ())))
-
-    def whole_chunk(h, _):
-        chunk(aligned(h, BLOCK), BLOCK)
-        return 0
-
-    lax.fori_loop(0, hidden // BLOCK, whole_chunk, 0)
-    if hidden % BLOCK:
-        chunk(hidden // BLOCK * BLOCK, hidden % BLOCK)
-
-    def unload(i, _):
+
+    def sums(start, wide, slot):
+        units_at = pl.ds(start, wide)
+        lanes = pl.ds(slot * BLOCK, wide)
+        sum_second[units_at, :] = dot(actives[:, lanes], cots[...], (((0,), (0,)), ((), ())))
+        sum_first[:, units_at] = dot(flipped[...], grads[:, lanes], (((1,), (0,)), ((), ())))
+
+    chunks = [(start, min(BLOCK, hidden - start)) for start in range(0, hidden, BLOCK)]
+    for i, (start, wide) in enumerate(chunks):
+        chunk(start, wide, i % 2)
+        if i:
+            sums(*chunks[i - 1], (i - 1) % 2)
+    sums(*chunks[-1], (len(chunks) - 1) % 2)
+
+    leaving = []
+
+    def leave(src, dst):
+        copy = pltpu.make_async_copy(src, dst, out_sems.at[len(leaving)])
+        copy.start()
+        leaving.append(copy)
+
+    leave(grad_normed.at[pl.ds(0, half), :], gn_mine_out)
+
+    def narrow(i, _):
         at = pl.ds(aligned(i, tall), tall)
-        gn_mine_ref[at, :] = grad_normed[at, :]
         gn_theirs_ref[at, :] = grad_normed[pl.ds(half + aligned(i, tall), tall), :].astype(BF16)
         return 0
 
-    lax.fori_loop(0, half // tall, unload, 0)
+    lax.fori_loop(0, half // tall, narrow, 0)
+    leave(gn_theirs_ref, gn_theirs_out)
 
     def scale_rows(i, total):
         at = pl.ds(aligned(i, tall), tall)
@@ -351,6 +364,10 @@
         return 0
 
     lax.fori_loop(0, shards // 2, pack_pair, 0)
+    for e in range(chips):
+        leave(
+            sums_ref.at[e, pl.ds(0, first_rows), :], sums_out.at[e, pl.ds(0, first_rows), :]
+        )
 
     def pack_shard(f, _):
         for e in range(chips):
@@ -366,6 +383,14 @@
         return 0
 
     lax.fori_loop(0, shards // 2, pack_shard, 0)
+    rest = sums_ref.shape[1] - first_rows
+    for e in range(chips):
+        leave(
+            sums_ref.at[e, pl.ds(first_rows, rest), :],
+            sums_out.at[e, pl.ds(first_rows, rest), :],
+        )
+    for copy in leaving:
+        copy.wait()
 
 
 def mlp(core, order, mine, theirs, gb_mine, gb_theirs, bias, second, pieces):
@@ -378,7 +403,7 @@
     return pl.pallas_call(
         functools.partial(mlp_kernel, count),
         in_specs=[smem, smem] + [anywhere] * 4 + [vmem, vmem] + [anywhere] * count,
-        out_specs=[vmem] * 5,
+        out_specs=[anywhere] * 3 + [vmem] * 2,
         out_shape=[
             jax.ShapeDtypeStruct(sums, BF16),
             jax.ShapeDtypeStruct((tokens, channels), F32),
@@ -395,10 +420,13 @@
             pltpu.VMEM((2 * tokens, channels), BF16),
             pltpu.VMEM((channels, 2 * tokens), BF16),
             pltpu.VMEM((2 * tokens, channels), F32),
-            pltpu.VMEM((2 * tokens, BLOCK), BF16),
-            pltpu.VMEM((2 * tokens, BLOCK), BF16),
+            pltpu.VMEM((2 * tokens, 2 * BLOCK), BF16),
+            pltpu.VMEM((2 * tokens, 2 * BLOCK), BF16),
+            pltpu.VMEM(sums, BF16),
+            pltpu.VMEM((tokens, channels), BF16),
             pltpu.SemaphoreType.DMA((count,)),
             pltpu.SemaphoreType.DMA((4,)),
+            pltpu.SemaphoreType.DMA((2 + 2 * sums[0],)),
         ],
         compiler_params=pltpu.CompilerParams(vmem_limit_bytes=VMEM_LIMIT),
         cost_estimate=pl.CostEstimate(
@@ -711,30 +739,30 @@
     )(terms, after)
 
 
-def finish_kernel(factor, side_ref, terms_ref, first_ref, second_ref, small_ref):
-    side = side_ref[0]
-    chips = terms_ref.shape[0] // 2
+def finish_kernel(
+    factor, place_ref, mine_ref, theirs_ref, first_ref, second_ref, small_ref
+):
+    core, side = place_ref[0], place_ref[1]
     small_rows = PART_TILES * 2 * SUBLANES
     half = small_rows // 2
     wide = first_ref.shape[1] // 2 // LANES
     small = None
-    for e in range(chips):
-        for core in range(2):
-            part = terms_ref[2 * e + core, :small_rows, :].astype(F32) * factor
+    for e in range(mine_ref.shape[0]):
+        mine, theirs = mine_ref[e].astype(F32), theirs_ref[e].astype(F32)
+        for k in range(2):
+            part = jnp.where(core == k, mine[:half], theirs[:half]) * factor
             for i in range(PART_TILES):
                 r, c = tile_of(e, i, wide)
                 if r * SUBLANES < first_ref.shape[0]:
-                    lane = (core * wide + c) * LANES
+                    lane = (k * wide + c) * LANES
                     first_ref[r * SUBLANES : (r + 1) * SUBLANES, lane : lane + LANES] = part[
                         i * SUBLANES : (i + 1) * SUBLANES
                     ]
-            more = terms_ref[2 * e + core, small_rows:, :].astype(F32)
-            small = more if small is None else small + more
+        more = mine[small_rows:] + theirs[small_rows:]
+        small = more if small is None else small + more
+        mine, theirs = mine[half:small_rows], theirs[half:small_rows]
         part = jnp.concatenate(
-            [
-                terms_ref[2 * e + core, :small_rows, :].astype(F32)[half:]
-                for core in (side, 1 - side)
-            ]
+            [jnp.where(core == side, mine, theirs), jnp.where(core == side, theirs, mine)]
         )
         part = part * factor
         for i in range(PART_TILES):
@@ -746,14 +774,12 @@
     small_ref[...] = small * factor
 
 
-def finish(side, terms, first_shape, second_shape, factor):
-    small = (terms.shape[1] - PART_TILES * 2 * SUBLANES, LANES)
+def finish(place, mine, theirs, first_shape, second_shape, factor):
+    small = (mine.shape[1] - PART_TILES * 2 * SUBLANES, LANES)
+    vmem = pl.BlockSpec(memory_space=pltpu.VMEM)
     return pl.pallas_call(
         functools.partial(finish_kernel, factor),
-        in_specs=[
-            pl.BlockSpec(memory_space=pltpu.SMEM),
-            pl.BlockSpec(memory_space=pltpu.VMEM),
-        ],
+        in_specs=[pl.BlockSpec(memory_space=pltpu.SMEM), vmem, vmem],
         out_shape=[
             jax.ShapeDtypeStruct(first_shape, F32),
             jax.ShapeDtypeStruct(second_shape, F32),
@@ -761,7 +787,7 @@
         ],
         compiler_params=pltpu.CompilerParams(vmem_limit_bytes=SMALL_VMEM),
         name="finish",
-    )(side, terms)
+    )(place, mine, theirs)
 
 
 def pack(rows):
@@ -877,11 +903,17 @@
     terms = lax.all_to_all(terms, "fsdp", 0, 0, tiled=True)
     terms = jnp.sum(terms.astype(F32), axis=0).astype(BF16)
     terms = lax.all_to_all(
-        jnp.broadcast_to(terms[None], (dp,) + terms.shape), "dp", 0, 0, tiled=True
+        jnp.broadcast_to(terms[None], (chips,) + terms.shape),
+        "dp", 0, 0, tiled=True, axis_index_groups=same_core,
     )
     factor = 1.0 / math.sqrt(fsdp * dp * ROWS * SPOTS)
     first, second, sums = finish(
-        side.reshape(1), terms, (own, hidden), (units, channels), factor
+        jnp.stack([core, side]).astype(jnp.int32),
+        terms,
+        move(terms, flip=1),
+        (own, hidden),
+        (units, channels),
+        factor,
     )
     sums = unpack(sums, lines, own)
     return (

time: 223 us -> 231 us (1.036); the launches traced: 222 us -> 227 us
  Pallas kernels: 86 us -> 93.4 us
  blocking collectives: 42.3 us -> 35.6 us
  starting transfers between devices: 40.9 us -> 44.3 us
    pallas_call x1, Pallas kernels: 33.6 us -> 40.5 us  [mlp(): pl.pallas_call(functools.partial(mlp_kernel, count), in_specs=[smem, smem...]
    all_to_all x1, blocking collectives: 19.3 us -> 12.6 us  [local(): lax.all_to_all(jnp.broadcast_to(terms[None], (chips,) + terms.shape), 'dp...]
    ppermute x12 -> x13, starting transfers between devices: 16.1 us -> 19.4 us  [move(): return lax.ppermute(value, AXES, pairs)]
    ppermute x12 -> x13, waiting for transfers between devices: 10.5 us -> 11.5 us  [move(): return lax.ppermute(value, AXES, pairs)]
  transfers between devices with their start and end apart: 16 -> 17, of which waited for: 9 -> 10; matrix products, arithmetic and copies ran while one was open for 1% -> 1% of each run, Pallas kernels for 21% -> 21%
where the time goes in v2:
time: 231 us; the launch traced here: 227 us
  Pallas kernels  93.4 us (40%)
  starting transfers between devices  44.3 us (19%)
  blocking collectives  35.6 us (15%)
  waiting for transfers between devices  28.1 us (12%)
  local copies, waits for them, and re-layouts  22.3 us (10%)
    pallas_call x1, Pallas kernels, mlp(): pl.pallas_call(functools.partial(mlp_kernel, count), in_specs=[smem, smem...  40.5 us
    all_to_all x1, blocking collectives, local(): terms = lax.all_to_all(terms, 'fsdp', 0, 0, tiled=True)  23 us
    ppermute x13, starting transfers between devices, move(): return lax.ppermute(value, AXES, pairs)  19.4 us
    unnamed x49, local copies, waits for them, and re-layouts  14.9 us
    pallas_call x3, Pallas kernels, taps_part(): pl.pallas_call(functools.partial(taps_kernel, slots), grid=(GROUP_STEPS,)...  13.7 us
    pallas_call x3, Pallas kernels, back_part(): pl.pallas_call(functools.partial(back_kernel, slots), grid=(GROUP_STEPS,)...  13.1 us
    all_to_all x1, blocking collectives, local(): lax.all_to_all(jnp.broadcast_to(terms[None], (chips,) + terms.shape), 'dp...  12.6 us
    ppermute x13, waiting for transfers between devices, move(): return lax.ppermute(value, AXES, pairs)  11.5 us
  transfers between devices with their start and end apart: 17, of which 10 were waited for; matrix products, arithmetic and copies ran while one was open for 1% of the time, Pallas kernels for 21%

profile of v2, /device:TPU:1, one launch (start us, length us, event | category | flops | bytes accessed | tf_op | source)
XLA Modules:
  0.0 226.8 jit_solution(7946516394892816331)
XLA Ops:
  0.7 1.2 reshape.119
  5.2 10.1 %all-to-all-start = ((bf16[16,88,128]{2,1,0:T(8,128)(2,1)}), bf16[16,88,128]{2,1,0:T(8,128)(2,1)S(1)}, u32[]{:S(2)}, u32[]{:S(2)}) async-start(bf16[16,88,128]{2,1,0:T(8,128)(2,1)} %broadcast_in_dim.37), calls=%async_computation | async-start | bytes 720896 | tf_op jit(solution)/shard_map/all_to_all | solution.py:845
  15.4 1.4 collective-permute-start.1
  16.8 2.4 %collective-permute-done.1 = bf16[144,384]{1,0:T(8,128)(2,1)S(1)} collective-permute-done((bf16[144,384]{1,0:T(8,128)(2,1)S(1)}, bf16[144,384]{1,0:T(8,128)(2,1)S(1)}, u32[]{:S(2)}, u32[]{:S(2)}) %collective-permute-start.1) | collective-permute-done | bytes 110624 | tf_op jit(solution)/shard_map/ppermute | solution.py:667
  19.3 2.0 collective-permute-start.2
  21.3 1.4 collective-permute-start.3
  22.7 5.2 %all-to-all-done = bf16[16,88,128]{2,1,0:T(8,128)(2,1)S(1)} async-done(((bf16[16,88,128]{2,1,0:T(8,128)(2,1)}), bf16[16,88,128]{2,1,0:T(8,128)(2,1)S(1)}, u32[]{:S(2)}, u32[]{:S(2)}) %all-to-all-start) | async-done | bytes 360480 | tf_op jit(solution)/shard_map/all_to_all | solution.py:845
  27.9 3.5 %collective-permute-start = (bf16[8,56,128]{2,1,0:T(8,128)(2,1)S(1)}, bf16[8,56,128]{2,1,0:T(8,128)(2,1)S(1)}, u32[]{:S(2)}, u32[]{:S(2)}) collective-permute-start(bf16[8,56,128]{2,1,0:T(8,128)(2,1)S(1)} %get-tuple-element.67), channel_id=1, source_target_pairs={{0,16},{16,0},{2,18},{18,2},{4,20},{20,4},{6,22},{22,6},{8,24},{24... | collective-permute-start | bytes 344072 | tf_op jit(solution)/shard_map/ppermute | solution.py:663
  31.5 1.0 collective-permute-done.swapped_ref
  32.4 1.5 copies.1
  34.6 2.7 %collective-permute-start.4 = (bf16[288,384]{1,0:T(8,128)(2,1)S(1)}, bf16[288,384]{1,0:T(8,128)(2,1)S(1)}, u32[]{:S(2)}, u32[]{:S(2)}) collective-permute-start(bf16[288,384]{1,0:T(8,128)(2,1)S(1)} %get-tuple-element.23.refs_2_), channel_id=1, source_target_pairs={{0,14},{16,30},{2,0},{18,16},{4,2},{20,18},{6,4},{22,20},{8,6},{24... | collective-permute-start | bytes 663560 | tf_op jit(solution)/shard_map/ppermute | solution.py:663
  37.3 4.5 %collective-permute-done.6.refs_3_ = bf16[288,384]{1,0:T(8,128)(2,1)S(1)} collective-permute-done((bf16[288,384]{1,0:T(8,128)(2,1)S(1)}, bf16[288,384]{1,0:T(8,128)(2,1)S(1)}, u32[]{:S(2)}, u32[]{:S(2)}) %collective-permute-start.6) | collective-permute-done | bytes 221216 | tf_op jit(solution)/shard_map/ppermute | solution.py:663
  42.5 6.4 %all-to-all-start.1 = ((bf16[8,896,128]{2,1,0:T(8,128)(2,1)}), bf16[8,896,128]{2,1,0:T(8,128)(2,1)}, u32[]{:S(2)}, u32[]{:S(2)}) async-start(bf16[8,896,128]{2,1,0:T(8,128)(2,1)} %get-tuple-element.27), calls=%async_computation.1 | async-start | bytes 3670016 | tf_op jit(solution)/shard_map/all_to_all | solution.py:854
  48.9 2.2 collective-permute-start.5
  51.9 3.6 %conv.3._buffer = f32[896,768]{1,0:T(8,128)S(1)} custom-call(bf16[14,8,8,768]{3,2,1,0:T(8,128)(2,1)S(1)} %bitcast.40, f32[49,768]{1,0:T(8,128)S(1)} %reshape.128.taps_ref, bf16[288,384]{1,0:T(8,128)(2,1)S(1)} %get-tuple-element.24._after._buffer.refs_1_, bf16[288,384]{1,0:T(8,128)(2,1)S(1)} %get-tuple-element.24._after._buffer.refs_1_), custom_call_target="tpu_custom_call" | custom-call | flops 22478848 | bytes 1376256 | tf_op jit(solution)/shard_map/conv/pallas_call | solution.py:110
  55.5 3.6 %conv.4._buffer = f32[896,768]{1,0:T(8,128)S(1)} custom-call(bf16[14,8,8,768]{3,2,1,0:T(8,128)(2,1)S(1)} %bitcast.41, f32[49,768]{1,0:T(8,128)S(1)} %reshape.128.taps_ref, bf16[288,384]{1,0:T(8,128)(2,1)S(1)} %collective-permute-done.4._after.refs_4_, f32[896,768]{1,0:T(8,128)S(1)} %conv.3._buffer), custom_call_target="tpu_custom_call", output_to_operand_aliasing={{}: (3, {})} | custom-call | flops 22478848 | bytes 1376256 | tf_op jit(solution)/shard_map/conv/pallas_call | solution.py:110
  59.1 3.6 %conv.5.conv_ref = f32[896,768]{1,0:T(8,128)S(1)} custom-call(bf16[14,8,8,768]{3,2,1,0:T(8,128)(2,1)S(1)} %bitcast.42, f32[49,768]{1,0:T(8,128)S(1)} %reshape.128.taps_ref, bf16[288,384]{1,0:T(8,128)(2,1)S(1)} %collective-permute-done.5._after.refs_6_, f32[896,768]{1,0:T(8,128)S(1)} %conv.4._buffer), custom_call_target="tpu_custom_call", output_to_operand_aliasing={{}: (3, {})} | custom-call | flops 22478848 | bytes 1376256 | tf_op jit(solution)/shard_map/conv/pallas_call | solution.py:110
  62.8 5.2 %norm.1 = (bf16[896,768]{1,0:T(8,128)(2,1)S(1)}, f32[896,768]{1,0:T(8,128)S(1)}, f32[896,1]{1,0:T(8,128)S(1)}, bf16[896,768]{1,0:T(8,128)(2,1)}) custom-call(f32[896,768]{1,0:T(8,128)S(1)} %conv.5.conv_ref, bf16[14,8,8,768]{3,2,1,0:T(8,128)(2,1)S(1)} %bitcast.47, s32[1,1]{1,0:T(1,128)S(6)} %copy.65.count_ref, f32[1,768]{1,0:T(1,128)S(1)} %reshape.129.gain_ref, ...), custom_call_target="tpu_custom_call" | custom-call | flops 13762560 | bytes 9633792 | tf_op jit(solution)/shard_map/norm/pallas_call | solution.py:175
  68.0 1.6 copy-done.7
  69.6 2.0 collective-permute-start.10
  73.5 1.6 all-to-all-done.1.second_ref
  75.1 1.4 collective-permute-done.9.theirs_ref
  76.5 40.5 %mlp.1 = (bf16[8,1792,128]{2,1,0:T(8,128)(2,1)}, f32[896,768]{1,0:T(8,128)}, bf16[896,768]{1,0:T(8,128)(2,1)}, f32[1,1152]{1,0:T(1,128)}, f32[1,768]{1,0:T(1,128)}) custom-call(s32[1]{0:T(128)} %bitcast.1.core_ref, s32[16]{0:T(128)} %stack.74.order_ref, bf16[896,768]{1,0:T(8,128)(2,1)} %copy-done.17, bf16[896,768]{1,0:T(8,128)(2,1)} %collective-permute-done.9.theirs_ref, ...), custom_call_target="tpu_custom_call" | custom-call | flops 15854469120 | bytes 10616832 | tf_op jit(solution)/shard_map/mlp/pallas_call | solution.py:403
  117.0 6.9 %all-to-all-start.2 = ((bf16[8,1792,128]{2,1,0:T(8,128)(2,1)}), bf16[8,1792,128]{2,1,0:T(8,128)(2,1)}, u32[]{:S(2)}, u32[]{:S(2)}) async-start(bf16[8,1792,128]{2,1,0:T(8,128)(2,1)} %get-tuple-element.33._after._buffer), calls=%async_computation.2 | async-start | bytes 7340032 | tf_op jit(solution)/shard_map/all_to_all | solution.py:887
  124.8 2.7 %collective-permute-done.11.gn_other_ref = bf16[896,768]{1,0:T(8,128)(2,1)S(1)} collective-permute-done((bf16[896,768]{1,0:T(8,128)(2,1)}, bf16[896,768]{1,0:T(8,128)(2,1)S(1)}, u32[]{:S(2)}, u32[]{:S(2)}) %collective-permute-start.11) | collective-permute-done | bytes 1376288 | tf_op jit(solution)/shard_map/ppermute | solution.py:663
  127.5 1.1 copy-done.11
  128.6 1.8 copy-done.8
  130.4 1.8 copy-done.9
  132.2 1.3 copy-done.12
  133.5 4.5 %unnorm.1 = (f32[896,768]{1,0:T(8,128)S(1)}, f32[2,768]{1,0:T(2,128)S(1)}) custom-call(f32[896,768]{1,0:T(8,128)S(1)} %copy-done.9, bf16[896,768]{1,0:T(8,128)(2,1)S(1)} %copy-done.12, f32[896,768]{1,0:T(8,128)S(1)} %copy-done.8, f32[896,1]{1,0:T(8,128)S(1)} %get-tuple-element.31.inv_ref, f32[1,768]{1,0:T(1,128)S(1)} %reshape.129.gain_ref), custom_call_target="tpu_custom_call" | custom-call | flops 13762560 | bytes 9633792 | tf_op jit(solution)/shard_map/unnorm/pallas_call | solution.py:482
  138.1 4.6 %taps.3._buffer = f32[49,768]{1,0:T(8,128)S(1)} custom-call(bf16[14,8,8,768]{3,2,1,0:T(8,128)(2,1)S(1)} %bitcast.43, f32[896,768]{1,0:T(8,128)S(1)} %get-tuple-element.32.grad_ref, bf16[8,1792,128]{2,1,0:T(8,128)(2,1)S(1)} %copy-done, bf16[8,1792,128]{2,1,0:T(8,128)(2,1)S(1)} %copy-done), custom_call_target="tpu_custom_call" | custom-call | flops 22478848 | bytes 1376256 | tf_op jit(solution)/shard_map/taps/pallas_call | solution.py:556
  142.6 4.6 %taps.4._buffer = f32[49,768]{1,0:T(8,128)S(1)} custom-call(bf16[14,8,8,768]{3,2,1,0:T(8,128)(2,1)S(1)} %bitcast.44, f32[896,768]{1,0:T(8,128)S(1)} %get-tuple-element.32.grad_ref, bf16[8,1792,128]{2,1,0:T(8,128)(2,1)S(1)} %copy-done, f32[49,768]{1,0:T(8,128)S(1)} %taps.3._buffer), custom_call_target="tpu_custom_call", output_to_operand_aliasing={{}: (3, {})} | custom-call | flops 22478848 | bytes 1376256 | tf_op jit(solution)/shard_map/taps/pallas_call | solution.py:556
  147.2 4.6 %taps.5 = f32[49,768]{1,0:T(8,128)S(1)} custom-call(bf16[14,8,8,768]{3,2,1,0:T(8,128)(2,1)S(1)} %bitcast.45, f32[896,768]{1,0:T(8,128)S(1)} %get-tuple-element.32.grad_ref, bf16[8,1792,128]{2,1,0:T(8,128)(2,1)S(1)} %copy-done, f32[49,768]{1,0:T(8,128)S(1)} %taps.4._buffer), custom_call_target="tpu_custom_call", output_to_operand_aliasing={{}: (3, {})} | custom-call | flops 22478848 | bytes 1376256 | tf_op jit(solution)/shard_map/taps/pallas_call | solution.py:556
  152.1 2.0 copy-done.1
  154.2 1.3 copy-done.6
  155.5 4.4 %back.3._buffer = f32[14,8,8,768]{3,2,1,0:T(8,128)} custom-call(bf16[14,8,8,768]{3,2,1,0:T(8,128)(2,1)S(1)} %bitcast.48, f32[896,768]{1,0:T(8,128)S(1)} %get-tuple-element.32.grad_ref, s32[1,1]{1,0:T(1,128)S(6)} %copy.65.count_ref, f32[49,768]{1,0:T(8,128)S(1)} %reshape.128.taps_ref, bf16[8,1792,128]{2,1,0:T(8,128)(2,1)S(1)} %copy-done.1, ...), custom_call_target="tpu_custom_call" | custom-call | flops 22478848 | bytes 2293760 | tf_op jit(solution)/shard_map/back/pallas_call | solution.py:620
  159.9 4.4 %back.4._buffer = f32[14,8,8,768]{3,2,1,0:T(8,128)} custom-call(bf16[14,8,8,768]{3,2,1,0:T(8,128)(2,1)S(1)} %bitcast.49, f32[896,768]{1,0:T(8,128)S(1)} %get-tuple-element.32.grad_ref, s32[1,1]{1,0:T(1,128)S(6)} %copy.65.count_ref, f32[49,768]{1,0:T(8,128)S(1)} %reshape.128.taps_ref, ...), custom_call_target="tpu_custom_call", output_to_operand_aliasing={{}: (5, {})} | custom-call | flops 22478848 | bytes 2293760 | tf_op jit(solution)/shard_map/back/pallas_call | solution.py:620
  164.2 4.4 %back.5._after = f32[14,8,8,768]{3,2,1,0:T(8,128)} custom-call(bf16[14,8,8,768]{3,2,1,0:T(8,128)(2,1)S(1)} %bitcast.50, f32[896,768]{1,0:T(8,128)S(1)} %get-tuple-element.32.grad_ref, s32[1,1]{1,0:T(1,128)S(6)} %copy.65.count_ref, f32[49,768]{1,0:T(8,128)S(1)} %reshape.128.taps_ref, ...), custom_call_target="tpu_custom_call", output_to_operand_aliasing={{}: (5, {})} | custom-call | flops 22478848 | bytes 2293760 | tf_op jit(solution)/shard_map/back/pallas_call | solution.py:620
  168.6 7.4 %all-to-all-done.2.terms_ref = bf16[8,1792,128]{2,1,0:T(8,128)(2,1)} async-done(((bf16[8,1792,128]{2,1,0:T(8,128)(2,1)}), bf16[8,1792,128]{2,1,0:T(8,128)(2,1)}, u32[]{:S(2)}, u32[]{:S(2)}) %all-to-all-start.2) | async-done | bytes 3670048 | tf_op jit(solution)/shard_map/all_to_all | solution.py:887
  176.0 1.8 copy-done.4
  177.8 2.6 %add_up.1 = bf16[1792,128]{1,0:T(8,128)(2,1)S(1)} custom-call(bf16[8,1792,128]{2,1,0:T(8,128)(2,1)} %all-to-all-done.2.terms_ref, f32[14,8,8,768]{3,2,1,0:T(8,128)S(1)} %copy-done.4), custom_call_target="tpu_custom_call" | custom-call | tf_op jit(solution)/shard_map/add_up/pallas_call | solution.py:730
  180.4 1.5 collective-permute-start.12
  182.1 0.8 collective-permute-done.12
  183.0 23.0 %all_to_all.25 = bf16[16,144,128]{2,1,0:T(8,128)(2,1)S(1)} all-to-all(bf16[16,144,128]{2,1,0:T(8,128)(2,1)S(1)} %fusion.1), channel_id=1, replica_groups=mesh['dp'=16,'fsdp'=16] {'fsdp'}, dimensions={0} | all-to-all | bytes 1179648 | tf_op jit(solution)/shard_map/all_to_all | solution.py:903
  206.2 12.6 %all_to_all.26.mine_ref = bf16[8,144,128]{2,1,0:T(8,128)(2,1)S(1)} all-to-all(bf16[8,144,128]{2,1,0:T(8,128)(2,1)S(1)} %broadcast_in_dim.41), channel_id=1, replica_groups={{0,32,64,96,128,160,192,224},{16,48,80,112,144,176,208,240},{1,33,65,97..., dimensions={0} | all-to-all | bytes 589824 | tf_op jit(solution)/shard_map/all_to_all | solution.py:905
  218.7 3.1 %collective-permute-start.13 = (bf16[8,144,128]{2,1,0:T(8,128)(2,1)S(1)}, bf16[8,144,128]{2,1,0:T(8,128)(2,1)S(1)}, u32[]{:S(2)}, u32[]{:S(2)}) collective-permute-start(bf16[8,144,128]{2,1,0:T(8,128)(2,1)S(1)} %all_to_all.26.mine_ref), channel_id=1, source_target_pairs={{0,16},{16,0},{2,18},{18,2},{4,20},{20,4},{6,22},{22,6},{8,24},{24... | collective-permute-start | bytes 884744 | tf_op jit(solution)/shard_map/ppermute | solution.py:663
  221.9 1.1 collective-permute-done.13.theirs_ref
  223.0 1.5 finish.1
  (102 shorter events, 10.2 us)
Async XLA Ops:
  0.7 14.7 %copy-start.19 = (bf16[48,2304]{1,0:T(8,128)(2,1)S(1)}, bf16[48,2304]{1,0:T(8,128)(2,1)}, u32[]{:S(2)}) copy-start(bf16[48,2304]{1,0:T(8,128)(2,1)} %param.16) | copy-start | bytes 663556
  5.2 22.7 %all-to-all-start = ((bf16[16,88,128]{2,1,0:T(8,128)(2,1)}), bf16[16,88,128]{2,1,0:T(8,128)(2,1)S(1)}, u32[]{:S(2)}, u32[]{:S(2)}) async-start(bf16[16,88,128]{2,1,0:T(8,128)(2,1)} %broadcast_in_dim.37), calls=%async_computation | async-start | bytes 720896 | tf_op jit(solution)/shard_map/all_to_all | solution.py:845
  15.4 3.9 %collective-permute-start.1 = (bf16[144,384]{1,0:T(8,128)(2,1)S(1)}, bf16[144,384]{1,0:T(8,128)(2,1)S(1)}, u32[]{:S(2)}, u32[]{:S(2)}) collective-permute-start(bf16[144,384]{1,0:T(8,128)(2,1)S(1)} %pad_maximum_fusion.3), channel_id=1, source_target_pairs={{0,1},{1,0},{2,3},{3,2},{4,5},{5,4},{6,7},{7,6},{8,9},{9,8},{10,11... | collective-permute-start | bytes 331784 | tf_op jit(solution)/shard_map/ppermute | solution.py:667
  19.3 22.6 %copy-start.18 = (bf16[288,384]{1,0:T(8,128)(2,1)}, bf16[288,384]{1,0:T(8,128)(2,1)S(1)}, u32[]{:S(2)}) copy-start(bf16[288,384]{1,0:T(8,128)(2,1)S(1)} %pad_maximum_fusion.1.refs_0_) | copy-start | bytes 663556
  19.3 12.2 %collective-permute-start.2 = (bf16[288,384]{1,0:T(8,128)(2,1)S(1)}, bf16[288,384]{1,0:T(8,128)(2,1)S(1)}, u32[]{:S(2)}, u32[]{:S(2)}) collective-permute-start(bf16[288,384]{1,0:T(8,128)(2,1)S(1)} %pad_maximum_fusion.1.refs_0_), channel_id=1, source_target_pairs={{0,2},{16,18},{2,4},{18,20},{4,6},{20,22},{6,8},{22,24},{8,10},{24... | collective-permute-start | bytes 663560 | tf_op jit(solution)/shard_map/ppermute | solution.py:663
  21.3 10.2 %collective-permute-start.3 = (bf16[288,384]{1,0:T(8,128)(2,1)S(1)}, bf16[288,384]{1,0:T(8,128)(2,1)S(1)}, u32[]{:S(2)}, u32[]{:S(2)}) collective-permute-start(bf16[288,384]{1,0:T(8,128)(2,1)S(1)} %pad_maximum_fusion.1.refs_0_), channel_id=1, source_target_pairs={{0,14},{16,30},{2,0},{18,16},{4,2},{20,18},{6,4},{22,20},{8,6},{24... | collective-permute-start | bytes 663560 | tf_op jit(solution)/shard_map/ppermute | solution.py:663
  27.9 4.5 %collective-permute-start = (bf16[8,56,128]{2,1,0:T(8,128)(2,1)S(1)}, bf16[8,56,128]{2,1,0:T(8,128)(2,1)S(1)}, u32[]{:S(2)}, u32[]{:S(2)}) collective-permute-start(bf16[8,56,128]{2,1,0:T(8,128)(2,1)S(1)} %get-tuple-element.67), channel_id=1, source_target_pairs={{0,16},{16,0},{2,18},{18,2},{4,20},{20,4},{6,22},{22,6},{8,24},{24... | collective-permute-start | bytes 344072 | tf_op jit(solution)/shard_map/ppermute | solution.py:663
  33.9 8.0 %copy-start.15 = (bf16[288,384]{1,0:T(8,128)(2,1)}, bf16[288,384]{1,0:T(8,128)(2,1)S(1)}, u32[]{:S(2)}) copy-start(bf16[288,384]{1,0:T(8,128)(2,1)S(1)} %get-tuple-element.23.refs_2_) | copy-start | bytes 663556
  33.9 17.9 %copy-start.10 = (bf16[288,384]{1,0:T(8,128)(2,1)}, bf16[288,384]{1,0:T(8,128)(2,1)S(1)}, u32[]{:S(2)}) copy-start(bf16[288,384]{1,0:T(8,128)(2,1)S(1)} %get-tuple-element.24._after._buffer.refs_1_) | copy-start | bytes 663556
  33.9 7.9 %collective-permute-start.6 = (bf16[288,384]{1,0:T(8,128)(2,1)S(1)}, bf16[288,384]{1,0:T(8,128)(2,1)S(1)}, u32[]{:S(2)}, u32[]{:S(2)}) collective-permute-start(bf16[288,384]{1,0:T(8,128)(2,1)S(1)} %get-tuple-element.24._after._buffer.refs_1_), channel_id=1, source_target_pairs={{0,2},{16,18},{2,4},{18,20},{4,6},{20,22},{6,8},{22,24},{8,10},{24... | collective-permute-start | bytes 663560 | tf_op jit(solution)/shard_map/ppermute | solution.py:663
  34.6 14.2 %collective-permute-start.4 = (bf16[288,384]{1,0:T(8,128)(2,1)S(1)}, bf16[288,384]{1,0:T(8,128)(2,1)S(1)}, u32[]{:S(2)}, u32[]{:S(2)}) collective-permute-start(bf16[288,384]{1,0:T(8,128)(2,1)S(1)} %get-tuple-element.23.refs_2_), channel_id=1, source_target_pairs={{0,14},{16,30},{2,0},{18,16},{4,2},{20,18},{6,4},{22,20},{8,6},{24... | collective-permute-start | bytes 663560 | tf_op jit(solution)/shard_map/ppermute | solution.py:663
  41.8 0.7 copy-start.22
  41.8 9.3 %collective-permute-start.7 = (bf16[288,384]{1,0:T(8,128)(2,1)S(1)}, bf16[288,384]{1,0:T(8,128)(2,1)}, u32[]{:S(2)}, u32[]{:S(2)}) collective-permute-start(bf16[288,384]{1,0:T(8,128)(2,1)S(1)} %collective-permute-done.6.refs_3_), channel_id=1, source_target_pairs={{0,2},{16,18},{2,4},{18,20},{4,6},{20,22},{6,8},{22,24},{8,10},{24... | collective-permute-start | bytes 663560 | tf_op jit(solution)/shard_map/ppermute | solution.py:663
  42.5 32.6 %all-to-all-start.1 = ((bf16[8,896,128]{2,1,0:T(8,128)(2,1)}), bf16[8,896,128]{2,1,0:T(8,128)(2,1)}, u32[]{:S(2)}, u32[]{:S(2)}) async-start(bf16[8,896,128]{2,1,0:T(8,128)(2,1)} %get-tuple-element.27), calls=%async_computation.1 | async-start | bytes 3670016 | tf_op jit(solution)/shard_map/all_to_all | solution.py:854
  48.8 3.0 %copy-start.2 = (bf16[1,14,8,8,768]{4,3,2,1,0:T(8,128)(2,1)S(1)}, bf16[1,14,8,8,768]{4,3,2,1,0:T(8,128)(2,1)}, u32[]{:S(2)}) copy-start(bf16[1,14,8,8,768]{4,3,2,1,0:T(8,128)(2,1)} %param.10) | copy-start | bytes 4128772
  48.9 6.6 %copy-start.13 = (bf16[288,384]{1,0:T(8,128)(2,1)}, bf16[288,384]{1,0:T(8,128)(2,1)S(1)}, u32[]{:S(2)}) copy-start(bf16[288,384]{1,0:T(8,128)(2,1)S(1)} %collective-permute-done.4._after.refs_4_) | copy-start | bytes 663556
  48.9 10.2 %collective-permute-start.5 = (bf16[288,384]{1,0:T(8,128)(2,1)S(1)}, bf16[288,384]{1,0:T(8,128)(2,1)S(1)}, u32[]{:S(2)}, u32[]{:S(2)}) collective-permute-start(bf16[288,384]{1,0:T(8,128)(2,1)S(1)} %collective-permute-done.4._after.refs_4_), channel_id=1, source_target_pairs={{0,14},{16,30},{2,0},{18,16},{4,2},{20,18},{6,4},{22,20},{8,6},{24... | collective-permute-start | bytes 663560 | tf_op jit(solution)/shard_map/ppermute | solution.py:663
  51.1 11.7 %collective-permute-start.8 = (bf16[288,384]{1,0:T(8,128)(2,1)}, bf16[288,384]{1,0:T(8,128)(2,1)S(1)}, u32[]{:S(2)}, u32[]{:S(2)}) collective-permute-start(bf16[288,384]{1,0:T(8,128)(2,1)} %collective-permute-done.7.refs_5_), channel_id=1, source_target_pairs={{0,2},{16,18},{2,4},{18,20},{4,6},{20,22},{6,8},{22,24},{8,10},{24... | collective-permute-start | bytes 663560 | tf_op jit(solution)/shard_map/ppermute | solution.py:663
  59.1 3.7 %copy-start.5 = (bf16[1,14,8,8,768]{4,3,2,1,0:T(8,128)(2,1)S(1)}, bf16[1,14,8,8,768]{4,3,2,1,0:T(8,128)(2,1)}, u32[]{:S(2)}) copy-start(bf16[1,14,8,8,768]{4,3,2,1,0:T(8,128)(2,1)} %param.11) | copy-start | bytes 4128772
  59.1 3.6 %copy-start.14 = (bf16[288,384]{1,0:T(8,128)(2,1)}, bf16[288,384]{1,0:T(8,128)(2,1)S(1)}, u32[]{:S(2)}) copy-start(bf16[288,384]{1,0:T(8,128)(2,1)S(1)} %collective-permute-done.5._after.refs_6_) | copy-start | bytes 663556
  62.7 5.2 %copy-start.16 = (bf16[288,384]{1,0:T(8,128)(2,1)}, bf16[288,384]{1,0:T(8,128)(2,1)S(1)}, u32[]{:S(2)}) copy-start(bf16[288,384]{1,0:T(8,128)(2,1)S(1)} %collective-permute-done.8._after.refs_7_) | copy-start | bytes 663556
  68.0 1.6 copy-start.7
  69.6 6.9 %copy-start.17 = (bf16[896,768]{1,0:T(8,128)(2,1)}, bf16[896,768]{1,0:T(8,128)(2,1)S(1)}, u32[]{:S(2)}) copy-start(bf16[896,768]{1,0:T(8,128)(2,1)S(1)} %get-tuple-element.25.mine_ref) | copy-start | bytes 4128772
  69.6 5.5 %collective-permute-start.10 = (bf16[896,768]{1,0:T(8,128)(2,1)}, bf16[896,768]{1,0:T(8,128)(2,1)}, u32[]{:S(2)}, u32[]{:S(2)}) collective-permute-start(bf16[896,768]{1,0:T(8,128)(2,1)} %get-tuple-element.26.gb_mine_ref), channel_id=1, source_target_pairs={{0,16},{16,0},{2,18},{18,2},{4,20},{20,4},{6,22},{22,6},{8,24},{24... | collective-permute-start | bytes 4128776 | tf_op jit(solution)/shard_map/ppermute | solution.py:663
  71.6 4.9 %collective-permute-start.9 = (bf16[896,768]{1,0:T(8,128)(2,1)S(1)}, bf16[896,768]{1,0:T(8,128)(2,1)}, u32[]{:S(2)}, u32[]{:S(2)}) collective-permute-start(bf16[896,768]{1,0:T(8,128)(2,1)S(1)} %get-tuple-element.25.mine_ref), channel_id=1, source_target_pairs={{0,16},{16,0},{2,18},{18,2},{4,20},{20,4},{6,22},{22,6},{8,24},{24... | collective-permute-start | bytes 4128776 | tf_op jit(solution)/shard_map/ppermute | solution.py:663
  116.9 7.6 %copy-start.20 = (f32[1,1152]{1,0:T(1,128)S(1)}, f32[1,1152]{1,0:T(1,128)}, u32[]{:S(2)}) copy-start(f32[1,1152]{1,0:T(1,128)} %get-tuple-element.36) | copy-start | bytes 13828
  117.0 7.7 %copy-start.21 = (f32[1,768]{1,0:T(1,128)S(1)}, f32[1,768]{1,0:T(1,128)}, u32[]{:S(2)}) copy-start(f32[1,768]{1,0:T(1,128)} %get-tuple-element.35) | copy-start | bytes 9220
  117.0 59.0 %all-to-all-start.2 = ((bf16[8,1792,128]{2,1,0:T(8,128)(2,1)}), bf16[8,1792,128]{2,1,0:T(8,128)(2,1)}, u32[]{:S(2)}, u32[]{:S(2)}) async-start(bf16[8,1792,128]{2,1,0:T(8,128)(2,1)} %get-tuple-element.33._after._buffer), calls=%async_computation.2 | async-start | bytes 7340032 | tf_op jit(solution)/shard_map/all_to_all | solution.py:887
  123.9 3.6 %collective-permute-start.11 = (bf16[896,768]{1,0:T(8,128)(2,1)}, bf16[896,768]{1,0:T(8,128)(2,1)S(1)}, u32[]{:S(2)}, u32[]{:S(2)}) collective-permute-start(bf16[896,768]{1,0:T(8,128)(2,1)} %get-tuple-element.29), channel_id=1, source_target_pairs={{0,16},{16,0},{2,18},{18,2},{4,20},{20,4},{6,22},{22,6},{8,24},{24... | collective-permute-start | bytes 4128776 | tf_op jit(solution)/shard_map/ppermute | solution.py:663
  127.5 1.1 copy-start.11
  128.6 1.8 copy-start.8
  130.4 1.8 copy-start.9
  132.2 1.3 copy-start.12
  133.5 4.5 %copy-start = (bf16[8,1792,128]{2,1,0:T(8,128)(2,1)S(1)}, bf16[8,1792,128]{2,1,0:T(8,128)(2,1)}, u32[]{:S(2)}) copy-start(bf16[8,1792,128]{2,1,0:T(8,128)(2,1)} %get-tuple-element.33._after._buffer) | copy-start | bytes 11010052
  133.5 4.6 %copy-start.3 = (bf16[1,14,8,8,768]{4,3,2,1,0:T(8,128)(2,1)S(1)}, bf16[1,14,8,8,768]{4,3,2,1,0:T(8,128)(2,1)}, u32[]{:S(2)}) copy-start(bf16[1,14,8,8,768]{4,3,2,1,0:T(8,128)(2,1)} %param.10) | copy-start | bytes 4128772
  152.1 2.0 copy-start.1
  154.2 1.3 copy-start.6
  176.0 1.8 copy-start.4
  180.4 2.5 %collective-permute-start.12 = (bf16[8,56,128]{2,1,0:T(8,128)(2,1)S(1)}, bf16[8,56,128]{2,1,0:T(8,128)(2,1)S(1)}, u32[]{:S(2)}, u32[]{:S(2)}) collective-permute-start(bf16[8,56,128]{2,1,0:T(8,128)(2,1)S(1)} %get-tuple-element.66), channel_id=1, source_target_pairs={{0,16},{16,0},{2,18},{18,2},{4,20},{20,4},{6,22},{22,6},{8,24},{24... | collective-permute-start | bytes 344072 | tf_op jit(solution)/shard_map/ppermute | solution.py:663
  218.7 4.3 %collective-permute-start.13 = (bf16[8,144,128]{2,1,0:T(8,128)(2,1)S(1)}, bf16[8,144,128]{2,1,0:T(8,128)(2,1)S(1)}, u32[]{:S(2)}, u32[]{:S(2)}) collective-permute-start(bf16[8,144,128]{2,1,0:T(8,128)(2,1)S(1)} %all_to_all.26.mine_ref), channel_id=1, source_target_pairs={{0,16},{16,0},{2,18},{18,2},{4,20},{20,4},{6,22},{22,6},{8,24},{24... | collective-permute-start | bytes 884744 | tf_op jit(solution)/shard_map/ppermute | solution.py:663

commit v3 on v2

--- a/solution.py
+++ b/solution.py
@@ -305,7 +305,7 @@
             return bias_sum + jnp.sum(grad_preact.astype(F32), axis=0, keepdims=True)
 
         grad_bias_ref[:, units_at] = lax.fori_loop(
-            0, 2, block, jnp.zeros((1, wide), F32), unroll=True
+            0, 2, block, jnp.zeros((1, wide), F32)
         )
 
     def sums(start, wide, slot):
@@ -314,12 +314,15 @@
         sum_second[units_at, :] = dot(actives[:, lanes], cots[...], (((0,), (0,)), ((), ())))
         sum_first[:, units_at] = dot(flipped[...], grads[:, lanes], (((1,), (0,)), ((), ())))
 
-    chunks = [(start, min(BLOCK, hidden - start)) for start in range(0, hidden, BLOCK)]
-    for i, (start, wide) in enumerate(chunks):
-        chunk(start, wide, i % 2)
-        if i:
-            sums(*chunks[i - 1], (i - 1) % 2)
-    sums(*chunks[-1], (len(chunks) - 1) % 2)
+    def whole_chunk(h, _):
+        chunk(aligned(h, BLOCK), BLOCK, 0)
+        sums(aligned(h, BLOCK), BLOCK, 0)
+        return 0
+
+    lax.fori_loop(0, hidden // BLOCK, whole_chunk, 0)
+    if hidden % BLOCK:
+        chunk(hidden // BLOCK * BLOCK, hidden % BLOCK, 0)
+        sums(hidden // BLOCK * BLOCK, hidden % BLOCK, 0)
 
     leaving = []
 
@@ -420,8 +423,8 @@
             pltpu.VMEM((2 * tokens, channels), BF16),
             pltpu.VMEM((channels, 2 * tokens), BF16),
             pltpu.VMEM((2 * tokens, channels), F32),
-            pltpu.VMEM((2 * tokens, 2 * BLOCK), BF16),
-            pltpu.VMEM((2 * tokens, 2 * BLOCK), BF16),
+            pltpu.VMEM((2 * tokens, BLOCK), BF16),
+            pltpu.VMEM((2 * tokens, BLOCK), BF16),
             pltpu.VMEM(sums, BF16),
             pltpu.VMEM((tokens, channels), BF16),
             pltpu.SemaphoreType.DMA((count,)),

time: 231 us -> 220 us (0.952); the launches traced: 227 us -> 219 us
  Pallas kernels: 93.4 us -> 85.4 us
    pallas_call x1, Pallas kernels: 40.5 us -> 32.5 us  [mlp(): pl.pallas_call(functools.partial(mlp_kernel, count), in_specs=[smem, smem...]
  transfers between devices with their start and end apart: 17 -> 17, of which waited for: 10 -> 10; matrix products, arithmetic and copies ran while one was open for 1% -> 1% of each run, Pallas kernels for 21% -> 22%
where the time goes in v3:
time: 220 us; the launch traced here: 219 us
  Pallas kernels  85.4 us (39%)
  starting transfers between devices  44 us (20%)
  blocking collectives  35.5 us (16%)
  waiting for transfers between devices  28.7 us (13%)
  local copies, waits for them, and re-layouts  22.3 us (10%)
    pallas_call x1, Pallas kernels, mlp(): pl.pallas_call(functools.partial(mlp_kernel, count), in_specs=[smem, smem...  32.5 us
    all_to_all x1, blocking collectives, local(): terms = lax.all_to_all(terms, 'fsdp', 0, 0, tiled=True)  23 us
    ppermute x13, starting transfers between devices, move(): return lax.ppermute(value, AXES, pairs)  19.2 us
    unnamed x49, local copies, waits for them, and re-layouts  14.9 us
    pallas_call x3, Pallas kernels, taps_part(): pl.pallas_call(functools.partial(taps_kernel, slots), grid=(GROUP_STEPS,)...  13.7 us
    pallas_call x3, Pallas kernels, back_part(): pl.pallas_call(functools.partial(back_kernel, slots), grid=(GROUP_STEPS,)...  13.1 us
    all_to_all x1, blocking collectives, local(): lax.all_to_all(jnp.broadcast_to(terms[None], (chips,) + terms.shape), 'dp...  12.5 us
    ppermute x13, waiting for transfers between devices, move(): return lax.ppermute(value, AXES, pairs)  11.7 us
  transfers between devices with their start and end apart: 17, of which 10 were waited for; matrix products, arithmetic and copies ran while one was open for 1% of the time, Pallas kernels for 22%

profile of v3, /device:TPU:1, one launch (start us, length us, event | category | flops | bytes accessed | tf_op | source)
XLA Modules:
  0.0 218.8 jit_solution(9813875101006405897)
XLA Ops:
  0.7 1.2 reshape.119
  5.2 10.1 %all-to-all-start = ((bf16[16,88,128]{2,1,0:T(8,128)(2,1)}), bf16[16,88,128]{2,1,0:T(8,128)(2,1)S(1)}, u32[]{:S(2)}, u32[]{:S(2)}) async-start(bf16[16,88,128]{2,1,0:T(8,128)(2,1)} %broadcast_in_dim.37), calls=%async_computation | async-start | bytes 720896 | tf_op jit(solution)/shard_map/all_to_all | solution.py:848
  15.4 1.4 collective-permute-start.1
  16.8 2.4 %collective-permute-done.1 = bf16[144,384]{1,0:T(8,128)(2,1)S(1)} collective-permute-done((bf16[144,384]{1,0:T(8,128)(2,1)S(1)}, bf16[144,384]{1,0:T(8,128)(2,1)S(1)}, u32[]{:S(2)}, u32[]{:S(2)}) %collective-permute-start.1) | collective-permute-done | bytes 110624 | tf_op jit(solution)/shard_map/ppermute | solution.py:670
  19.3 2.0 collective-permute-start.2
  21.3 1.4 collective-permute-start.3
  22.7 5.2 %all-to-all-done = bf16[16,88,128]{2,1,0:T(8,128)(2,1)S(1)} async-done(((bf16[16,88,128]{2,1,0:T(8,128)(2,1)}), bf16[16,88,128]{2,1,0:T(8,128)(2,1)S(1)}, u32[]{:S(2)}, u32[]{:S(2)}) %all-to-all-start) | async-done | bytes 360480 | tf_op jit(solution)/shard_map/all_to_all | solution.py:848
  27.9 3.5 %collective-permute-start = (bf16[8,56,128]{2,1,0:T(8,128)(2,1)S(1)}, bf16[8,56,128]{2,1,0:T(8,128)(2,1)S(1)}, u32[]{:S(2)}, u32[]{:S(2)}) collective-permute-start(bf16[8,56,128]{2,1,0:T(8,128)(2,1)S(1)} %get-tuple-element.67), channel_id=1, source_target_pairs={{0,16},{16,0},{2,18},{18,2},{4,20},{20,4},{6,22},{22,6},{8,24},{24... | collective-permute-start | bytes 344072 | tf_op jit(solution)/shard_map/ppermute | solution.py:666
  31.5 1.0 collective-permute-done.swapped_ref
  32.4 1.5 copies.1
  34.6 2.7 %collective-permute-start.4 = (bf16[288,384]{1,0:T(8,128)(2,1)S(1)}, bf16[288,384]{1,0:T(8,128)(2,1)S(1)}, u32[]{:S(2)}, u32[]{:S(2)}) collective-permute-start(bf16[288,384]{1,0:T(8,128)(2,1)S(1)} %get-tuple-element.23.refs_2_), channel_id=1, source_target_pairs={{0,14},{16,30},{2,0},{18,16},{4,2},{20,18},{6,4},{22,20},{8,6},{24... | collective-permute-start | bytes 663560 | tf_op jit(solution)/shard_map/ppermute | solution.py:666
  37.3 4.5 %collective-permute-done.6.refs_3_ = bf16[288,384]{1,0:T(8,128)(2,1)S(1)} collective-permute-done((bf16[288,384]{1,0:T(8,128)(2,1)S(1)}, bf16[288,384]{1,0:T(8,128)(2,1)S(1)}, u32[]{:S(2)}, u32[]{:S(2)}) %collective-permute-start.6) | collective-permute-done | bytes 221216 | tf_op jit(solution)/shard_map/ppermute | solution.py:666
  42.5 6.4 %all-to-all-start.1 = ((bf16[8,896,128]{2,1,0:T(8,128)(2,1)}), bf16[8,896,128]{2,1,0:T(8,128)(2,1)}, u32[]{:S(2)}, u32[]{:S(2)}) async-start(bf16[8,896,128]{2,1,0:T(8,128)(2,1)} %get-tuple-element.27), calls=%async_computation.1 | async-start | bytes 3670016 | tf_op jit(solution)/shard_map/all_to_all | solution.py:857
  48.9 2.2 %collective-permute-start.5 = (bf16[288,384]{1,0:T(8,128)(2,1)S(1)}, bf16[288,384]{1,0:T(8,128)(2,1)S(1)}, u32[]{:S(2)}, u32[]{:S(2)}) collective-permute-start(bf16[288,384]{1,0:T(8,128)(2,1)S(1)} %collective-permute-done.4._after.refs_4_), channel_id=1, source_target_pairs={{0,14},{16,30},{2,0},{18,16},{4,2},{20,18},{6,4},{22,20},{8,6},{24... | collective-permute-start | bytes 663560 | tf_op jit(solution)/shard_map/ppermute | solution.py:666
  51.9 3.6 %conv.3._buffer = f32[896,768]{1,0:T(8,128)S(1)} custom-call(bf16[14,8,8,768]{3,2,1,0:T(8,128)(2,1)S(1)} %bitcast.40, f32[49,768]{1,0:T(8,128)S(1)} %reshape.128.taps_ref, bf16[288,384]{1,0:T(8,128)(2,1)S(1)} %get-tuple-element.24._after._buffer.refs_1_, bf16[288,384]{1,0:T(8,128)(2,1)S(1)} %get-tuple-element.24._after._buffer.refs_1_), custom_call_target="tpu_custom_call" | custom-call | flops 22478848 | bytes 1376256 | tf_op jit(solution)/shard_map/conv/pallas_call | solution.py:110
  55.5 3.6 %conv.4._buffer = f32[896,768]{1,0:T(8,128)S(1)} custom-call(bf16[14,8,8,768]{3,2,1,0:T(8,128)(2,1)S(1)} %bitcast.41, f32[49,768]{1,0:T(8,128)S(1)} %reshape.128.taps_ref, bf16[288,384]{1,0:T(8,128)(2,1)S(1)} %collective-permute-done.4._after.refs_4_, f32[896,768]{1,0:T(8,128)S(1)} %conv.3._buffer), custom_call_target="tpu_custom_call", output_to_operand_aliasing={{}: (3, {})} | custom-call | flops 22478848 | bytes 1376256 | tf_op jit(solution)/shard_map/conv/pallas_call | solution.py:110
  59.1 3.6 %conv.5.conv_ref = f32[896,768]{1,0:T(8,128)S(1)} custom-call(bf16[14,8,8,768]{3,2,1,0:T(8,128)(2,1)S(1)} %bitcast.42, f32[49,768]{1,0:T(8,128)S(1)} %reshape.128.taps_ref, bf16[288,384]{1,0:T(8,128)(2,1)S(1)} %collective-permute-done.5._after.refs_6_, f32[896,768]{1,0:T(8,128)S(1)} %conv.4._buffer), custom_call_target="tpu_custom_call", output_to_operand_aliasing={{}: (3, {})} | custom-call | flops 22478848 | bytes 1376256 | tf_op jit(solution)/shard_map/conv/pallas_call | solution.py:110
  62.8 5.2 %norm.1 = (bf16[896,768]{1,0:T(8,128)(2,1)S(1)}, f32[896,768]{1,0:T(8,128)S(1)}, f32[896,1]{1,0:T(8,128)S(1)}, bf16[896,768]{1,0:T(8,128)(2,1)}) custom-call(f32[896,768]{1,0:T(8,128)S(1)} %conv.5.conv_ref, bf16[14,8,8,768]{3,2,1,0:T(8,128)(2,1)S(1)} %bitcast.47, s32[1,1]{1,0:T(1,128)S(6)} %copy.65.count_ref, f32[1,768]{1,0:T(1,128)S(1)} %reshape.129.gain_ref, ...), custom_call_target="tpu_custom_call" | custom-call | flops 13762560 | bytes 9633792 | tf_op jit(solution)/shard_map/norm/pallas_call | solution.py:175
  68.0 1.6 copy-done.7
  69.6 2.0 collective-permute-start.10
  73.1 2.0 all-to-all-done.1.second_ref
  75.1 1.6 collective-permute-done.10.gb_theirs_ref
  76.7 32.5 %mlp.1 = (bf16[8,1792,128]{2,1,0:T(8,128)(2,1)}, f32[896,768]{1,0:T(8,128)}, bf16[896,768]{1,0:T(8,128)(2,1)}, f32[1,1152]{1,0:T(1,128)}, f32[1,768]{1,0:T(1,128)}) custom-call(s32[1]{0:T(128)} %bitcast.1.core_ref, s32[16]{0:T(128)} %stack.74.order_ref, bf16[896,768]{1,0:T(8,128)(2,1)} %copy-done.17, bf16[896,768]{1,0:T(8,128)(2,1)} %collective-permute-done.9.theirs_ref, ...), custom_call_target="tpu_custom_call" | custom-call | flops 15854469120 | bytes 10616832 | tf_op jit(solution)/shard_map/mlp/pallas_call | solution.py:406
  109.2 6.9 %all-to-all-start.2 = ((bf16[8,1792,128]{2,1,0:T(8,128)(2,1)}), bf16[8,1792,128]{2,1,0:T(8,128)(2,1)}, u32[]{:S(2)}, u32[]{:S(2)}) async-start(bf16[8,1792,128]{2,1,0:T(8,128)(2,1)} %get-tuple-element.33._after._buffer), calls=%async_computation.2 | async-start | bytes 7340032 | tf_op jit(solution)/shard_map/all_to_all | solution.py:890
  117.0 2.7 %collective-permute-done.11.gn_other_ref = bf16[896,768]{1,0:T(8,128)(2,1)S(1)} collective-permute-done((bf16[896,768]{1,0:T(8,128)(2,1)}, bf16[896,768]{1,0:T(8,128)(2,1)S(1)}, u32[]{:S(2)}, u32[]{:S(2)}) %collective-permute-start.11) | collective-permute-done | bytes 1376288 | tf_op jit(solution)/shard_map/ppermute | solution.py:666
  119.7 1.1 copy-done.11
  120.8 1.8 copy-done.8
  122.6 1.8 copy-done.9
  124.4 1.3 copy-done.12
  125.7 4.5 %unnorm.1 = (f32[896,768]{1,0:T(8,128)S(1)}, f32[2,768]{1,0:T(2,128)S(1)}) custom-call(f32[896,768]{1,0:T(8,128)S(1)} %copy-done.9, bf16[896,768]{1,0:T(8,128)(2,1)S(1)} %copy-done.12, f32[896,768]{1,0:T(8,128)S(1)} %copy-done.8, f32[896,1]{1,0:T(8,128)S(1)} %get-tuple-element.31.inv_ref, f32[1,768]{1,0:T(1,128)S(1)} %reshape.129.gain_ref), custom_call_target="tpu_custom_call" | custom-call | flops 13762560 | bytes 9633792 | tf_op jit(solution)/shard_map/unnorm/pallas_call | solution.py:485
  130.3 4.6 %taps.3._buffer = f32[49,768]{1,0:T(8,128)S(1)} custom-call(bf16[14,8,8,768]{3,2,1,0:T(8,128)(2,1)S(1)} %bitcast.43, f32[896,768]{1,0:T(8,128)S(1)} %get-tuple-element.32.grad_ref, bf16[8,1792,128]{2,1,0:T(8,128)(2,1)S(1)} %copy-done, bf16[8,1792,128]{2,1,0:T(8,128)(2,1)S(1)} %copy-done), custom_call_target="tpu_custom_call" | custom-call | flops 22478848 | bytes 1376256 | tf_op jit(solution)/shard_map/taps/pallas_call | solution.py:559
  134.8 4.6 %taps.4._buffer = f32[49,768]{1,0:T(8,128)S(1)} custom-call(bf16[14,8,8,768]{3,2,1,0:T(8,128)(2,1)S(1)} %bitcast.44, f32[896,768]{1,0:T(8,128)S(1)} %get-tuple-element.32.grad_ref, bf16[8,1792,128]{2,1,0:T(8,128)(2,1)S(1)} %copy-done, f32[49,768]{1,0:T(8,128)S(1)} %taps.3._buffer), custom_call_target="tpu_custom_call", output_to_operand_aliasing={{}: (3, {})} | custom-call | flops 22478848 | bytes 1376256 | tf_op jit(solution)/shard_map/taps/pallas_call | solution.py:559
  139.4 4.6 %taps.5 = f32[49,768]{1,0:T(8,128)S(1)} custom-call(bf16[14,8,8,768]{3,2,1,0:T(8,128)(2,1)S(1)} %bitcast.45, f32[896,768]{1,0:T(8,128)S(1)} %get-tuple-element.32.grad_ref, bf16[8,1792,128]{2,1,0:T(8,128)(2,1)S(1)} %copy-done, f32[49,768]{1,0:T(8,128)S(1)} %taps.4._buffer), custom_call_target="tpu_custom_call", output_to_operand_aliasing={{}: (3, {})} | custom-call | flops 22478848 | bytes 1376256 | tf_op jit(solution)/shard_map/taps/pallas_call | solution.py:559
  144.3 2.0 copy-done.1
  146.4 1.3 copy-done.6
  147.7 4.4 %back.3._buffer = f32[14,8,8,768]{3,2,1,0:T(8,128)} custom-call(bf16[14,8,8,768]{3,2,1,0:T(8,128)(2,1)S(1)} %bitcast.48, f32[896,768]{1,0:T(8,128)S(1)} %get-tuple-element.32.grad_ref, s32[1,1]{1,0:T(1,128)S(6)} %copy.65.count_ref, f32[49,768]{1,0:T(8,128)S(1)} %reshape.128.taps_ref, bf16[8,1792,128]{2,1,0:T(8,128)(2,1)S(1)} %copy-done.1, ...), custom_call_target="tpu_custom_call" | custom-call | flops 22478848 | bytes 2293760 | tf_op jit(solution)/shard_map/back/pallas_call | solution.py:623
  152.1 4.4 %back.4._buffer = f32[14,8,8,768]{3,2,1,0:T(8,128)} custom-call(bf16[14,8,8,768]{3,2,1,0:T(8,128)(2,1)S(1)} %bitcast.49, f32[896,768]{1,0:T(8,128)S(1)} %get-tuple-element.32.grad_ref, s32[1,1]{1,0:T(1,128)S(6)} %copy.65.count_ref, f32[49,768]{1,0:T(8,128)S(1)} %reshape.128.taps_ref, ...), custom_call_target="tpu_custom_call", output_to_operand_aliasing={{}: (5, {})} | custom-call | flops 22478848 | bytes 2293760 | tf_op jit(solution)/shard_map/back/pallas_call | solution.py:623
  156.4 4.4 %back.5._after = f32[14,8,8,768]{3,2,1,0:T(8,128)} custom-call(bf16[14,8,8,768]{3,2,1,0:T(8,128)(2,1)S(1)} %bitcast.50, f32[896,768]{1,0:T(8,128)S(1)} %get-tuple-element.32.grad_ref, s32[1,1]{1,0:T(1,128)S(6)} %copy.65.count_ref, f32[49,768]{1,0:T(8,128)S(1)} %reshape.128.taps_ref, ...), custom_call_target="tpu_custom_call", output_to_operand_aliasing={{}: (5, {})} | custom-call | flops 22478848 | bytes 2293760 | tf_op jit(solution)/shard_map/back/pallas_call | solution.py:623
  160.8 7.4 %all-to-all-done.2.terms_ref = bf16[8,1792,128]{2,1,0:T(8,128)(2,1)} async-done(((bf16[8,1792,128]{2,1,0:T(8,128)(2,1)}), bf16[8,1792,128]{2,1,0:T(8,128)(2,1)}, u32[]{:S(2)}, u32[]{:S(2)}) %all-to-all-start.2) | async-done | bytes 3670048 | tf_op jit(solution)/shard_map/all_to_all | solution.py:890
  168.2 1.8 copy-done.4
  170.0 2.6 %add_up.1 = bf16[1792,128]{1,0:T(8,128)(2,1)S(1)} custom-call(bf16[8,1792,128]{2,1,0:T(8,128)(2,1)} %all-to-all-done.2.terms_ref, f32[14,8,8,768]{3,2,1,0:T(8,128)S(1)} %copy-done.4), custom_call_target="tpu_custom_call" | custom-call | tf_op jit(solution)/shard_map/add_up/pallas_call | solution.py:733
  172.6 1.5 collective-permute-start.12
  174.3 0.8 collective-permute-done.12
  175.2 23.0 %all_to_all.25 = bf16[16,144,128]{2,1,0:T(8,128)(2,1)S(1)} all-to-all(bf16[16,144,128]{2,1,0:T(8,128)(2,1)S(1)} %fusion.1), channel_id=1, replica_groups=mesh['dp'=16,'fsdp'=16] {'fsdp'}, dimensions={0} | all-to-all | bytes 1179648 | tf_op jit(solution)/shard_map/all_to_all | solution.py:906
  198.4 12.5 %all_to_all.26.mine_ref = bf16[8,144,128]{2,1,0:T(8,128)(2,1)S(1)} all-to-all(bf16[8,144,128]{2,1,0:T(8,128)(2,1)S(1)} %broadcast_in_dim.41), channel_id=1, replica_groups={{0,32,64,96,128,160,192,224},{16,48,80,112,144,176,208,240},{1,33,65,97..., dimensions={0} | all-to-all | bytes 589824 | tf_op jit(solution)/shard_map/all_to_all | solution.py:908
  210.9 3.1 %collective-permute-start.13 = (bf16[8,144,128]{2,1,0:T(8,128)(2,1)S(1)}, bf16[8,144,128]{2,1,0:T(8,128)(2,1)S(1)}, u32[]{:S(2)}, u32[]{:S(2)}) collective-permute-start(bf16[8,144,128]{2,1,0:T(8,128)(2,1)S(1)} %all_to_all.26.mine_ref), channel_id=1, source_target_pairs={{0,16},{16,0},{2,18},{18,2},{4,20},{20,4},{6,22},{22,6},{8,24},{24... | collective-permute-start | bytes 884744 | tf_op jit(solution)/shard_map/ppermute | solution.py:666
  214.1 1.1 collective-permute-done.13.theirs_ref
  215.2 1.5 finish.1
  (102 shorter events, 10.0 us)
Async XLA Ops:
  0.7 14.7 %copy-start.19 = (bf16[48,2304]{1,0:T(8,128)(2,1)S(1)}, bf16[48,2304]{1,0:T(8,128)(2,1)}, u32[]{:S(2)}) copy-start(bf16[48,2304]{1,0:T(8,128)(2,1)} %param.16) | copy-start | bytes 663556
  5.2 22.7 %all-to-all-start = ((bf16[16,88,128]{2,1,0:T(8,128)(2,1)}), bf16[16,88,128]{2,1,0:T(8,128)(2,1)S(1)}, u32[]{:S(2)}, u32[]{:S(2)}) async-start(bf16[16,88,128]{2,1,0:T(8,128)(2,1)} %broadcast_in_dim.37), calls=%async_computation | async-start | bytes 720896 | tf_op jit(solution)/shard_map/all_to_all | solution.py:848
  15.4 3.9 %collective-permute-start.1 = (bf16[144,384]{1,0:T(8,128)(2,1)S(1)}, bf16[144,384]{1,0:T(8,128)(2,1)S(1)}, u32[]{:S(2)}, u32[]{:S(2)}) collective-permute-start(bf16[144,384]{1,0:T(8,128)(2,1)S(1)} %pad_maximum_fusion.3), channel_id=1, source_target_pairs={{0,1},{1,0},{2,3},{3,2},{4,5},{5,4},{6,7},{7,6},{8,9},{9,8},{10,11... | collective-permute-start | bytes 331784 | tf_op jit(solution)/shard_map/ppermute | solution.py:670
  19.3 22.6 %copy-start.18 = (bf16[288,384]{1,0:T(8,128)(2,1)}, bf16[288,384]{1,0:T(8,128)(2,1)S(1)}, u32[]{:S(2)}) copy-start(bf16[288,384]{1,0:T(8,128)(2,1)S(1)} %pad_maximum_fusion.1.refs_0_) | copy-start | bytes 663556
  19.3 12.2 %collective-permute-start.2 = (bf16[288,384]{1,0:T(8,128)(2,1)S(1)}, bf16[288,384]{1,0:T(8,128)(2,1)S(1)}, u32[]{:S(2)}, u32[]{:S(2)}) collective-permute-start(bf16[288,384]{1,0:T(8,128)(2,1)S(1)} %pad_maximum_fusion.1.refs_0_), channel_id=1, source_target_pairs={{0,2},{16,18},{2,4},{18,20},{4,6},{20,22},{6,8},{22,24},{8,10},{24... | collective-permute-start | bytes 663560 | tf_op jit(solution)/shard_map/ppermute | solution.py:666
  21.3 10.2 %collective-permute-start.3 = (bf16[288,384]{1,0:T(8,128)(2,1)S(1)}, bf16[288,384]{1,0:T(8,128)(2,1)S(1)}, u32[]{:S(2)}, u32[]{:S(2)}) collective-permute-start(bf16[288,384]{1,0:T(8,128)(2,1)S(1)} %pad_maximum_fusion.1.refs_0_), channel_id=1, source_target_pairs={{0,14},{16,30},{2,0},{18,16},{4,2},{20,18},{6,4},{22,20},{8,6},{24... | collective-permute-start | bytes 663560 | tf_op jit(solution)/shard_map/ppermute | solution.py:666
  27.9 4.5 %collective-permute-start = (bf16[8,56,128]{2,1,0:T(8,128)(2,1)S(1)}, bf16[8,56,128]{2,1,0:T(8,128)(2,1)S(1)}, u32[]{:S(2)}, u32[]{:S(2)}) collective-permute-start(bf16[8,56,128]{2,1,0:T(8,128)(2,1)S(1)} %get-tuple-element.67), channel_id=1, source_target_pairs={{0,16},{16,0},{2,18},{18,2},{4,20},{20,4},{6,22},{22,6},{8,24},{24... | collective-permute-start | bytes 344072 | tf_op jit(solution)/shard_map/ppermute | solution.py:666
  33.9 8.0 %copy-start.15 = (bf16[288,384]{1,0:T(8,128)(2,1)}, bf16[288,384]{1,0:T(8,128)(2,1)S(1)}, u32[]{:S(2)}) copy-start(bf16[288,384]{1,0:T(8,128)(2,1)S(1)} %get-tuple-element.23.refs_2_) | copy-start | bytes 663556
  33.9 17.9 %copy-start.10 = (bf16[288,384]{1,0:T(8,128)(2,1)}, bf16[288,384]{1,0:T(8,128)(2,1)S(1)}, u32[]{:S(2)}) copy-start(bf16[288,384]{1,0:T(8,128)(2,1)S(1)} %get-tuple-element.24._after._buffer.refs_1_) | copy-start | bytes 663556
  33.9 7.9 %collective-permute-start.6 = (bf16[288,384]{1,0:T(8,128)(2,1)S(1)}, bf16[288,384]{1,0:T(8,128)(2,1)S(1)}, u32[]{:S(2)}, u32[]{:S(2)}) collective-permute-start(bf16[288,384]{1,0:T(8,128)(2,1)S(1)} %get-tuple-element.24._after._buffer.refs_1_), channel_id=1, source_target_pairs={{0,2},{16,18},{2,4},{18,20},{4,6},{20,22},{6,8},{22,24},{8,10},{24... | collective-permute-start | bytes 663560 | tf_op jit(solution)/shard_map/ppermute | solution.py:666
  34.6 14.2 %collective-permute-start.4 = (bf16[288,384]{1,0:T(8,128)(2,1)S(1)}, bf16[288,384]{1,0:T(8,128)(2,1)S(1)}, u32[]{:S(2)}, u32[]{:S(2)}) collective-permute-start(bf16[288,384]{1,0:T(8,128)(2,1)S(1)} %get-tuple-element.23.refs_2_), channel_id=1, source_target_pairs={{0,14},{16,30},{2,0},{18,16},{4,2},{20,18},{6,4},{22,20},{8,6},{24... | collective-permute-start | bytes 663560 | tf_op jit(solution)/shard_map/ppermute | solution.py:666
  41.8 0.7 copy-start.22
  41.8 9.3 %collective-permute-start.7 = (bf16[288,384]{1,0:T(8,128)(2,1)S(1)}, bf16[288,384]{1,0:T(8,128)(2,1)}, u32[]{:S(2)}, u32[]{:S(2)}) collective-permute-start(bf16[288,384]{1,0:T(8,128)(2,1)S(1)} %collective-permute-done.6.refs_3_), channel_id=1, source_target_pairs={{0,2},{16,18},{2,4},{18,20},{4,6},{20,22},{6,8},{22,24},{8,10},{24... | collective-permute-start | bytes 663560 | tf_op jit(solution)/shard_map/ppermute | solution.py:666
  42.5 32.6 %all-to-all-start.1 = ((bf16[8,896,128]{2,1,0:T(8,128)(2,1)}), bf16[8,896,128]{2,1,0:T(8,128)(2,1)}, u32[]{:S(2)}, u32[]{:S(2)}) async-start(bf16[8,896,128]{2,1,0:T(8,128)(2,1)} %get-tuple-element.27), calls=%async_computation.1 | async-start | bytes 3670016 | tf_op jit(solution)/shard_map/all_to_all | solution.py:857
  48.8 3.0 %copy-start.2 = (bf16[1,14,8,8,768]{4,3,2,1,0:T(8,128)(2,1)S(1)}, bf16[1,14,8,8,768]{4,3,2,1,0:T(8,128)(2,1)}, u32[]{:S(2)}) copy-start(bf16[1,14,8,8,768]{4,3,2,1,0:T(8,128)(2,1)} %param.10) | copy-start | bytes 4128772
  48.9 6.6 %copy-start.13 = (bf16[288,384]{1,0:T(8,128)(2,1)}, bf16[288,384]{1,0:T(8,128)(2,1)S(1)}, u32[]{:S(2)}) copy-start(bf16[288,384]{1,0:T(8,128)(2,1)S(1)} %collective-permute-done.4._after.refs_4_) | copy-start | bytes 663556
  48.9 10.2 %collective-permute-start.5 = (bf16[288,384]{1,0:T(8,128)(2,1)S(1)}, bf16[288,384]{1,0:T(8,128)(2,1)S(1)}, u32[]{:S(2)}, u32[]{:S(2)}) collective-permute-start(bf16[288,384]{1,0:T(8,128)(2,1)S(1)} %collective-permute-done.4._after.refs_4_), channel_id=1, source_target_pairs={{0,14},{16,30},{2,0},{18,16},{4,2},{20,18},{6,4},{22,20},{8,6},{24... | collective-permute-start | bytes 663560 | tf_op jit(solution)/shard_map/ppermute | solution.py:666
  51.1 11.7 %collective-permute-start.8 = (bf16[288,384]{1,0:T(8,128)(2,1)}, bf16[288,384]{1,0:T(8,128)(2,1)S(1)}, u32[]{:S(2)}, u32[]{:S(2)}) collective-permute-start(bf16[288,384]{1,0:T(8,128)(2,1)} %collective-permute-done.7.refs_5_), channel_id=1, source_target_pairs={{0,2},{16,18},{2,4},{18,20},{4,6},{20,22},{6,8},{22,24},{8,10},{24... | collective-permute-start | bytes 663560 | tf_op jit(solution)/shard_map/ppermute | solution.py:666
  59.1 3.7 %copy-start.5 = (bf16[1,14,8,8,768]{4,3,2,1,0:T(8,128)(2,1)S(1)}, bf16[1,14,8,8,768]{4,3,2,1,0:T(8,128)(2,1)}, u32[]{:S(2)}) copy-start(bf16[1,14,8,8,768]{4,3,2,1,0:T(8,128)(2,1)} %param.11) | copy-start | bytes 4128772
  59.1 3.6 %copy-start.14 = (bf16[288,384]{1,0:T(8,128)(2,1)}, bf16[288,384]{1,0:T(8,128)(2,1)S(1)}, u32[]{:S(2)}) copy-start(bf16[288,384]{1,0:T(8,128)(2,1)S(1)} %collective-permute-done.5._after.refs_6_) | copy-start | bytes 663556
  62.7 5.2 %copy-start.16 = (bf16[288,384]{1,0:T(8,128)(2,1)}, bf16[288,384]{1,0:T(8,128)(2,1)S(1)}, u32[]{:S(2)}) copy-start(bf16[288,384]{1,0:T(8,128)(2,1)S(1)} %collective-permute-done.8._after.refs_7_) | copy-start | bytes 663556
  68.0 1.6 copy-start.7
  69.6 7.1 %copy-start.17 = (bf16[896,768]{1,0:T(8,128)(2,1)}, bf16[896,768]{1,0:T(8,128)(2,1)S(1)}, u32[]{:S(2)}) copy-start(bf16[896,768]{1,0:T(8,128)(2,1)S(1)} %get-tuple-element.25.mine_ref) | copy-start | bytes 4128772
  69.6 7.1 %collective-permute-start.10 = (bf16[896,768]{1,0:T(8,128)(2,1)}, bf16[896,768]{1,0:T(8,128)(2,1)}, u32[]{:S(2)}, u32[]{:S(2)}) collective-permute-start(bf16[896,768]{1,0:T(8,128)(2,1)} %get-tuple-element.26.gb_mine_ref), channel_id=1, source_target_pairs={{0,16},{16,0},{2,18},{18,2},{4,20},{20,4},{6,22},{22,6},{8,24},{24... | collective-permute-start | bytes 4128776 | tf_op jit(solution)/shard_map/ppermute | solution.py:666
  71.6 5.0 %collective-permute-start.9 = (bf16[896,768]{1,0:T(8,128)(2,1)S(1)}, bf16[896,768]{1,0:T(8,128)(2,1)}, u32[]{:S(2)}, u32[]{:S(2)}) collective-permute-start(bf16[896,768]{1,0:T(8,128)(2,1)S(1)} %get-tuple-element.25.mine_ref), channel_id=1, source_target_pairs={{0,16},{16,0},{2,18},{18,2},{4,20},{20,4},{6,22},{22,6},{8,24},{24... | collective-permute-start | bytes 4128776 | tf_op jit(solution)/shard_map/ppermute | solution.py:666
  109.1 7.6 %copy-start.20 = (f32[1,1152]{1,0:T(1,128)S(1)}, f32[1,1152]{1,0:T(1,128)}, u32[]{:S(2)}) copy-start(f32[1,1152]{1,0:T(1,128)} %get-tuple-element.36) | copy-start | bytes 13828
  109.2 7.7 %copy-start.21 = (f32[1,768]{1,0:T(1,128)S(1)}, f32[1,768]{1,0:T(1,128)}, u32[]{:S(2)}) copy-start(f32[1,768]{1,0:T(1,128)} %get-tuple-element.35) | copy-start | bytes 9220
  109.2 59.0 %all-to-all-start.2 = ((bf16[8,1792,128]{2,1,0:T(8,128)(2,1)}), bf16[8,1792,128]{2,1,0:T(8,128)(2,1)}, u32[]{:S(2)}, u32[]{:S(2)}) async-start(bf16[8,1792,128]{2,1,0:T(8,128)(2,1)} %get-tuple-element.33._after._buffer), calls=%async_computation.2 | async-start | bytes 7340032 | tf_op jit(solution)/shard_map/all_to_all | solution.py:890
  116.1 3.6 %collective-permute-start.11 = (bf16[896,768]{1,0:T(8,128)(2,1)}, bf16[896,768]{1,0:T(8,128)(2,1)S(1)}, u32[]{:S(2)}, u32[]{:S(2)}) collective-permute-start(bf16[896,768]{1,0:T(8,128)(2,1)} %get-tuple-element.29), channel_id=1, source_target_pairs={{0,16},{16,0},{2,18},{18,2},{4,20},{20,4},{6,22},{22,6},{8,24},{24... | collective-permute-start | bytes 4128776 | tf_op jit(solution)/shard_map/ppermute | solution.py:666
  119.7 1.1 copy-start.11
  120.8 1.8 copy-start.8
  122.6 1.8 copy-start.9
  124.3 1.3 copy-start.12
  125.7 4.5 %copy-start = (bf16[8,1792,128]{2,1,0:T(8,128)(2,1)S(1)}, bf16[8,1792,128]{2,1,0:T(8,128)(2,1)}, u32[]{:S(2)}) copy-start(bf16[8,1792,128]{2,1,0:T(8,128)(2,1)} %get-tuple-element.33._after._buffer) | copy-start | bytes 11010052
  125.7 4.6 %copy-start.3 = (bf16[1,14,8,8,768]{4,3,2,1,0:T(8,128)(2,1)S(1)}, bf16[1,14,8,8,768]{4,3,2,1,0:T(8,128)(2,1)}, u32[]{:S(2)}) copy-start(bf16[1,14,8,8,768]{4,3,2,1,0:T(8,128)(2,1)} %param.10) | copy-start | bytes 4128772
  144.3 2.0 copy-start.1
  146.4 1.3 copy-start.6
  168.2 1.8 copy-start.4
  172.6 2.5 %collective-permute-start.12 = (bf16[8,56,128]{2,1,0:T(8,128)(2,1)S(1)}, bf16[8,56,128]{2,1,0:T(8,128)(2,1)S(1)}, u32[]{:S(2)}, u32[]{:S(2)}) collective-permute-start(bf16[8,56,128]{2,1,0:T(8,128)(2,1)S(1)} %get-tuple-element.66), channel_id=1, source_target_pairs={{0,16},{16,0},{2,18},{18,2},{4,20},{20,4},{6,22},{22,6},{8,24},{24... | collective-permute-start | bytes 344072 | tf_op jit(solution)/shard_map/ppermute | solution.py:666
  210.9 4.3 %collective-permute-start.13 = (bf16[8,144,128]{2,1,0:T(8,128)(2,1)S(1)}, bf16[8,144,128]{2,1,0:T(8,128)(2,1)S(1)}, u32[]{:S(2)}, u32[]{:S(2)}) collective-permute-start(bf16[8,144,128]{2,1,0:T(8,128)(2,1)S(1)} %all_to_all.26.mine_ref), channel_id=1, source_target_pairs={{0,16},{16,0},{2,18},{18,2},{4,20},{20,4},{6,22},{22,6},{8,24},{24... | collective-permute-start | bytes 884744 | tf_op jit(solution)/shard_map/ppermute | solution.py:666
